TPU v7x, 128 devices: a whole 4x4x4 slice. The times are simulated.
128 devices in a mesh: ex: 16 (over x, z), tp: 8 (over y, core).
Axes of the slice: x: 4, y: 4, z: 4, core: 2. Of those that a mesh axis runs over, the one named last changes fastest.
Arguments:
- activations: bfloat16 [64, 128, 8192], P('ex', None, 'tp'), may hold values from -6 to 6
- out_grads: bfloat16 [64, 128, 8192], P('ex', None, 'tp'), may hold values from -0.5390625 to 0.5390625
Outputs:
- fisher: float32 [8192, 8192], P('ex', 'tp')
All inputs are finite; a program needn't handle non-finite values.
Results may differ from a plain program's by a relative error of at most 0.0003.
Values may be sent and summed in bfloat16 or wider, within the bound.
No kernel may reach another device: no remote copies, remote signals or barrier semaphores. Data moves between devices by JAX's collectives and lax.ppermute only.
A program may use at most 128 MiB of HBM per device.

v0:
```python
import math

import jax
import jax.numpy as jnp
from jax import lax
from jax.sharding import PartitionSpec as P


def body(activations, out_grads):
    width_out = out_grads.shape[2]
    width_local = activations.shape[2]
    full_width = width_local * lax.axis_size("tp")
    own_rows = full_width // lax.axis_size("ex")
    whole_inputs = lax.all_gather(activations, "tp", axis=2, tiled=True)
    block_rows = math.gcd(lax.axis_size("ex") * own_rows, 512)

    def one_block(position, result):
        window = lax.dynamic_slice_in_dim(whole_inputs, position * block_rows, block_rows, 2)
        gradient = jnp.einsum("etd,etc->edc", window, out_grads, preferred_element_type=jnp.float32)
        squared = jnp.sum(gradient * gradient, axis=0)
        return lax.dynamic_update_slice_in_dim(result, squared, position * block_rows, 0)

    initial = jnp.zeros((lax.axis_size("ex") * own_rows, width_out), jnp.float32)
    return lax.psum_scatter(
        lax.fori_loop(0, lax.axis_size("ex") * own_rows // block_rows, one_block, initial),
        "ex",
        scatter_dimension=0,
        tiled=True,
    )


def solution(mesh):
    return jax.shard_map(
        body,
        mesh=mesh,
        in_specs=(P("ex", None, "tp"), P("ex", None, "tp")),
        out_specs=P("ex", "tp"),
        check_vma=False,
    )
```

profile of v0, /device:TPU:1, one launch (start us, length us, event | category | flops | bytes accessed | tf_op | source)
XLA Modules:
  0.0 340.8 jit_solution(5607944191279526594)
XLA Ops:
  6.5 0.0 all-gather.2.cloned.1.call-start
  6.5 2.3 copy.3
  8.8 0.0 all-gather.2.cloned.1.call-update
  8.8 0.0 reduce-scatter.2.cloned.1.call-start
  8.9 0.0 copy-start
  8.9 53.6 %all-gather.2.cloned.1.call-done = bf16[4,128,8192]{1,2,0:T(8,128)(2,1)} async-done(((bf16[4,128,1024]{1,2,0:T(8,128)(2,1)}), bf16[4,128,8192]{1,2,0:T(8,128)(2,1)}) %all-gather.2.cloned.1.call-update) | async-done | bytes 8388624 | tf_op jit(solution)/shard_map/all_gather | solution.py:14
  62.5 11.2 %broadcast_in_dim.3 = f32[8192,1024]{1,0:T(8,128)} broadcast(f32[]{:T(128)} %constant.37.clone.1), dimensions={} | broadcast | bytes 33554436 | tf_op jit(solution)/shard_map/broadcast_in_dim | solution.py:23
  73.7 0.0 copy-done
  73.7 65.5 %while.13 = (s32[]{:T(128)}, f32[8192,1024]{1,0:T(8,128)}, bf16[4,128,8192]{1,2,0:T(8,128)(2,1)}, bf16[4,128,1024]{2,1,0:T(8,128)(2,1)S(1)}, s32[]{:T(128)}, /*index=5*/s32[]{:T(128)}, s32[]{:T(128)}, s32[]{:T(128)}) while((s32[]{:T(128)}, f32[8192,1024]{1,0:T(8,128)}, bf16[4,128,8192]{1,2,0:T(8,128)(2,1)}, ...), condition=%wide.region_2.0_spmd, body=%wide.region_0.0_spmd.sunk | while | flops 540540928 | bytes 7864459 | solution.py:25
  73.7 2.5 multiply_reduce_fusion.2
  76.2 1.6 constant_dynamic-update-slice_fusion.2
  77.8 2.5 multiply_reduce_fusion.2
  80.3 1.6 constant_dynamic-update-slice_fusion.2
  81.9 2.5 multiply_reduce_fusion.2
  84.4 1.6 constant_dynamic-update-slice_fusion.2
  86.0 2.5 multiply_reduce_fusion.2
  88.5 1.6 constant_dynamic-update-slice_fusion.2
  90.1 2.5 multiply_reduce_fusion.2
  92.6 1.6 constant_dynamic-update-slice_fusion.2
  94.2 2.5 multiply_reduce_fusion.2
  96.7 1.6 constant_dynamic-update-slice_fusion.2
  98.3 2.5 multiply_reduce_fusion.2
  100.8 1.6 constant_dynamic-update-slice_fusion.2
  102.4 2.5 multiply_reduce_fusion.2
  104.9 1.6 constant_dynamic-update-slice_fusion.2
  106.5 2.5 multiply_reduce_fusion.2
  109.0 1.6 constant_dynamic-update-slice_fusion.2
  110.6 2.5 multiply_reduce_fusion.2
  113.1 1.6 constant_dynamic-update-slice_fusion.2
  114.6 2.5 multiply_reduce_fusion.2
  117.2 1.6 constant_dynamic-update-slice_fusion.2
  118.7 2.5 multiply_reduce_fusion.2
  121.2 1.6 constant_dynamic-update-slice_fusion.2
  122.8 2.5 multiply_reduce_fusion.2
  125.3 1.6 constant_dynamic-update-slice_fusion.2
  127.0 2.5 multiply_reduce_fusion.2
  129.5 1.6 constant_dynamic-update-slice_fusion.2
  131.0 2.5 multiply_reduce_fusion.2
  133.5 1.6 constant_dynamic-update-slice_fusion.2
  135.1 2.5 multiply_reduce_fusion.2
  137.7 1.6 constant_dynamic-update-slice_fusion.2
  139.2 0.0 reduce-scatter.2.cloned.1.call-update
  139.3 194.7 %reduce-scatter.2.cloned.1.call-done = f32[512,1024]{1,0:T(8,128)} async-done(((f32[8192,1024]{1,0:T(8,128)}), f32[512,1024]{1,0:T(8,128)}) %reduce-scatter.2.cloned.1.call-update) | async-done | bytes 2097168 | tf_op jit(solution)/shard_map/reduce_scatter | solution.py:24
Async XLA Ops:
  6.5 55.9 %all-gather.2.cloned.1.call-start = ((), (), s32[]{:S(2)}) async-start(), calls=%async_computation.1 | async-start | bytes 9437184 | tf_op jit(solution)/shard_map/all_gather | solution.py:14
  8.8 325.2 %reduce-scatter.2.cloned.1.call-start = ((), (), s32[]{:S(2)}) async-start(), calls=%async_computation.2 | async-start | bytes 35651584 | tf_op jit(solution)/shard_map/reduce_scatter | solution.py:24
  8.9 64.8 %copy-start = (bf16[4,128,1024]{2,1,0:T(8,128)(2,1)S(1)}, bf16[4,128,1024]{2,1,0:T(8,128)(2,1)}, u32[]{:S(2)}) copy-start(bf16[4,128,1024]{2,1,0:T(8,128)(2,1)} %param.5) | copy-start | bytes 3145732
Sparse Core Ops, SparseCore 0:
  9.0 53.3 all-gather.1
  139.4 194.5 reduce-scatter.1
where the time goes:
time: 342 us; the launch traced here: 341 us
  waiting for transfers between devices  248 us (73%)
  matrix products  40.1 us (12%)
  local copies, waits for them, and re-layouts  38.9 us (11%)
  between operations  13.4 us (4%)
    reduce_scatter x1, waiting for transfers between devices, body(): lax.psum_scatter(lax.fori_loop(0, lax.axis_size('ex') * own_rows // block...  195 us
    all_gather x1, waiting for transfers between devices, body(): whole_inputs = lax.all_gather(activations, 'tp', axis=2, tiled=True)  53.6 us
    dot_general x16, matrix products, one_block(): jnp.einsum('etd,etc->edc', window, out_grads, preferred_element_type=jnp....  40.1 us
    dynamic_update_slice x16, local copies, waits for them, and re-layouts, one_block(): lax.dynamic_update_slice_in_dim(result, squared, position * block_rows, 0)  25.3 us
    broadcast_in_dim x1, local copies, waits for them, and re-layouts, body(): jnp.zeros((lax.axis_size('ex') * own_rows, width_out), jnp.float32)  11.2 us
  transfers between devices with their start and end apart: 2, of which 2 were waited for; matrix products, arithmetic and copies ran while one was open for 0% of the time, Pallas kernels for 0%

commit v1 on v0

v1 whole, which is shorter than its diff:
```python
import functools

import jax
import jax.numpy as jnp
from jax import lax
from jax.experimental import pallas as pl
from jax.experimental.pallas import tpu as pltpu
from jax.sharding import Mesh, PartitionSpec as P

BF, F32 = jnp.bfloat16, jnp.float32
ANY = pl.BlockSpec(memory_space=pl.ANY)
VM = pl.BlockSpec(memory_space=pltpu.VMEM)
POWER = 12
TOP = 9.625
VMEM_LIMIT = 40 << 20


def ring(n, k):
    return [(i, (i + k) % n) for i in range(n)]


def code_of(u):
    return jnp.where(u == 0, 0, jnp.where(u == 1, 3, jnp.where(u == 2, 1, 2)))


def source_of(code):
    return jnp.where(code == 0, 0, jnp.where(code == 1, 2, jnp.where(code == 2, 3, 1)))


def round_pairs(k):
    pairs = []
    for z in range(4):
        for c in range(2):
            code = [0, 3, 1, 2][(z - 2 * c) % 4] ^ k
            pairs.append((z * 2 + c, (2 * c + code // 2) * 2 + code % 2))
    return pairs


def prep_kernel(a_ref, *o_refs):
    z, c = lax.axis_index("z"), lax.axis_index("c")
    first = code_of(lax.rem(z - 2 * c + 4, 4))
    for k in range(4):
        code = first ^ k
        off = pl.multiple_of(code * 256, 256)
        for e in range(4):
            o_refs[k][e] = a_ref[e, :, pl.ds(off, 256)].T


def prep(a):
    return pl.pallas_call(
        prep_kernel,
        out_shape=[jax.ShapeDtypeStruct((4, 256, 128), BF)] * 4,
        in_specs=[VM],
        out_specs=[VM] * 4,
        compiler_params=pltpu.CompilerParams(vmem_limit_bytes=VMEM_LIMIT),
        name="prep",
    )(a)


def encode(acc, o_ref):
    rows, cols = acc.shape
    top = jnp.max(acc[...], axis=0, keepdims=True)
    top = jnp.max(top, axis=1, keepdims=True)
    k = jnp.clip(jnp.floor(jnp.log2(jnp.maximum(top, 1e-36))), -100.0, 100.0)
    scale = jnp.exp2(TOP - k)
    u = acc[...] * scale
    u2 = u * u
    u4 = u2 * u2
    o_ref[0:rows, :] = (u4 * u4 * u4).astype(BF)
    o_ref[rows : rows + 16, :] = jnp.broadcast_to(k, (16, cols)).astype(BF)


def decode(t, k):
    t = t.astype(F32)
    root = jnp.exp2(jnp.log2(jnp.maximum(t, 1e-38)) * (1.0 / POWER))
    return jnp.where(t > 0, root, 0.0) * jnp.exp2(k.astype(F32) - TOP)


def block_kernel(d, coded, *refs):
    g0, gm, gp, h1, h2, s0, s0c, sm, smc, sp, spc, t1, t1c, t2, t2c, o_ref, a_vm, g_vm, acc_vm, sem = refs
    acc = acc_vm if coded else o_ref
    x, z, y, c = (lax.axis_index(n) for n in "xzyc")
    r = lax.rem(x - y + d + 4, 4)
    a_sem = sem.at[4]
    for slot, src in ((0, g0), (3, gm), (1, gp)):
        pltpu.make_async_copy(src, g_vm.at[slot], sem.at[slot]).start()

    def load(pieces):
        for half, parts in pieces:
            row = pl.multiple_of(half * 256, 256)
            for k, (ref, at) in enumerate(parts):
                u = source_of((2 * lax.rem(z, 2) + half) ^ k)
                slot = lax.rem(u - lax.rem(z, 2) + 4, 4)
                pltpu.make_async_copy(ref.at[pl.ds(at, 4)], a_vm.at[slot, :, pl.ds(row, 256), :], a_sem).start()

    def whole(ref):
        return [(ref, 4 * k) for k in range(4)]

    def parts(one, two):
        return [(one, 0), (one, 4), (two, 0), (two, 4)]

    for value, mine, theirs in ((0, whole(s0), whole(s0c)), (3, whole(sm), whole(smc)), (1, whole(sp), whole(spc)), (2, parts(t1, t2), parts(t1c, t2c))):
        @pl.when(r == value)
        def _():
            load(((c, mine), (1 - c, theirs)))
    pltpu.make_async_copy(h1, g_vm.at[2, 0:2], sem.at[2]).start()
    pltpu.make_async_copy(h2, g_vm.at[2, 2:4], sem.at[5]).start()

    pltpu.make_async_copy(a_vm, a_vm, a_sem).wait()
    for n, slot in enumerate((0, 3, 1, 2)):
        if slot == 2:
            pltpu.make_async_copy(h1, g_vm.at[2, 0:2], sem.at[2]).wait()
            pltpu.make_async_copy(h2, g_vm.at[2, 2:4], sem.at[5]).wait()
        else:
            pltpu.make_async_copy(g0, g_vm.at[slot], sem.at[slot]).wait()

        def tile(t, carry):
            cols = pl.ds(pl.multiple_of(t * 256, 256), 256)
            for i in range(4):
                v = jnp.dot(a_vm[slot, i], g_vm[slot, i, :, cols], preferred_element_type=F32)
                if n == 0 and i == 0:
                    acc[:, cols] = v * v
                else:
                    acc[:, cols] += v * v
            return carry

        lax.fori_loop(0, 4, tile, 0)
    if coded:
        encode(acc, o_ref)


def block(d, coded, refs):
    return pl.pallas_call(
        functools.partial(block_kernel, d, coded),
        out_shape=jax.ShapeDtypeStruct((528, 1024), BF) if coded else jax.ShapeDtypeStruct((512, 1024), F32),
        in_specs=[ANY] * 15,
        out_specs=VM,
        scratch_shapes=[
            pltpu.VMEM((4, 4, 512, 128), BF),
            pltpu.VMEM((4, 4, 128, 1024), BF),
            pltpu.VMEM((512, 1024) if coded else (8, 128), F32),
            pltpu.SemaphoreType.DMA((6,)),
        ],
        compiler_params=pltpu.CompilerParams(vmem_limit_bytes=VMEM_LIMIT),
        cost_estimate=pl.CostEstimate(flops=2 * 16 * 128 * 512 * 1024, bytes_accessed=7 << 20, transcendentals=0),
        name=f"block{d % 4}",
    )(*refs)


def final_kernel(own, p1, p2, p3, k1, k2, k3, o_ref):
    total = own[...]
    for p, k in ((p1, k1), (p2, k2), (p3, k3)):
        total += decode(p[...], k[0:1, 0:1])
    o_ref[...] = total


def final(own, payloads):
    rows = 128
    payload = pl.BlockSpec((rows, 1024), lambda i: (i, 0))
    exponent = pl.BlockSpec((16, 1024), lambda i: (32, 0))
    return pl.pallas_call(
        final_kernel,
        grid=(512 // rows,),
        out_shape=jax.ShapeDtypeStruct((512, 1024), F32),
        in_specs=[payload] * 4 + [exponent] * 3,
        out_specs=payload,
        compiler_params=pltpu.CompilerParams(vmem_limit_bytes=VMEM_LIMIT),
        name="final",
    )(own, *payloads, *payloads)


def body(a, g):
    rounds = [lax.ppermute(p, ("z", "c"), round_pairs(k)) for k, p in enumerate(prep(a))]
    s0 = jnp.concatenate(rounds, axis=0)

    def other(v):
        return lax.ppermute(v, "c", ring(2, 1))

    sm, sp = lax.ppermute(s0, "y", ring(4, 1)), lax.ppermute(s0, "y", ring(4, -1))
    t1, t2 = lax.ppermute(sm[:8], "y", ring(4, 1)), lax.ppermute(sp[8:], "y", ring(4, -1))
    gm, gp = lax.ppermute(g, "z", ring(4, 1)), lax.ppermute(g, "z", ring(4, -1))
    h1, h2 = lax.ppermute(gm[:2], "z", ring(4, 1)), lax.ppermute(gp[2:], "z", ring(4, -1))
    refs = (g, gm, gp, h1, h2, s0, other(s0), sm, other(sm), sp, other(sp), t1, other(t1), t2, other(t2))
    far = lax.ppermute(block(2, True, refs), "x", ring(4, 2))
    right = lax.ppermute(block(1, True, refs), "x", ring(4, 1))
    left = lax.ppermute(block(-1, True, refs), "x", ring(4, -1))
    own = block(0, False, refs)
    return final(own, (far, right, left))


def solution(mesh):
    fine = Mesh(mesh.devices.reshape(4, 4, 4, 2), ("x", "z", "y", "c"))
    spec = P(("x", "z"), None, ("y", "c"))
    return jax.shard_map(body, mesh=fine, in_specs=(spec, spec), out_specs=P(("x", "z"), ("y", "c")), check_vma=False)
```

time: 342 us -> 138 us (0.40)
  waiting for transfers between devices: 248 us -> 58.4 us
  matrix products: 40.1 us -> 0 us
  Pallas kernels: 0 us -> 39.5 us
  starting transfers between devices: 0.04 us -> 36.2 us
  local copies, waits for them, and re-layouts: 38.9 us -> 3.09 us
  between operations: 13.4 us -> 0.16 us
    reduce_scatter x1 -> x0, waiting for transfers between devices: 195 us -> none  [body(): lax.psum_scatter(lax.fori_loop(0, lax.axis_size('ex') * own_rows // block...]
    ppermute x0 -> x20, waiting for transfers between devices: none -> 58.4 us  [the longest x1 18.6 us: body(): right = lax.ppermute(block(1, True, refs), 'x', ring(4, 1))]
    all_gather x1 -> x0, waiting for transfers between devices: 53.6 us -> none  [body(): whole_inputs = lax.all_gather(activations, 'tp', axis=2, tiled=True)]
    dot_general x16 -> x0, matrix products: 40.1 us -> none  [one_block(): jnp.einsum('etd,etc->edc', window, out_grads, preferred_element_type=jnp....]
    pallas_call x0 -> x6, Pallas kernels: none -> 39.5 us  [the longest x4 34.8 us: block(): pl.pallas_call(functools.partial(block_kernel, d, coded), out_shape=jax.S...]
    ppermute x0 -> x20, starting transfers between devices: none -> 36.2 us  [the longest x4 12.5 us: body(): lax.ppermute(p, ('z', 'c'), round_pairs(k))]
    dynamic_update_slice x16 -> x0, local copies, waits for them, and re-layouts: 25.3 us -> none  [one_block(): lax.dynamic_update_slice_in_dim(result, squared, position * block_rows, 0)]
    broadcast_in_dim x1 -> x0, local copies, waits for them, and re-layouts: 11.2 us -> none  [body(): jnp.zeros((lax.axis_size('ex') * own_rows, width_out), jnp.float32)]
  transfers between devices with their start and end apart: 2 -> 20, of which waited for: 2 -> 11; matrix products, arithmetic and copies ran while one was open for 0% -> 0% of each run, Pallas kernels for 0% -> 19%
where the time goes in v1:
time: 138 us; the launch traced here: 137 us
  waiting for transfers between devices  58.4 us (42%)
  Pallas kernels  39.5 us (29%)
  starting transfers between devices  36.2 us (26%)
  local copies, waits for them, and re-layouts  3.09 us (2%)
    pallas_call x4, Pallas kernels, block(): pl.pallas_call(functools.partial(block_kernel, d, coded), out_shape=jax.S...  34.8 us
    ppermute x1, waiting for transfers between devices, body(): right = lax.ppermute(block(1, True, refs), 'x', ring(4, 1))  18.6 us
    ppermute x1, waiting for transfers between devices, body(): lax.ppermute(g, 'z', ring(4, -1))  12.8 us
    ppermute x4, starting transfers between devices, body(): lax.ppermute(p, ('z', 'c'), round_pairs(k))  12.5 us
    ppermute x4, waiting for transfers between devices, body(): lax.ppermute(p, ('z', 'c'), round_pairs(k))  10.8 us
    ppermute x5, starting transfers between devices, other(): return lax.ppermute(v, 'c', ring(2, 1))  8.31 us
    ppermute x1, waiting for transfers between devices, body(): lax.ppermute(sp[8:], 'y', ring(4, -1))  6.21 us
    pallas_call x1, Pallas kernels, final(): pl.pallas_call(final_kernel, grid=(512 // rows,), out_shape=jax.ShapeDtyp...  4.3 us
  transfers between devices with their start and end apart: 20, of which 11 were waited for; matrix products, arithmetic and copies ran while one was open for 0% of the time, Pallas kernels for 19%

profile of v1, /device:TPU:1, one launch (start us, length us, event | category | flops | bytes accessed | tf_op | source)
XLA Modules:
  0.0 137.3 jit_solution(15936968685707234400)
XLA Ops:
  0.0 1.2 copy-done.2
  1.2 0.3 prep.1
  1.6 0.0 copy-start
  1.6 6.5 %collective-permute-start.4 = (bf16[4,256,128]{2,1,0:T(8,128)(2,1)S(1)}, bf16[4,256,128]{2,1,0:T(8,128)(2,1)S(1)}, u32[]{:S(2)}, u32[]{:S(2)}) collective-permute-start(bf16[4,256,128]{2,1,0:T(8,128)(2,1)S(1)} %get-tuple-element.9), channel_id=1, source_target_pairs={{0,0},{1,17},{8,9},{9,24},{16,1},{17,16},{24,8},{25,25},{2,2},{3,1... | collective-permute-start | bytes 786440 | tf_op jit(solution)/shard_map/ppermute | solution.py:173
  8.0 2.5 %collective-permute-start.5 = (bf16[4,256,128]{2,1,0:T(8,128)(2,1)S(1)}, bf16[4,256,128]{2,1,0:T(8,128)(2,1)S(1)}, u32[]{:S(2)}, u32[]{:S(2)}) collective-permute-start(bf16[4,256,128]{2,1,0:T(8,128)(2,1)S(1)} %get-tuple-element.10), channel_id=1, source_target_pairs={{0,1},{1,16},{8,8},{9,25},{16,0},{17,17},{24,9},{25,24},{2,3},{3,1... | collective-permute-start | bytes 786440 | tf_op jit(solution)/shard_map/ppermute | solution.py:173
  10.5 0.9 collective-permute-start.6
  11.4 2.7 %collective-permute-start.7 = (bf16[4,256,128]{2,1,0:T(8,128)(2,1)S(1)}, bf16[4,256,128]{2,1,0:T(8,128)(2,1)S(1)}, u32[]{:S(2)}, u32[]{:S(2)}) collective-permute-start(bf16[4,256,128]{2,1,0:T(8,128)(2,1)S(1)} %get-tuple-element.12), channel_id=1, source_target_pairs={{0,9},{1,24},{8,0},{9,17},{16,8},{17,25},{24,1},{25,16},{2,11},{3,... | collective-permute-start | bytes 786440 | tf_op jit(solution)/shard_map/ppermute | solution.py:173
  14.1 0.0 collective-permute-start.1
  14.1 0.0 collective-permute-done.4
  14.1 2.9 %collective-permute-done.5 = bf16[4,256,128]{2,1,0:T(8,128)(2,1)S(1)} collective-permute-done((bf16[4,256,128]{2,1,0:T(8,128)(2,1)S(1)}, bf16[4,256,128]{2,1,0:T(8,128)(2,1)S(1)}, u32[]{:S(2)}, u32[]{:S(2)}) %collective-permute-start.5) | collective-permute-done | bytes 262176 | tf_op jit(solution)/shard_map/ppermute | solution.py:173
  17.0 2.3 %collective-permute-done.6 = bf16[4,256,128]{2,1,0:T(8,128)(2,1)S(1)} collective-permute-done((bf16[4,256,128]{2,1,0:T(8,128)(2,1)S(1)}, bf16[4,256,128]{2,1,0:T(8,128)(2,1)S(1)}, u32[]{:S(2)}, u32[]{:S(2)}) %collective-permute-start.6) | collective-permute-done | bytes 262176 | tf_op jit(solution)/shard_map/ppermute | solution.py:173
  19.4 5.6 %collective-permute-done.7 = bf16[4,256,128]{2,1,0:T(8,128)(2,1)S(1)} collective-permute-done((bf16[4,256,128]{2,1,0:T(8,128)(2,1)S(1)}, bf16[4,256,128]{2,1,0:T(8,128)(2,1)S(1)}, u32[]{:S(2)}, u32[]{:S(2)}) %collective-permute-start.7) | collective-permute-done | bytes 262176 | tf_op jit(solution)/shard_map/ppermute | solution.py:173
  25.0 2.8 %collective-permute-start.11 = (bf16[16,256,128]{2,1,0:T(8,128)(2,1)S(1)}, bf16[16,256,128]{2,1,0:T(8,128)(2,1)S(1)}, u32[]{:S(2)}, u32[]{:S(2)}) collective-permute-start(bf16[16,256,128]{2,1,0:T(8,128)(2,1)S(1)} %constant_dynamic-update-slice_fusion.refs_5_), channel_id=1, source_target_pairs={{0,6},{2,0},{4,2},{6,4},{1,7},{3,1},{5,3},{7,5},{8,14},{10,8},{12,... | collective-permute-start | bytes 3145736 | tf_op jit(solution)/shard_map/ppermute | solution.py:179
  27.8 0.0 collective-permute-start.9
  27.8 0.0 collective-permute-start
  27.8 2.8 %collective-permute-start.8 = (bf16[16,256,128]{2,1,0:T(8,128)(2,1)S(1)}, bf16[16,256,128]{2,1,0:T(8,128)(2,1)S(1)}, u32[]{:S(2)}, u32[]{:S(2)}) collective-permute-start(bf16[16,256,128]{2,1,0:T(8,128)(2,1)S(1)} %constant_dynamic-update-slice_fusion.refs_5_), channel_id=1, source_target_pairs={{0,1},{1,0},{2,3},{3,2},{4,5},{5,4},{6,7},{7,6},{8,9},{9,8},{10,11... | collective-permute-start | bytes 3145736 | tf_op jit(solution)/shard_map/ppermute | solution.py:177
  30.6 12.8 %collective-permute-done.1.refs_2_ = bf16[4,128,1024]{2,1,0:T(8,128)(2,1)S(1)} collective-permute-done((bf16[4,128,1024]{2,1,0:T(8,128)(2,1)}, bf16[4,128,1024]{2,1,0:T(8,128)(2,1)S(1)}, u32[]{:S(2)}, u32[]{:S(2)}) %collective-permute-start.1) | collective-permute-done | bytes 1048608 | tf_op jit(solution)/shard_map/ppermute | solution.py:181
  43.4 3.4 %collective-permute-start.3 = (bf16[2,128,1024]{2,1,0:T(8,128)(2,1)S(1)}, bf16[2,128,1024]{2,1,0:T(8,128)(2,1)S(1)}, u32[]{:S(2)}, u32[]{:S(2)}) collective-permute-start(bf16[2,128,1024]{2,1,0:T(8,128)(2,1)S(1)} %slice.17), channel_id=1, source_target_pairs={{0,24},{8,0},{16,8},{24,16},{1,25},{9,1},{17,9},{25,17},{2,26},{10... | collective-permute-start | bytes 1572872 | tf_op jit(solution)/shard_map/ppermute | solution.py:182
  46.8 2.9 %collective-permute-done.11.refs_9_ = bf16[16,256,128]{2,1,0:T(8,128)(2,1)S(1)} collective-permute-done((bf16[16,256,128]{2,1,0:T(8,128)(2,1)S(1)}, bf16[16,256,128]{2,1,0:T(8,128)(2,1)S(1)}, u32[]{:S(2)}, u32[]{:S(2)}) %collective-permute-start.11) | collective-permute-done | bytes 1048608 | tf_op jit(solution)/shard_map/ppermute | solution.py:179
  49.7 3.5 %collective-permute-start.15 = (bf16[8,256,128]{2,1,0:T(8,128)(2,1)S(1)}, bf16[8,256,128]{2,1,0:T(8,128)(2,1)S(1)}, u32[]{:S(2)}, u32[]{:S(2)}) collective-permute-start(bf16[8,256,128]{2,1,0:T(8,128)(2,1)S(1)} %slice.19), channel_id=1, source_target_pairs={{0,6},{2,0},{4,2},{6,4},{1,7},{3,1},{5,3},{7,5},{8,14},{10,8},{12,... | collective-permute-start | bytes 1572872 | tf_op jit(solution)/shard_map/ppermute | solution.py:180
  53.2 0.0 collective-permute-done.9.refs_7_
  53.2 1.8 %collective-permute-start.12 = (bf16[16,256,128]{2,1,0:T(8,128)(2,1)S(1)}, bf16[16,256,128]{2,1,0:T(8,128)(2,1)S(1)}, u32[]{:S(2)}, u32[]{:S(2)}) collective-permute-start(bf16[16,256,128]{2,1,0:T(8,128)(2,1)S(1)} %collective-permute-done.11.refs_9_), channel_id=1, source_target_pairs={{0,1},{1,0},{2,3},{3,2},{4,5},{5,4},{6,7},{7,6},{8,9},{9,8},{10,11... | collective-permute-start | bytes 3145736 | tf_op jit(solution)/shard_map/ppermute | solution.py:177
  55.0 0.0 collective-permute-done.refs_1_
  55.0 0.1 collective-permute-start.10
  55.1 0.0 collective-permute-done.8.refs_6_
  55.1 0.1 collective-permute-start.13
  55.3 1.4 %collective-permute-done.3.refs_4_ = bf16[2,128,1024]{2,1,0:T(8,128)(2,1)S(1)} collective-permute-done((bf16[2,128,1024]{2,1,0:T(8,128)(2,1)S(1)}, bf16[2,128,1024]{2,1,0:T(8,128)(2,1)S(1)}, u32[]{:S(2)}, u32[]{:S(2)}) %collective-permute-start.3) | collective-permute-done | bytes 524320 | tf_op jit(solution)/shard_map/ppermute | solution.py:182
  56.7 0.0 collective-permute-start.2
  56.7 6.2 %collective-permute-done.15.refs_13_ = bf16[8,256,128]{2,1,0:T(8,128)(2,1)S(1)} collective-permute-done((bf16[8,256,128]{2,1,0:T(8,128)(2,1)S(1)}, bf16[8,256,128]{2,1,0:T(8,128)(2,1)S(1)}, u32[]{:S(2)}, u32[]{:S(2)}) %collective-permute-start.15) | collective-permute-done | bytes 524320 | tf_op jit(solution)/shard_map/ppermute | solution.py:180
  62.9 2.4 %collective-permute-start.16 = (bf16[8,256,128]{2,1,0:T(8,128)(2,1)S(1)}, bf16[8,256,128]{2,1,0:T(8,128)(2,1)S(1)}, u32[]{:S(2)}, u32[]{:S(2)}) collective-permute-start(bf16[8,256,128]{2,1,0:T(8,128)(2,1)S(1)} %collective-permute-done.15.refs_13_), channel_id=1, source_target_pairs={{0,1},{1,0},{2,3},{3,2},{4,5},{5,4},{6,7},{7,6},{8,9},{9,8},{10,11... | collective-permute-start | bytes 1572872 | tf_op jit(solution)/shard_map/ppermute | solution.py:177
  65.3 4.2 %collective-permute-done.13.refs_11_ = bf16[8,256,128]{2,1,0:T(8,128)(2,1)S(1)} collective-permute-done((bf16[8,256,128]{2,1,0:T(8,128)(2,1)S(1)}, bf16[8,256,128]{2,1,0:T(8,128)(2,1)S(1)}, u32[]{:S(2)}, u32[]{:S(2)}) %collective-permute-start.13) | collective-permute-done | bytes 524320 | tf_op jit(solution)/shard_map/ppermute | solution.py:180
  69.5 1.3 collective-permute-start.14
  70.7 1.0 collective-permute-done.2.refs_3_
  71.8 0.0 collective-permute-done.12.refs_10_
  71.8 0.0 collective-permute-done.10.refs_8_
  71.8 0.0 collective-permute-done.16.refs_14_
  71.8 0.5 collective-permute-done.14.refs_12_
  72.3 8.6 %block2.1 = bf16[528,1024]{1,0:T(8,128)(2,1)S(1)} custom-call(bf16[4,128,1024]{2,1,0:T(8,128)(2,1)S(1)} %copy-done, bf16[4,128,1024]{2,1,0:T(8,128)(2,1)S(1)} %collective-permute-done.refs_1_, bf16[4,128,1024]{2,1,0:T(8,128)(2,1)S(1)} %collective-permute-done.1.refs_2_, bf16[2,128,1024]{2,1,0:T(8,128)(2,1)S(1)} %collective-permute-done.2.refs_3_, ...), custom_call_target="tpu_custom_call" | custom-call | flops 2147483648 | bytes 7340032 | tf_op jit(solution)/shard_map/block2/pallas_call | solution.py:133
  80.9 2.8 %collective-permute-start.17 = (bf16[528,1024]{1,0:T(8,128)(2,1)S(1)}, bf16[528,1024]{1,0:T(8,128)(2,1)S(1)}, u32[]{:S(2)}, u32[]{:S(2)}) collective-permute-start(bf16[528,1024]{1,0:T(8,128)(2,1)S(1)} %block2.1), channel_id=1, source_target_pairs={{0,64},{32,96},{64,0},{96,32},{1,65},{33,97},{65,1},{97,33},{2,66}... | collective-permute-start | bytes 3244040 | tf_op jit(solution)/shard_map/ppermute | solution.py:184
  83.7 8.8 %block1.1 = bf16[528,1024]{1,0:T(8,128)(2,1)S(1)} custom-call(bf16[4,128,1024]{2,1,0:T(8,128)(2,1)S(1)} %copy-done, bf16[4,128,1024]{2,1,0:T(8,128)(2,1)S(1)} %collective-permute-done.refs_1_, bf16[4,128,1024]{2,1,0:T(8,128)(2,1)S(1)} %collective-permute-done.1.refs_2_, bf16[2,128,1024]{2,1,0:T(8,128)(2,1)S(1)} %collective-permute-done.2.refs_3_, ...), custom_call_target="tpu_custom_call" | custom-call | flops 2147483648 | bytes 7340032 | tf_op jit(solution)/shard_map/block1/pallas_call | solution.py:133
  92.5 0.4 collective-permute-start.18
  92.8 8.6 %block3.1 = bf16[528,1024]{1,0:T(8,128)(2,1)S(1)} custom-call(bf16[4,128,1024]{2,1,0:T(8,128)(2,1)S(1)} %copy-done, bf16[4,128,1024]{2,1,0:T(8,128)(2,1)S(1)} %collective-permute-done.refs_1_, bf16[4,128,1024]{2,1,0:T(8,128)(2,1)S(1)} %collective-permute-done.1.refs_2_, bf16[2,128,1024]{2,1,0:T(8,128)(2,1)S(1)} %collective-permute-done.2.refs_3_, ...), custom_call_target="tpu_custom_call" | custom-call | flops 2147483648 | bytes 7340032 | tf_op jit(solution)/shard_map/block3/pallas_call | solution.py:133
  101.5 2.5 %collective-permute-start.19 = (bf16[528,1024]{1,0:T(8,128)(2,1)S(1)}, bf16[528,1024]{1,0:T(8,128)(2,1)S(1)}, u32[]{:S(2)}, u32[]{:S(2)}) collective-permute-start(bf16[528,1024]{1,0:T(8,128)(2,1)S(1)} %block3.1), channel_id=1, source_target_pairs={{0,96},{32,0},{64,32},{96,64},{1,97},{33,1},{65,33},{97,65},{2,98}... | collective-permute-start | bytes 3244040 | tf_op jit(solution)/shard_map/ppermute | solution.py:186
  103.9 8.9 %block0.1.own = f32[512,1024]{1,0:T(8,128)} custom-call(bf16[4,128,1024]{2,1,0:T(8,128)(2,1)S(1)} %copy-done, bf16[4,128,1024]{2,1,0:T(8,128)(2,1)S(1)} %collective-permute-done.refs_1_, bf16[4,128,1024]{2,1,0:T(8,128)(2,1)S(1)} %collective-permute-done.1.refs_2_, bf16[2,128,1024]{2,1,0:T(8,128)(2,1)S(1)} %collective-permute-done.2.refs_3_, ...), custom_call_target="tpu_custom_call" | custom-call | flops 2147483648 | bytes 7340032 | tf_op jit(solution)/shard_map/block0/pallas_call | solution.py:133
  112.8 18.6 %collective-permute-done.18.p2.k2 = bf16[528,1024]{1,0:T(8,128)(2,1)S(1)} collective-permute-done((bf16[528,1024]{1,0:T(8,128)(2,1)S(1)}, bf16[528,1024]{1,0:T(8,128)(2,1)S(1)}, u32[]{:S(2)}, u32[]{:S(2)}) %collective-permute-start.18) | collective-permute-done | bytes 1081376 | tf_op jit(solution)/shard_map/ppermute | solution.py:185
  131.4 0.0 collective-permute-done.19.p3.k3
  131.4 1.6 %copy-done.1 = f32[512,1024]{1,0:T(8,128)S(1)} copy-done((f32[512,1024]{1,0:T(8,128)S(1)}, f32[512,1024]{1,0:T(8,128)}, u32[]{:S(2)}) %copy-start.1) | copy-done | bytes 2097176
  133.0 4.3 %final.1 = f32[512,1024]{1,0:T(8,128)} custom-call(f32[512,1024]{1,0:T(8,128)S(1)} %copy-done.1, bf16[528,1024]{1,0:T(8,128)(2,1)S(1)} %collective-permute-done.17.p1.k1, bf16[528,1024]{1,0:T(8,128)(2,1)S(1)} %collective-permute-done.18.p2.k2, bf16[528,1024]{1,0:T(8,128)(2,1)S(1)} %collective-permute-done.19.p3.k3, ...), custom_call_target="tpu_custom_call" | custom-call | tf_op jit(solution)/shard_map/final/pallas_call | solution.py:161
  (12 shorter events, 0.3 us)
Async XLA Ops:
  0.0 1.2 copy-start.2
  1.6 26.3 %copy-start = (bf16[4,128,1024]{2,1,0:T(8,128)(2,1)S(1)}, bf16[4,128,1024]{2,1,0:T(8,128)(2,1)}, u32[]{:S(2)}) copy-start(bf16[4,128,1024]{2,1,0:T(8,128)(2,1)} %refs_0_.7) | copy-start | bytes 3145732
  1.6 12.5 %collective-permute-start.4 = (bf16[4,256,128]{2,1,0:T(8,128)(2,1)S(1)}, bf16[4,256,128]{2,1,0:T(8,128)(2,1)S(1)}, u32[]{:S(2)}, u32[]{:S(2)}) collective-permute-start(bf16[4,256,128]{2,1,0:T(8,128)(2,1)S(1)} %get-tuple-element.9), channel_id=1, source_target_pairs={{0,0},{1,17},{8,9},{9,24},{16,1},{17,16},{24,8},{25,25},{2,2},{3,1... | collective-permute-start | bytes 786440 | tf_op jit(solution)/shard_map/ppermute | solution.py:173
  8.0 8.9 %collective-permute-start.5 = (bf16[4,256,128]{2,1,0:T(8,128)(2,1)S(1)}, bf16[4,256,128]{2,1,0:T(8,128)(2,1)S(1)}, u32[]{:S(2)}, u32[]{:S(2)}) collective-permute-start(bf16[4,256,128]{2,1,0:T(8,128)(2,1)S(1)} %get-tuple-element.10), channel_id=1, source_target_pairs={{0,1},{1,16},{8,8},{9,25},{16,0},{17,17},{24,9},{25,24},{2,3},{3,1... | collective-permute-start | bytes 786440 | tf_op jit(solution)/shard_map/ppermute | solution.py:173
  10.5 8.8 %collective-permute-start.6 = (bf16[4,256,128]{2,1,0:T(8,128)(2,1)S(1)}, bf16[4,256,128]{2,1,0:T(8,128)(2,1)S(1)}, u32[]{:S(2)}, u32[]{:S(2)}) collective-permute-start(bf16[4,256,128]{2,1,0:T(8,128)(2,1)S(1)} %get-tuple-element.11), channel_id=1, source_target_pairs={{0,8},{1,25},{8,1},{9,16},{16,9},{17,24},{24,0},{25,17},{2,10},{3,... | collective-permute-start | bytes 786440 | tf_op jit(solution)/shard_map/ppermute | solution.py:173
  11.4 13.5 %collective-permute-start.7 = (bf16[4,256,128]{2,1,0:T(8,128)(2,1)S(1)}, bf16[4,256,128]{2,1,0:T(8,128)(2,1)S(1)}, u32[]{:S(2)}, u32[]{:S(2)}) collective-permute-start(bf16[4,256,128]{2,1,0:T(8,128)(2,1)S(1)} %get-tuple-element.12), channel_id=1, source_target_pairs={{0,9},{1,24},{8,0},{9,17},{16,8},{17,25},{24,1},{25,16},{2,11},{3,... | collective-permute-start | bytes 786440 | tf_op jit(solution)/shard_map/ppermute | solution.py:173
  14.1 29.3 %collective-permute-start.1 = (bf16[4,128,1024]{2,1,0:T(8,128)(2,1)}, bf16[4,128,1024]{2,1,0:T(8,128)(2,1)S(1)}, u32[]{:S(2)}, u32[]{:S(2)}) collective-permute-start(bf16[4,128,1024]{2,1,0:T(8,128)(2,1)} %refs_0_.7), channel_id=1, source_target_pairs={{0,24},{8,0},{16,8},{24,16},{1,25},{9,1},{17,9},{25,17},{2,26},{10... | collective-permute-start | bytes 3145736 | tf_op jit(solution)/shard_map/ppermute | solution.py:181
  25.0 24.7 %collective-permute-start.11 = (bf16[16,256,128]{2,1,0:T(8,128)(2,1)S(1)}, bf16[16,256,128]{2,1,0:T(8,128)(2,1)S(1)}, u32[]{:S(2)}, u32[]{:S(2)}) collective-permute-start(bf16[16,256,128]{2,1,0:T(8,128)(2,1)S(1)} %constant_dynamic-update-slice_fusion.refs_5_), channel_id=1, source_target_pairs={{0,6},{2,0},{4,2},{6,4},{1,7},{3,1},{5,3},{7,5},{8,14},{10,8},{12,... | collective-permute-start | bytes 3145736 | tf_op jit(solution)/shard_map/ppermute | solution.py:179
  27.8 25.4 %collective-permute-start.9 = (bf16[16,256,128]{2,1,0:T(8,128)(2,1)S(1)}, bf16[16,256,128]{2,1,0:T(8,128)(2,1)S(1)}, u32[]{:S(2)}, u32[]{:S(2)}) collective-permute-start(bf16[16,256,128]{2,1,0:T(8,128)(2,1)S(1)} %constant_dynamic-update-slice_fusion.refs_5_), channel_id=1, source_target_pairs={{0,2},{2,4},{4,6},{6,0},{1,3},{3,5},{5,7},{7,1},{8,10},{10,12},{12... | collective-permute-start | bytes 3145736 | tf_op jit(solution)/shard_map/ppermute | solution.py:179
  27.8 27.2 %collective-permute-start = (bf16[4,128,1024]{2,1,0:T(8,128)(2,1)S(1)}, bf16[4,128,1024]{2,1,0:T(8,128)(2,1)S(1)}, u32[]{:S(2)}, u32[]{:S(2)}) collective-permute-start(bf16[4,128,1024]{2,1,0:T(8,128)(2,1)S(1)} %copy-done), channel_id=1, source_target_pairs={{0,8},{8,16},{16,24},{24,0},{1,9},{9,17},{17,25},{25,1},{2,10},{10... | collective-permute-start | bytes 3145736 | tf_op jit(solution)/shard_map/ppermute | solution.py:181
  27.8 27.3 %collective-permute-start.8 = (bf16[16,256,128]{2,1,0:T(8,128)(2,1)S(1)}, bf16[16,256,128]{2,1,0:T(8,128)(2,1)S(1)}, u32[]{:S(2)}, u32[]{:S(2)}) collective-permute-start(bf16[16,256,128]{2,1,0:T(8,128)(2,1)S(1)} %constant_dynamic-update-slice_fusion.refs_5_), channel_id=1, source_target_pairs={{0,1},{1,0},{2,3},{3,2},{4,5},{5,4},{6,7},{7,6},{8,9},{9,8},{10,11... | collective-permute-start | bytes 3145736 | tf_op jit(solution)/shard_map/ppermute | solution.py:177
  43.4 13.3 %collective-permute-start.3 = (bf16[2,128,1024]{2,1,0:T(8,128)(2,1)S(1)}, bf16[2,128,1024]{2,1,0:T(8,128)(2,1)S(1)}, u32[]{:S(2)}, u32[]{:S(2)}) collective-permute-start(bf16[2,128,1024]{2,1,0:T(8,128)(2,1)S(1)} %slice.17), channel_id=1, source_target_pairs={{0,24},{8,0},{16,8},{24,16},{1,25},{9,1},{17,9},{25,17},{2,26},{10... | collective-permute-start | bytes 1572872 | tf_op jit(solution)/shard_map/ppermute | solution.py:182
  49.7 13.2 %collective-permute-start.15 = (bf16[8,256,128]{2,1,0:T(8,128)(2,1)S(1)}, bf16[8,256,128]{2,1,0:T(8,128)(2,1)S(1)}, u32[]{:S(2)}, u32[]{:S(2)}) collective-permute-start(bf16[8,256,128]{2,1,0:T(8,128)(2,1)S(1)} %slice.19), channel_id=1, source_target_pairs={{0,6},{2,0},{4,2},{6,4},{1,7},{3,1},{5,3},{7,5},{8,14},{10,8},{12,... | collective-permute-start | bytes 1572872 | tf_op jit(solution)/shard_map/ppermute | solution.py:180
  53.2 18.6 %collective-permute-start.12 = (bf16[16,256,128]{2,1,0:T(8,128)(2,1)S(1)}, bf16[16,256,128]{2,1,0:T(8,128)(2,1)S(1)}, u32[]{:S(2)}, u32[]{:S(2)}) collective-permute-start(bf16[16,256,128]{2,1,0:T(8,128)(2,1)S(1)} %collective-permute-done.11.refs_9_), channel_id=1, source_target_pairs={{0,1},{1,0},{2,3},{3,2},{4,5},{5,4},{6,7},{7,6},{8,9},{9,8},{10,11... | collective-permute-start | bytes 3145736 | tf_op jit(solution)/shard_map/ppermute | solution.py:177
  55.0 16.8 %collective-permute-start.10 = (bf16[16,256,128]{2,1,0:T(8,128)(2,1)S(1)}, bf16[16,256,128]{2,1,0:T(8,128)(2,1)S(1)}, u32[]{:S(2)}, u32[]{:S(2)}) collective-permute-start(bf16[16,256,128]{2,1,0:T(8,128)(2,1)S(1)} %collective-permute-done.9.refs_7_), channel_id=1, source_target_pairs={{0,1},{1,0},{2,3},{3,2},{4,5},{5,4},{6,7},{7,6},{8,9},{9,8},{10,11... | collective-permute-start | bytes 3145736 | tf_op jit(solution)/shard_map/ppermute | solution.py:177
  55.1 14.4 %collective-permute-start.13 = (bf16[8,256,128]{2,1,0:T(8,128)(2,1)S(1)}, bf16[8,256,128]{2,1,0:T(8,128)(2,1)S(1)}, u32[]{:S(2)}, u32[]{:S(2)}) collective-permute-start(bf16[8,256,128]{2,1,0:T(8,128)(2,1)S(1)} %slice.18), channel_id=1, source_target_pairs={{0,2},{2,4},{4,6},{6,0},{1,3},{3,5},{5,7},{7,1},{8,10},{10,12},{12... | collective-permute-start | bytes 1572872 | tf_op jit(solution)/shard_map/ppermute | solution.py:180
  56.7 15.1 %collective-permute-start.2 = (bf16[2,128,1024]{2,1,0:T(8,128)(2,1)S(1)}, bf16[2,128,1024]{2,1,0:T(8,128)(2,1)S(1)}, u32[]{:S(2)}, u32[]{:S(2)}) collective-permute-start(bf16[2,128,1024]{2,1,0:T(8,128)(2,1)S(1)} %slice.16), channel_id=1, source_target_pairs={{0,8},{8,16},{16,24},{24,0},{1,9},{9,17},{17,25},{25,1},{2,10},{10... | collective-permute-start | bytes 1572872 | tf_op jit(solution)/shard_map/ppermute | solution.py:182
  62.9 8.9 %collective-permute-start.16 = (bf16[8,256,128]{2,1,0:T(8,128)(2,1)S(1)}, bf16[8,256,128]{2,1,0:T(8,128)(2,1)S(1)}, u32[]{:S(2)}, u32[]{:S(2)}) collective-permute-start(bf16[8,256,128]{2,1,0:T(8,128)(2,1)S(1)} %collective-permute-done.15.refs_13_), channel_id=1, source_target_pairs={{0,1},{1,0},{2,3},{3,2},{4,5},{5,4},{6,7},{7,6},{8,9},{9,8},{10,11... | collective-permute-start | bytes 1572872 | tf_op jit(solution)/shard_map/ppermute | solution.py:177
  69.5 2.8 %collective-permute-start.14 = (bf16[8,256,128]{2,1,0:T(8,128)(2,1)S(1)}, bf16[8,256,128]{2,1,0:T(8,128)(2,1)S(1)}, u32[]{:S(2)}, u32[]{:S(2)}) collective-permute-start(bf16[8,256,128]{2,1,0:T(8,128)(2,1)S(1)} %collective-permute-done.13.refs_11_), channel_id=1, source_target_pairs={{0,1},{1,0},{2,3},{3,2},{4,5},{5,4},{6,7},{7,6},{8,9},{9,8},{10,11... | collective-permute-start | bytes 1572872 | tf_op jit(solution)/shard_map/ppermute | solution.py:177
  80.9 32.0 %collective-permute-start.17 = (bf16[528,1024]{1,0:T(8,128)(2,1)S(1)}, bf16[528,1024]{1,0:T(8,128)(2,1)S(1)}, u32[]{:S(2)}, u32[]{:S(2)}) collective-permute-start(bf16[528,1024]{1,0:T(8,128)(2,1)S(1)} %block2.1), channel_id=1, source_target_pairs={{0,64},{32,96},{64,0},{96,32},{1,65},{33,97},{65,1},{97,33},{2,66}... | collective-permute-start | bytes 3244040 | tf_op jit(solution)/shard_map/ppermute | solution.py:184
  92.5 38.9 %collective-permute-start.18 = (bf16[528,1024]{1,0:T(8,128)(2,1)S(1)}, bf16[528,1024]{1,0:T(8,128)(2,1)S(1)}, u32[]{:S(2)}, u32[]{:S(2)}) collective-permute-start(bf16[528,1024]{1,0:T(8,128)(2,1)S(1)} %block1.1), channel_id=1, source_target_pairs={{0,32},{32,64},{64,96},{96,0},{1,33},{33,65},{65,97},{97,1},{2,34}... | collective-permute-start | bytes 3244040 | tf_op jit(solution)/shard_map/ppermute | solution.py:185
  101.5 30.0 %collective-permute-start.19 = (bf16[528,1024]{1,0:T(8,128)(2,1)S(1)}, bf16[528,1024]{1,0:T(8,128)(2,1)S(1)}, u32[]{:S(2)}, u32[]{:S(2)}) collective-permute-start(bf16[528,1024]{1,0:T(8,128)(2,1)S(1)} %block3.1), channel_id=1, source_target_pairs={{0,96},{32,0},{64,32},{96,64},{1,97},{33,1},{65,33},{97,65},{2,98}... | collective-permute-start | bytes 3244040 | tf_op jit(solution)/shard_map/ppermute | solution.py:186
  131.4 1.6 %copy-start.1 = (f32[512,1024]{1,0:T(8,128)S(1)}, f32[512,1024]{1,0:T(8,128)}, u32[]{:S(2)}) copy-start(f32[512,1024]{1,0:T(8,128)} %block0.1.own) | copy-start | bytes 6291460

commit v2 on v0

v2 whole, which is shorter than its diff:
```python
import functools

import jax
import jax.numpy as jnp
from jax import lax
from jax.experimental import pallas as pl
from jax.experimental.pallas import tpu as pltpu
from jax.sharding import Mesh, PartitionSpec as P

BF, F32 = jnp.bfloat16, jnp.float32
ANY = pl.BlockSpec(memory_space=pl.ANY)
VM = pl.BlockSpec(memory_space=pltpu.VMEM)
POWER = 12
TOP = 9.625
VMEM_LIMIT = 16 << 20


def ring(n, k):
    return [(i, (i + k) % n) for i in range(n)]


def code_of(u):
    return jnp.where(u == 0, 0, jnp.where(u == 1, 3, jnp.where(u == 2, 1, 2)))


def source_of(code):
    return jnp.where(code == 0, 0, jnp.where(code == 1, 2, jnp.where(code == 2, 3, 1)))


def round_pairs(k):
    pairs = []
    for z in range(4):
        for c in range(2):
            code = [0, 3, 1, 2][(z - 2 * c) % 4] ^ (2 * k)
            pairs.append((z * 2 + c, (2 * c + code // 2) * 2 + code % 2))
    return pairs


def prep_kernel(a_ref, *o_refs):
    z, c = lax.axis_index("z"), lax.axis_index("c")
    first = code_of(lax.rem(z - 2 * c + 4, 4))
    for k in range(2):
        off = pl.multiple_of(((first ^ (2 * k)) // 2) * 512, 512)
        o_refs[k][0] = a_ref[0, :, pl.ds(off, 512)].T


def prep(a):
    return pl.pallas_call(
        prep_kernel,
        grid=(4,),
        out_shape=[jax.ShapeDtypeStruct((4, 512, 128), BF)] * 2,
        in_specs=[pl.BlockSpec((1, 128, 1024), lambda e: (e, 0, 0))],
        out_specs=[pl.BlockSpec((1, 512, 128), lambda e: (e, 0, 0))] * 2,
        compiler_params=pltpu.CompilerParams(vmem_limit_bytes=VMEM_LIMIT),
        name="prep",
    )(a)


def encode(acc, o_ref):
    rows, cols = acc.shape
    step = 32

    def largest(i, top):
        part = acc[pl.ds(pl.multiple_of(i * step, step), step), :].reshape(step // 8, 8, cols)
        return jnp.maximum(top, jnp.max(part, axis=0))

    top = lax.fori_loop(0, rows // step, largest, jnp.zeros((8, cols), F32))
    top = jnp.max(jnp.max(top, axis=0, keepdims=True), axis=1, keepdims=True)
    k = jnp.clip(jnp.floor(jnp.log2(jnp.maximum(top, 1e-36))), -100.0, 100.0)
    scale = jnp.exp2(TOP - k)

    def power(u):
        u2 = u * u
        u4 = u2 * u2
        return u4 * u4 * u4

    @pl.loop(0, rows // step)
    def _(i):
        at = pl.ds(pl.multiple_of(i * step, step), step)
        o_ref[at, :] = power(acc[at, :] * scale).astype(BF)

    lane, row = (lax.broadcasted_iota(jnp.int32, (16, 128), d) for d in (1, 0))
    shifted = jnp.floor((k + 128.0) * jnp.exp2(-lane.astype(F32)))
    odd = (shifted - 2.0 * jnp.floor(0.5 * shifted)) > 0.5
    t = power(acc[0:16, 0:128] * scale)
    coded = jnp.where(odd, -1.0, 1.0) * jnp.maximum(t, 1e-37)
    o_ref[0:16, 0:128] = jnp.where((row == 0) & (lane < 8), coded, t).astype(BF)


def exponent(p_ref):
    lane, row = (lax.broadcasted_iota(jnp.int32, (16, 128), d) for d in (1, 0))
    bit = (row == 0) & (lane < 8) & (p_ref[0:16, 0:128].astype(F32) < 0)
    value = jnp.where(bit, jnp.exp2(lane.astype(F32)), 0.0)
    return jnp.sum(jnp.sum(value, axis=0, keepdims=True), axis=1, keepdims=True) - 128.0


def decode(t, k):
    t = jnp.abs(t.astype(F32))
    root = jnp.exp2(jnp.log2(jnp.maximum(t, 1e-38)) * (1.0 / POWER))
    return jnp.where(t > 0, root, 0.0) * jnp.exp2(k - TOP)


def gather_kernel(g, gp, h1, h2, gm, o_ref, sem):
    copies = [pltpu.make_async_copy(src, o_ref.at[slot], sem.at[slot]) for slot, src in ((0, g), (1, gp), (3, gm))]
    copies += [pltpu.make_async_copy(src, o_ref.at[2, pl.ds(2 * i, 2)], sem.at[2 + 2 * i]) for i, src in enumerate((h1, h2))]
    for copy in copies:
        copy.start()
    for copy in copies:
        copy.wait()


def gather(*pieces):
    return pl.pallas_call(
        gather_kernel,
        out_shape=jax.ShapeDtypeStruct((4, 4, 128, 1024), BF),
        in_specs=[ANY] * 5,
        out_specs=VM,
        scratch_shapes=[pltpu.SemaphoreType.DMA((5,))],
        compiler_params=pltpu.CompilerParams(vmem_limit_bytes=16 << 20),
        name="gather",
    )(*pieces)


OWN = (((0, 0), (0, 4)), ((2, 0), (2, 4)), ((3, 0), (4, 0)), ((1, 0), (1, 4)))
OTHER = (((5, 0), (5, 4)), ((6, 8), (6, 12)), ((7, 0), (7, 4)), ((6, 0), (6, 4)))


ALL, MINE, THEIRS = (0, 1, 2, 3), (0, 1), (2, 3)
ROWS = (288, 224)


def blocks_kernel(jobs, n_extra, *refs):
    n = len(jobs)
    a_refs, g_ref = refs[:8], refs[8]
    extra = refs[9 : 9 + n_extra]
    outs = refs[9 + n_extra : 9 + n_extra + n]
    a_vm, acc_vm, sem = refs[9 + n_extra + n :]
    x, z, y, c = (lax.axis_index(name) for name in "xzyc")
    odd = lax.rem(z, 2)
    for j, (d, first_row, rows, _, _, _, pieces) in enumerate(jobs):
        r = lax.rem(x - y + d + 4, 4)
        for value in range(4):
            @pl.when(r == value)
            def _():
                for piece in pieces:
                    ref, first = (OWN[value] + OTHER[value])[piece]
                    src = a_refs[ref].at[pl.ds(first, 4), pl.ds(first_row, rows), :]
                    pltpu.make_async_copy(src, a_vm.at[j, piece, :, 0:rows, :], sem.at[j, piece]).start()
    for j, (_, first_row, rows, begin, add, coded, pieces) in enumerate(jobs):
        acc = acc_vm.at[0:rows] if coded else outs[j]
        if begin is None:
            acc[...] = jnp.zeros_like(acc)
        else:
            acc[...] = extra[begin][first_row : first_row + rows, :]

        @pl.loop(pieces[0], pieces[-1] + 1)
        def _(piece):
            core = jnp.where(piece < 2, c, 1 - c)
            slot = lax.rem(source_of((2 * odd + core) ^ (2 * lax.rem(piece, 2))) - odd + 4, 4)
            held = a_vm.at[j, piece, :, 0:rows, :]
            pltpu.make_async_copy(held, held, sem.at[j, piece]).wait()
            for e in range(4):
                v = jnp.dot(a_vm[j, piece, e, 0:rows, :], g_ref[slot, e], preferred_element_type=F32)
                acc[...] += v * v

        if add is not None:
            k = exponent(extra[add])

            @pl.loop(0, rows // 32)
            def _(i):
                at = pl.ds(pl.multiple_of(i * 32, 32), 32)
                acc[at, :] += decode(extra[add][at, :], k)

        if coded:
            encode(acc, outs[j])


def blocks(jobs, a_refs, g, extra=()):
    n = len(jobs)
    most = max(j[2] for j in jobs)
    return pl.pallas_call(
        functools.partial(blocks_kernel, jobs, len(extra)),
        out_shape=[jax.ShapeDtypeStruct((j[2], 1024), BF if j[5] else F32) for j in jobs],
        in_specs=[ANY] * 8 + [VM] * (1 + len(extra)),
        out_specs=[VM] * n,
        scratch_shapes=[
            pltpu.VMEM((n, 4, 4, most, 128), BF),
            pltpu.VMEM((most, 1024), F32),
            pltpu.SemaphoreType.DMA((n, 4)),
        ],
        compiler_params=pltpu.CompilerParams(vmem_limit_bytes=VMEM_LIMIT),
        cost_estimate=pl.CostEstimate(flops=4 * n * 16 * 128 * 512 * 512, bytes_accessed=5 * n << 20, transcendentals=0),
        name="blocks_" + "_".join(f"{j[0] % 4}r{j[1]}" for j in jobs),
    )(*a_refs, g, *extra)


def final_kernel(part, own, p1, p2, *rest):
    o_ref, tmp, sem = rest[-3:]
    rows = ROWS[part]
    k1, k2 = exponent(p1), exponent(p2)

    @pl.loop(0, rows // 32)
    def _(i):
        at = pl.ds(pl.multiple_of(i * 32, 32), 32)
        tmp[at, :] = own[at, :] + decode(p1[at, :], k1) + decode(p2[at, :], k2)
        to = pl.ds(pl.multiple_of(ROWS[0] * part + i * 32, 32), 32)
        pltpu.make_async_copy(tmp.at[at], o_ref.at[to], sem).start()

    pltpu.make_async_copy(tmp, tmp, sem).wait()


def final(part, own, one, two, result=None):
    return pl.pallas_call(
        functools.partial(final_kernel, part),
        out_shape=jax.ShapeDtypeStruct((512, 1024), F32),
        in_specs=[VM] * 3 + ([] if result is None else [ANY]),
        out_specs=ANY,
        scratch_shapes=[pltpu.VMEM((ROWS[part], 1024), F32), pltpu.SemaphoreType.DMA],
        input_output_aliases={} if result is None else {3: 0},
        compiler_params=pltpu.CompilerParams(vmem_limit_bytes=VMEM_LIMIT),
        name=f"final{part}",
    )(own, one, two, *(() if result is None else (result,)))


def send(v, axis, step):
    return lax.ppermute(v, axis, ring(2 if axis == "c" else 4, step))


def body(a, g):
    r0, r1 = (lax.ppermute(p, ("z", "c"), round_pairs(k)) for k, p in enumerate(prep(a)))
    r0, r1, g = lax.optimization_barrier((r0, r1, g))
    s = jnp.concatenate([r0, r1], axis=0)
    sm, sp, gm, gp, sc = send(s, "y", 1), send(s, "y", -1), send(g, "z", 1), send(g, "z", -1), send(s, "c", 1)
    sm, sp, gm, gp, sc = lax.optimization_barrier((sm, sp, gm, gp, sc))
    t1, t2 = send(sm[:4], "y", 1), send(sp[4:], "y", -1)
    h1, h2 = send(gm[:2], "z", 1), send(gp[2:], "z", -1)
    both = send(jnp.concatenate([sm, sp], axis=0), "c", 1)
    t1, t2, h1, h2, both = lax.optimization_barrier((t1, t2, h1, h2, both))
    tc = send(jnp.concatenate([t1, t2], axis=0), "c", 1)
    gs = gather(g, gp, h1, h2, gm)
    a_refs = (s, sm, sp, t1, t2, sc, both, tc)

    def run(jobs, extra=()):
        return blocks(jobs, a_refs, gs, extra)

    def job(d, part, add=None, coded=True):
        return (d, ROWS[0] * part, ROWS[part], None, add, coded, ALL)

    (early,) = blocks(((2, 0, 512, None, None, False, MINE),), (*a_refs[:5], s, s, s), gs)
    (far0,) = run(((2, 0, ROWS[0], 0, None, True, THEIRS),), (early,))
    up0 = send(far0, "x", 1)
    (far1,) = run(((2, ROWS[0], ROWS[1], 0, None, True, THEIRS),), (early,))
    up1 = send(far1, "x", -1)
    left0, right1 = run((job(-1, 0), job(1, 1)))
    left0, right1 = send(left0, "x", -1), send(right1, "x", 1)
    (right0,) = run((job(1, 0, 0),), (up0,))
    right0 = send(right0, "x", 1)
    (left1,) = run((job(-1, 1, 0),), (up1,))
    left1 = send(left1, "x", -1)
    own0, own1 = run((job(0, 0, coded=False), job(0, 1, coded=False)))
    return final(1, own1, left1, right1, final(0, own0, left0, right0))


def solution(mesh):
    fine = Mesh(mesh.devices.reshape(4, 4, 4, 2), ("x", "z", "y", "c"))
    spec = P(("x", "z"), None, ("y", "c"))
    return jax.shard_map(body, mesh=fine, in_specs=(spec, spec), out_specs=P(("x", "z"), ("y", "c")), check_vma=False)
```

time: 342 us -> 120 us (0.35)
  waiting for transfers between devices: 248 us -> 58.1 us
  matrix products: 40.1 us -> 0 us
  local copies, waits for them, and re-layouts: 38.9 us -> 1.48 us
  Pallas kernels: 0 us -> 32.5 us
  starting transfers between devices: 0.04 us -> 27 us
  between operations: 13.4 us -> 0.37 us
    reduce_scatter x1 -> x0, waiting for transfers between devices: 195 us -> none  [body(): lax.psum_scatter(lax.fori_loop(0, lax.axis_size('ex') * own_rows // block...]
    ppermute x0 -> x19, waiting for transfers between devices: none -> 58.1 us  [the longest x17 44.8 us: send(): return lax.ppermute(v, axis, ring(2 if axis == 'c' else 4, step))]
    all_gather x1 -> x0, waiting for transfers between devices: 53.6 us -> none  [body(): whole_inputs = lax.all_gather(activations, 'tp', axis=2, tiled=True)]
    dot_general x16 -> x0, matrix products: 40.1 us -> none  [one_block(): jnp.einsum('etd,etc->edc', window, out_grads, preferred_element_type=jnp....]
    pallas_call x0 -> x11, Pallas kernels: none -> 32.5 us  [the longest x7 28.5 us: blocks(): pl.pallas_call(functools.partial(blocks_kernel, jobs, len(extra)), out_sh...]
    ppermute x0 -> x19, starting transfers between devices: none -> 27 us  [the longest x17 20.6 us: send(): return lax.ppermute(v, axis, ring(2 if axis == 'c' else 4, step))]
    dynamic_update_slice x16 -> x0, local copies, waits for them, and re-layouts: 25.3 us -> none  [one_block(): lax.dynamic_update_slice_in_dim(result, squared, position * block_rows, 0)]
    broadcast_in_dim x1 -> x0, local copies, waits for them, and re-layouts: 11.2 us -> none  [body(): jnp.zeros((lax.axis_size('ex') * own_rows, width_out), jnp.float32)]
  transfers between devices with their start and end apart: 2 -> 19, of which waited for: 2 -> 9; matrix products, arithmetic and copies ran while one was open for 0% -> 0% of each run, Pallas kernels for 0% -> 24%
where the time goes in v2:
time: 120 us
  waiting for transfers between devices  58.1 us (48%)
  Pallas kernels  32.5 us (27%)
  starting transfers between devices  27 us (22%)
  local copies, waits for them, and re-layouts  1.48 us (1%)
    ppermute x17, waiting for transfers between devices, send(): return lax.ppermute(v, axis, ring(2 if axis == 'c' else 4, step))  44.8 us
    pallas_call x7, Pallas kernels, blocks(): pl.pallas_call(functools.partial(blocks_kernel, jobs, len(extra)), out_sh...  28.5 us
    ppermute x17, starting transfers between devices, send(): return lax.ppermute(v, axis, ring(2 if axis == 'c' else 4, step))  20.6 us
    ppermute x2, waiting for transfers between devices, body(): lax.ppermute(p, ('z', 'c'), round_pairs(k))  13.4 us
    ppermute x2, starting transfers between devices, body(): lax.ppermute(p, ('z', 'c'), round_pairs(k))  6.42 us
    pallas_call x2, Pallas kernels, final(): pl.pallas_call(functools.partial(final_kernel, part), out_shape=jax.Shape...  3.07 us
  transfers between devices with their start and end apart: 19, of which 9 were waited for; matrix products, arithmetic and copies ran while one was open for 0% of the time, Pallas kernels for 24%

profile of v2, /device:TPU:1, one launch (start us, length us, event | category | flops | bytes accessed | tf_op | source)
XLA Modules:
  0.0 119.8 jit_solution(2764654748221654060)
XLA Ops:
  0.0 1.2 %copy-done = bf16[4,128,1024]{2,1,0:T(8,128)(2,1)S(1)} copy-done((bf16[4,128,1024]{2,1,0:T(8,128)(2,1)S(1)}, bf16[4,128,1024]{2,1,0:T(8,128)(2,1)}, u32[]{:S(2)}) %copy-start) | copy-done | bytes 1048600
  1.2 0.6 prep.1
  1.8 6.3 %collective-permute-start = (bf16[4,512,128]{2,1,0:T(8,128)(2,1)S(1)}, bf16[4,512,128]{2,1,0:T(8,128)(2,1)S(1)}, u32[]{:S(2)}, u32[]{:S(2)}) collective-permute-start(bf16[4,512,128]{2,1,0:T(8,128)(2,1)S(1)} %get-tuple-element.24), channel_id=1, source_target_pairs={{0,0},{1,17},{8,9},{9,24},{16,1},{17,16},{24,8},{25,25},{2,2},{3,1... | collective-permute-start | bytes 1572872 | tf_op jit(solution)/shard_map/ppermute | solution.py:230
  8.2 0.1 collective-permute-start.1
  8.2 11.2 %collective-permute-done = bf16[4,512,128]{2,1,0:T(8,128)(2,1)S(1)} collective-permute-done((bf16[4,512,128]{2,1,0:T(8,128)(2,1)S(1)}, bf16[4,512,128]{2,1,0:T(8,128)(2,1)S(1)}, u32[]{:S(2)}, u32[]{:S(2)}) %collective-permute-start) | collective-permute-done | bytes 524320 | tf_op jit(solution)/shard_map/ppermute | solution.py:230
  19.4 2.2 %collective-permute-done.1 = bf16[4,512,128]{2,1,0:T(8,128)(2,1)S(1)} collective-permute-done((bf16[4,512,128]{2,1,0:T(8,128)(2,1)S(1)}, bf16[4,512,128]{2,1,0:T(8,128)(2,1)S(1)}, u32[]{:S(2)}, u32[]{:S(2)}) %collective-permute-start.1) | collective-permute-done | bytes 524320 | tf_op jit(solution)/shard_map/ppermute | solution.py:230
  21.6 0.1 constant_dynamic-update-slice_fusion.refs_0_.refs_5_.refs_6_.refs_7_
  21.7 0.3 collective-permute-start.6
  22.1 2.7 %collective-permute-start.3 = (bf16[8,512,128]{2,1,0:T(8,128)(2,1)S(1)}, bf16[8,512,128]{2,1,0:T(8,128)(2,1)S(1)}, u32[]{:S(2)}, u32[]{:S(2)}) collective-permute-start(bf16[8,512,128]{2,1,0:T(8,128)(2,1)S(1)} %constant_dynamic-update-slice_fusion.refs_0_.refs_5_.refs_6_.refs_7_), channel_id=1, source_target_pairs={{0,6},{2,0},{4,2},{6,4},{1,7},{3,1},{5,3},{7,5},{8,14},{10,8},{12,... | collective-permute-start | bytes 3145736 | tf_op jit(solution)/shard_map/ppermute | solution.py:226
  24.8 0.0 collective-permute-start.2
  24.8 2.0 %collective-permute-start.5 = (bf16[4,128,1024]{2,1,0:T(8,128)(2,1)S(1)}, bf16[4,128,1024]{2,1,0:T(8,128)(2,1)S(1)}, u32[]{:S(2)}, u32[]{:S(2)}) collective-permute-start(bf16[4,128,1024]{2,1,0:T(8,128)(2,1)S(1)} %copy-done.1), channel_id=1, source_target_pairs={{0,24},{8,0},{16,8},{24,16},{1,25},{9,1},{17,9},{25,17},{2,26},{10... | collective-permute-start | bytes 3145736 | tf_op jit(solution)/shard_map/ppermute | solution.py:226
  26.8 0.0 collective-permute-start.4
  26.8 0.0 collective-permute-done.6.refs_5_
  26.8 20.3 %collective-permute-done.3.refs_2_ = bf16[8,512,128]{2,1,0:T(8,128)(2,1)S(1)} collective-permute-done((bf16[8,512,128]{2,1,0:T(8,128)(2,1)S(1)}, bf16[8,512,128]{2,1,0:T(8,128)(2,1)S(1)}, u32[]{:S(2)}, u32[]{:S(2)}) %collective-permute-start.3) | collective-permute-done | bytes 1048608 | tf_op jit(solution)/shard_map/ppermute | solution.py:226
  47.1 3.1 %collective-permute-done.2.refs_1_ = bf16[8,512,128]{2,1,0:T(8,128)(2,1)S(1)} collective-permute-done((bf16[8,512,128]{2,1,0:T(8,128)(2,1)S(1)}, bf16[8,512,128]{2,1,0:T(8,128)(2,1)S(1)}, u32[]{:S(2)}, u32[]{:S(2)}) %collective-permute-start.2) | collective-permute-done | bytes 1048608 | tf_op jit(solution)/shard_map/ppermute | solution.py:226
  50.2 0.0 collective-permute-done.5.gp
  50.2 1.9 %collective-permute-done.4.gm = bf16[4,128,1024]{2,1,0:T(8,128)(2,1)S(1)} collective-permute-done((bf16[4,128,1024]{2,1,0:T(8,128)(2,1)S(1)}, bf16[4,128,1024]{2,1,0:T(8,128)(2,1)S(1)}, u32[]{:S(2)}, u32[]{:S(2)}) %collective-permute-start.4) | collective-permute-done | bytes 1048608 | tf_op jit(solution)/shard_map/ppermute | solution.py:226
  52.1 0.2 pad_maximum_fusion
  52.3 1.6 %collective-permute-start.11 = (bf16[16,512,128]{2,1,0:T(8,128)(2,1)S(1)}, bf16[16,512,128]{2,1,0:T(8,128)(2,1)S(1)}, u32[]{:S(2)}, u32[]{:S(2)}) collective-permute-start(bf16[16,512,128]{2,1,0:T(8,128)(2,1)S(1)} %pad_maximum_fusion), channel_id=1, source_target_pairs={{0,1},{1,0},{2,3},{3,2},{4,5},{5,4},{6,7},{7,6},{8,9},{9,8},{10,11... | collective-permute-start | bytes 6291464 | tf_op jit(solution)/shard_map/ppermute | solution.py:226
  54.0 2.7 %collective-permute-start.8 = (bf16[4,512,128]{2,1,0:T(8,128)(2,1)S(1)}, bf16[4,512,128]{2,1,0:T(8,128)(2,1)S(1)}, u32[]{:S(2)}, u32[]{:S(2)}) collective-permute-start(bf16[4,512,128]{2,1,0:T(8,128)(2,1)S(1)} %slice.13), channel_id=1, source_target_pairs={{0,6},{2,0},{4,2},{6,4},{1,7},{3,1},{5,3},{7,5},{8,14},{10,8},{12,... | collective-permute-start | bytes 1572872 | tf_op jit(solution)/shard_map/ppermute | solution.py:226
  56.8 0.0 collective-permute-start.7
  56.8 0.0 collective-permute-start.10
  56.8 1.5 %collective-permute-start.9 = (bf16[2,128,1024]{2,1,0:T(8,128)(2,1)S(1)}, bf16[2,128,1024]{2,1,0:T(8,128)(2,1)S(1)}, u32[]{:S(2)}, u32[]{:S(2)}) collective-permute-start(bf16[2,128,1024]{2,1,0:T(8,128)(2,1)S(1)} %slice.14), channel_id=1, source_target_pairs={{0,8},{8,16},{16,24},{24,0},{1,9},{9,17},{17,25},{25,1},{2,10},{10... | collective-permute-start | bytes 1572872 | tf_op jit(solution)/shard_map/ppermute | solution.py:226
  58.3 9.9 %collective-permute-done.8.refs_4_ = bf16[4,512,128]{2,1,0:T(8,128)(2,1)S(1)} collective-permute-done((bf16[4,512,128]{2,1,0:T(8,128)(2,1)S(1)}, bf16[4,512,128]{2,1,0:T(8,128)(2,1)S(1)}, u32[]{:S(2)}, u32[]{:S(2)}) %collective-permute-start.8) | collective-permute-done | bytes 524320 | tf_op jit(solution)/shard_map/ppermute | solution.py:226
  68.1 3.1 %collective-permute-done.7.refs_3_ = bf16[4,512,128]{2,1,0:T(8,128)(2,1)S(1)} collective-permute-done((bf16[4,512,128]{2,1,0:T(8,128)(2,1)S(1)}, bf16[4,512,128]{2,1,0:T(8,128)(2,1)S(1)}, u32[]{:S(2)}, u32[]{:S(2)}) %collective-permute-start.7) | collective-permute-done | bytes 524320 | tf_op jit(solution)/shard_map/ppermute | solution.py:226
  71.2 0.0 collective-permute-done.10.h2
  71.2 0.0 collective-permute-done.9.h1
  71.2 0.0 collective-permute-done.11.refs_6_
  71.2 0.1 pad_maximum_fusion.1
  71.3 1.2 %collective-permute-start.12 = (bf16[8,512,128]{2,1,0:T(8,128)(2,1)S(1)}, bf16[8,512,128]{2,1,0:T(8,128)(2,1)S(1)}, u32[]{:S(2)}, u32[]{:S(2)}) collective-permute-start(bf16[8,512,128]{2,1,0:T(8,128)(2,1)S(1)} %pad_maximum_fusion.1), channel_id=1, source_target_pairs={{0,1},{1,0},{2,3},{3,2},{4,5},{5,4},{6,7},{7,6},{8,9},{9,8},{10,11... | collective-permute-start | bytes 3145736 | tf_op jit(solution)/shard_map/ppermute | solution.py:226
  72.5 0.3 gather.1.refs_8_
  72.9 2.8 %blocks_2r0.2.refs_9_ = f32[512,1024]{1,0:T(8,128)S(1)} custom-call(bf16[8,512,128]{2,1,0:T(8,128)(2,1)S(1)} %constant_dynamic-update-slice_fusion.refs_0_.refs_5_.refs_6_.refs_7_, bf16[8,512,128]{2,1,0:T(8,128)(2,1)S(1)} %collective-permute-done.2.refs_1_, bf16[8,512,128]{2,1,0:T(8,128)(2,1)S(1)} %collective-permute-done.3.refs_2_, ...), custom_call_target="tpu_custom_call" | custom-call | flops 2147483648 | bytes 5242880 | tf_op jit(solution)/shard_map/blocks_2r0/pallas_call | solution.py:181
  75.7 2.2 %blocks_2r0.3 = bf16[288,1024]{1,0:T(8,128)(2,1)S(1)} custom-call(bf16[8,512,128]{2,1,0:T(8,128)(2,1)S(1)} %constant_dynamic-update-slice_fusion.refs_0_.refs_5_.refs_6_.refs_7_, bf16[8,512,128]{2,1,0:T(8,128)(2,1)S(1)} %collective-permute-done.2.refs_1_, bf16[8,512,128]{2,1,0:T(8,128)(2,1)S(1)} %collective-permute-done.3.refs_2_, ...), custom_call_target="tpu_custom_call" | custom-call | flops 2147483648 | bytes 5242880 | tf_op jit(solution)/shard_map/blocks_2r0/pallas_call | solution.py:181
  77.9 1.3 %collective-permute-start.17 = (bf16[288,1024]{1,0:T(8,128)(2,1)S(1)}, bf16[288,1024]{1,0:T(8,128)(2,1)S(1)}, u32[]{:S(2)}, u32[]{:S(2)}) collective-permute-start(bf16[288,1024]{1,0:T(8,128)(2,1)S(1)} %blocks_2r0.3), channel_id=1, source_target_pairs={{0,32},{32,64},{64,96},{96,0},{1,33},{33,65},{65,97},{97,1},{2,34}... | collective-permute-start | bytes 1769480 | tf_op jit(solution)/shard_map/ppermute | solution.py:226
  79.2 1.9 %blocks_2r288.1 = bf16[224,1024]{1,0:T(8,128)(2,1)S(1)} custom-call(bf16[8,512,128]{2,1,0:T(8,128)(2,1)S(1)} %constant_dynamic-update-slice_fusion.refs_0_.refs_5_.refs_6_.refs_7_, bf16[8,512,128]{2,1,0:T(8,128)(2,1)S(1)} %collective-permute-done.2.refs_1_, bf16[8,512,128]{2,1,0:T(8,128)(2,1)S(1)} %collective-permute-done.3.refs_2_, ...), custom_call_target="tpu_custom_call" | custom-call | flops 2147483648 | bytes 5242880 | tf_op jit(solution)/shard_map/blocks_2r288/pallas_call | solution.py:181
  81.1 1.5 %collective-permute-start.13 = (bf16[224,1024]{1,0:T(8,128)(2,1)S(1)}, bf16[224,1024]{1,0:T(8,128)(2,1)S(1)}, u32[]{:S(2)}, u32[]{:S(2)}) collective-permute-start(bf16[224,1024]{1,0:T(8,128)(2,1)S(1)} %blocks_2r288.1), channel_id=1, source_target_pairs={{0,96},{32,0},{64,32},{96,64},{1,97},{33,1},{65,33},{97,65},{2,98}... | collective-permute-start | bytes 1376264 | tf_op jit(solution)/shard_map/ppermute | solution.py:226
  82.7 7.1 %blocks_3r0_1r288.1 = (bf16[288,1024]{1,0:T(8,128)(2,1)S(1)}, bf16[224,1024]{1,0:T(8,128)(2,1)S(1)}) custom-call(bf16[8,512,128]{2,1,0:T(8,128)(2,1)S(1)} %constant_dynamic-update-slice_fusion.refs_0_.refs_5_.refs_6_.refs_7_, bf16[8,512,128]{2,1,0:T(8,128)(2,1)S(1)} %collective-permute-done.2.refs_1_, ...), custom_call_target="tpu_custom_call" | custom-call | flops 4294967296 | bytes 10485760 | tf_op jit(solution)/shard_map/blocks_3r0_1r288/pallas_call | solution.py:181
  89.8 0.3 collective-permute-start.15
  90.1 2.7 %collective-permute-start.16 = (bf16[288,1024]{1,0:T(8,128)(2,1)S(1)}, bf16[288,1024]{1,0:T(8,128)(2,1)S(1)}, u32[]{:S(2)}, u32[]{:S(2)}) collective-permute-start(bf16[288,1024]{1,0:T(8,128)(2,1)S(1)} %get-tuple-element.42), channel_id=1, source_target_pairs={{0,96},{32,0},{64,32},{96,64},{1,97},{33,1},{65,33},{97,65},{2,98}... | collective-permute-start | bytes 1769480 | tf_op jit(solution)/shard_map/ppermute | solution.py:226
  92.7 1.4 %collective-permute-done.17.refs_9_ = bf16[288,1024]{1,0:T(8,128)(2,1)S(1)} collective-permute-done((bf16[288,1024]{1,0:T(8,128)(2,1)S(1)}, bf16[288,1024]{1,0:T(8,128)(2,1)S(1)}, u32[]{:S(2)}, u32[]{:S(2)}) %collective-permute-start.17) | collective-permute-done | bytes 589856 | tf_op jit(solution)/shard_map/ppermute | solution.py:226
  94.2 4.4 %blocks_1r0.1 = bf16[288,1024]{1,0:T(8,128)(2,1)S(1)} custom-call(bf16[8,512,128]{2,1,0:T(8,128)(2,1)S(1)} %constant_dynamic-update-slice_fusion.refs_0_.refs_5_.refs_6_.refs_7_, bf16[8,512,128]{2,1,0:T(8,128)(2,1)S(1)} %collective-permute-done.2.refs_1_, bf16[8,512,128]{2,1,0:T(8,128)(2,1)S(1)} %collective-permute-done.3.refs_2_, ...), custom_call_target="tpu_custom_call" | custom-call | flops 2147483648 | bytes 5242880 | tf_op jit(solution)/shard_map/blocks_1r0/pallas_call | solution.py:181
  98.6 0.1 collective-permute-start.18
  98.6 3.9 %blocks_3r288.1 = bf16[224,1024]{1,0:T(8,128)(2,1)S(1)} custom-call(bf16[8,512,128]{2,1,0:T(8,128)(2,1)S(1)} %constant_dynamic-update-slice_fusion.refs_0_.refs_5_.refs_6_.refs_7_, bf16[8,512,128]{2,1,0:T(8,128)(2,1)S(1)} %collective-permute-done.2.refs_1_, bf16[8,512,128]{2,1,0:T(8,128)(2,1)S(1)} %collective-permute-done.3.refs_2_, ...), custom_call_target="tpu_custom_call" | custom-call | flops 2147483648 | bytes 5242880 | tf_op jit(solution)/shard_map/blocks_3r288/pallas_call | solution.py:181
  102.5 2.7 %collective-permute-start.14 = (bf16[224,1024]{1,0:T(8,128)(2,1)S(1)}, bf16[224,1024]{1,0:T(8,128)(2,1)S(1)}, u32[]{:S(2)}, u32[]{:S(2)}) collective-permute-start(bf16[224,1024]{1,0:T(8,128)(2,1)S(1)} %blocks_3r288.1), channel_id=1, source_target_pairs={{0,96},{32,0},{64,32},{96,64},{1,97},{33,1},{65,33},{97,65},{2,98}... | collective-permute-start | bytes 1376264 | tf_op jit(solution)/shard_map/ppermute | solution.py:226
  105.2 6.2 %blocks_0r0_0r288.1 = (f32[288,1024]{1,0:T(8,128)S(1)}, f32[224,1024]{1,0:T(8,128)S(1)}) custom-call(bf16[8,512,128]{2,1,0:T(8,128)(2,1)S(1)} %constant_dynamic-update-slice_fusion.refs_0_.refs_5_.refs_6_.refs_7_, bf16[8,512,128]{2,1,0:T(8,128)(2,1)S(1)} %collective-permute-done.2.refs_1_, bf16[8,512,128]{2,1,0:T(8,128)(2,1)S(1)} %collective-permute-done.3.refs_2_, ...), custom_call_target="tpu_custom_call" | custom-call | flops 4294967296 | bytes 10485760 | tf_op jit(solution)/shard_map/blocks_0r0_0r288/pallas_call | solution.py:181
  111.4 5.1 %collective-permute-done.18.p2 = bf16[288,1024]{1,0:T(8,128)(2,1)S(1)} collective-permute-done((bf16[288,1024]{1,0:T(8,128)(2,1)S(1)}, bf16[288,1024]{1,0:T(8,128)(2,1)S(1)}, u32[]{:S(2)}, u32[]{:S(2)}) %collective-permute-start.18) | collective-permute-done | bytes 589856 | tf_op jit(solution)/shard_map/ppermute | solution.py:226
  116.5 1.6 %final0.1.rest_0_ = f32[512,1024]{1,0:T(8,128)} custom-call(f32[288,1024]{1,0:T(8,128)S(1)} %get-tuple-element.41.own, bf16[288,1024]{1,0:T(8,128)(2,1)S(1)} %collective-permute-done.16.p1, bf16[288,1024]{1,0:T(8,128)(2,1)S(1)} %collective-permute-done.18.p2), custom_call_target="tpu_custom_call" | custom-call | tf_op jit(solution)/shard_map/final0/pallas_call | solution.py:213
  118.2 1.4 %final1.1 = f32[512,1024]{1,0:T(8,128)} custom-call(f32[224,1024]{1,0:T(8,128)S(1)} %get-tuple-element.39.own, bf16[224,1024]{1,0:T(8,128)(2,1)S(1)} %collective-permute-done.14.p1, bf16[224,1024]{1,0:T(8,128)(2,1)S(1)} %collective-permute-done.15.p2, f32[512,1024]{1,0:T(8,128)} %final0.1.rest_0_), custom_call_target="tpu_custom_call", output_to_operand_aliasing={{}: (3, {})} | custom-call | tf_op jit(solution)/shard_map/final1/pallas_call | solution.py:213
  (13 shorter events, 0.2 us)
Async XLA Ops:
  0.0 1.2 %copy-start = (bf16[4,128,1024]{2,1,0:T(8,128)(2,1)S(1)}, bf16[4,128,1024]{2,1,0:T(8,128)(2,1)}, u32[]{:S(2)}) copy-start(bf16[4,128,1024]{2,1,0:T(8,128)(2,1)} %a_ref.1) | copy-start | bytes 3145732
  1.2 23.6 %copy-start.1 = (bf16[4,128,1024]{2,1,0:T(8,128)(2,1)S(1)}, bf16[4,128,1024]{2,1,0:T(8,128)(2,1)}, u32[]{:S(2)}) copy-start(bf16[4,128,1024]{2,1,0:T(8,128)(2,1)} %g) | copy-start | bytes 3145732
  1.8 17.6 %collective-permute-start = (bf16[4,512,128]{2,1,0:T(8,128)(2,1)S(1)}, bf16[4,512,128]{2,1,0:T(8,128)(2,1)S(1)}, u32[]{:S(2)}, u32[]{:S(2)}) collective-permute-start(bf16[4,512,128]{2,1,0:T(8,128)(2,1)S(1)} %get-tuple-element.24), channel_id=1, source_target_pairs={{0,0},{1,17},{8,9},{9,24},{16,1},{17,16},{24,8},{25,25},{2,2},{3,1... | collective-permute-start | bytes 1572872 | tf_op jit(solution)/shard_map/ppermute | solution.py:230
  8.2 13.5 %collective-permute-start.1 = (bf16[4,512,128]{2,1,0:T(8,128)(2,1)S(1)}, bf16[4,512,128]{2,1,0:T(8,128)(2,1)S(1)}, u32[]{:S(2)}, u32[]{:S(2)}) collective-permute-start(bf16[4,512,128]{2,1,0:T(8,128)(2,1)S(1)} %get-tuple-element.25), channel_id=1, source_target_pairs={{0,8},{1,25},{8,1},{9,16},{16,9},{17,24},{24,0},{25,17},{2,10},{3,... | collective-permute-start | bytes 1572872 | tf_op jit(solution)/shard_map/ppermute | solution.py:230
  21.7 5.1 %collective-permute-start.6 = (bf16[8,512,128]{2,1,0:T(8,128)(2,1)S(1)}, bf16[8,512,128]{2,1,0:T(8,128)(2,1)S(1)}, u32[]{:S(2)}, u32[]{:S(2)}) collective-permute-start(bf16[8,512,128]{2,1,0:T(8,128)(2,1)S(1)} %constant_dynamic-update-slice_fusion.refs_0_.refs_5_.refs_6_.refs_7_), channel_id=1, source_target_pairs={{0,1},{1,0},{2,3},{3,2},{4,5},{5,4},{6,7},{7,6},{8,9},{9,8},{10,11... | collective-permute-start | bytes 3145736 | tf_op jit(solution)/shard_map/ppermute | solution.py:226
  22.1 25.0 %collective-permute-start.3 = (bf16[8,512,128]{2,1,0:T(8,128)(2,1)S(1)}, bf16[8,512,128]{2,1,0:T(8,128)(2,1)S(1)}, u32[]{:S(2)}, u32[]{:S(2)}) collective-permute-start(bf16[8,512,128]{2,1,0:T(8,128)(2,1)S(1)} %constant_dynamic-update-slice_fusion.refs_0_.refs_5_.refs_6_.refs_7_), channel_id=1, source_target_pairs={{0,6},{2,0},{4,2},{6,4},{1,7},{3,1},{5,3},{7,5},{8,14},{10,8},{12,... | collective-permute-start | bytes 3145736 | tf_op jit(solution)/shard_map/ppermute | solution.py:226
  24.8 25.4 %collective-permute-start.2 = (bf16[8,512,128]{2,1,0:T(8,128)(2,1)S(1)}, bf16[8,512,128]{2,1,0:T(8,128)(2,1)S(1)}, u32[]{:S(2)}, u32[]{:S(2)}) collective-permute-start(bf16[8,512,128]{2,1,0:T(8,128)(2,1)S(1)} %constant_dynamic-update-slice_fusion.refs_0_.refs_5_.refs_6_.refs_7_), channel_id=1, source_target_pairs={{0,2},{2,4},{4,6},{6,0},{1,3},{3,5},{5,7},{7,1},{8,10},{10,12},{12... | collective-permute-start | bytes 3145736 | tf_op jit(solution)/shard_map/ppermute | solution.py:226
  24.8 25.4 %collective-permute-start.5 = (bf16[4,128,1024]{2,1,0:T(8,128)(2,1)S(1)}, bf16[4,128,1024]{2,1,0:T(8,128)(2,1)S(1)}, u32[]{:S(2)}, u32[]{:S(2)}) collective-permute-start(bf16[4,128,1024]{2,1,0:T(8,128)(2,1)S(1)} %copy-done.1), channel_id=1, source_target_pairs={{0,24},{8,0},{16,8},{24,16},{1,25},{9,1},{17,9},{25,17},{2,26},{10... | collective-permute-start | bytes 3145736 | tf_op jit(solution)/shard_map/ppermute | solution.py:226
  26.8 25.3 %collective-permute-start.4 = (bf16[4,128,1024]{2,1,0:T(8,128)(2,1)S(1)}, bf16[4,128,1024]{2,1,0:T(8,128)(2,1)S(1)}, u32[]{:S(2)}, u32[]{:S(2)}) collective-permute-start(bf16[4,128,1024]{2,1,0:T(8,128)(2,1)S(1)} %copy-done.1), channel_id=1, source_target_pairs={{0,8},{8,16},{16,24},{24,0},{1,9},{9,17},{17,25},{25,1},{2,10},{10... | collective-permute-start | bytes 3145736 | tf_op jit(solution)/shard_map/ppermute | solution.py:226
  52.3 18.9 %collective-permute-start.11 = (bf16[16,512,128]{2,1,0:T(8,128)(2,1)S(1)}, bf16[16,512,128]{2,1,0:T(8,128)(2,1)S(1)}, u32[]{:S(2)}, u32[]{:S(2)}) collective-permute-start(bf16[16,512,128]{2,1,0:T(8,128)(2,1)S(1)} %pad_maximum_fusion), channel_id=1, source_target_pairs={{0,1},{1,0},{2,3},{3,2},{4,5},{5,4},{6,7},{7,6},{8,9},{9,8},{10,11... | collective-permute-start | bytes 6291464 | tf_op jit(solution)/shard_map/ppermute | solution.py:226
  54.0 14.1 %collective-permute-start.8 = (bf16[4,512,128]{2,1,0:T(8,128)(2,1)S(1)}, bf16[4,512,128]{2,1,0:T(8,128)(2,1)S(1)}, u32[]{:S(2)}, u32[]{:S(2)}) collective-permute-start(bf16[4,512,128]{2,1,0:T(8,128)(2,1)S(1)} %slice.13), channel_id=1, source_target_pairs={{0,6},{2,0},{4,2},{6,4},{1,7},{3,1},{5,3},{7,5},{8,14},{10,8},{12,... | collective-permute-start | bytes 1572872 | tf_op jit(solution)/shard_map/ppermute | solution.py:226
  56.8 14.4 %collective-permute-start.7 = (bf16[4,512,128]{2,1,0:T(8,128)(2,1)S(1)}, bf16[4,512,128]{2,1,0:T(8,128)(2,1)S(1)}, u32[]{:S(2)}, u32[]{:S(2)}) collective-permute-start(bf16[4,512,128]{2,1,0:T(8,128)(2,1)S(1)} %slice.12), channel_id=1, source_target_pairs={{0,2},{2,4},{4,6},{6,0},{1,3},{3,5},{5,7},{7,1},{8,10},{10,12},{12... | collective-permute-start | bytes 1572872 | tf_op jit(solution)/shard_map/ppermute | solution.py:226
  56.8 14.4 %collective-permute-start.10 = (bf16[2,128,1024]{2,1,0:T(8,128)(2,1)S(1)}, bf16[2,128,1024]{2,1,0:T(8,128)(2,1)S(1)}, u32[]{:S(2)}, u32[]{:S(2)}) collective-permute-start(bf16[2,128,1024]{2,1,0:T(8,128)(2,1)S(1)} %slice.15), channel_id=1, source_target_pairs={{0,24},{8,0},{16,8},{24,16},{1,25},{9,1},{17,9},{25,17},{2,26},{10... | collective-permute-start | bytes 1572872 | tf_op jit(solution)/shard_map/ppermute | solution.py:226
  56.8 14.4 %collective-permute-start.9 = (bf16[2,128,1024]{2,1,0:T(8,128)(2,1)S(1)}, bf16[2,128,1024]{2,1,0:T(8,128)(2,1)S(1)}, u32[]{:S(2)}, u32[]{:S(2)}) collective-permute-start(bf16[2,128,1024]{2,1,0:T(8,128)(2,1)S(1)} %slice.14), channel_id=1, source_target_pairs={{0,8},{8,16},{16,24},{24,0},{1,9},{9,17},{17,25},{25,1},{2,10},{10... | collective-permute-start | bytes 1572872 | tf_op jit(solution)/shard_map/ppermute | solution.py:226
  71.3 4.3 %collective-permute-start.12 = (bf16[8,512,128]{2,1,0:T(8,128)(2,1)S(1)}, bf16[8,512,128]{2,1,0:T(8,128)(2,1)S(1)}, u32[]{:S(2)}, u32[]{:S(2)}) collective-permute-start(bf16[8,512,128]{2,1,0:T(8,128)(2,1)S(1)} %pad_maximum_fusion.1), channel_id=1, source_target_pairs={{0,1},{1,0},{2,3},{3,2},{4,5},{5,4},{6,7},{7,6},{8,9},{9,8},{10,11... | collective-permute-start | bytes 3145736 | tf_op jit(solution)/shard_map/ppermute | solution.py:226
  77.9 16.2 %collective-permute-start.17 = (bf16[288,1024]{1,0:T(8,128)(2,1)S(1)}, bf16[288,1024]{1,0:T(8,128)(2,1)S(1)}, u32[]{:S(2)}, u32[]{:S(2)}) collective-permute-start(bf16[288,1024]{1,0:T(8,128)(2,1)S(1)} %blocks_2r0.3), channel_id=1, source_target_pairs={{0,32},{32,64},{64,96},{96,0},{1,33},{33,65},{65,97},{97,1},{2,34}... | collective-permute-start | bytes 1769480 | tf_op jit(solution)/shard_map/ppermute | solution.py:226
  81.1 17.5 %collective-permute-start.13 = (bf16[224,1024]{1,0:T(8,128)(2,1)S(1)}, bf16[224,1024]{1,0:T(8,128)(2,1)S(1)}, u32[]{:S(2)}, u32[]{:S(2)}) collective-permute-start(bf16[224,1024]{1,0:T(8,128)(2,1)S(1)} %blocks_2r288.1), channel_id=1, source_target_pairs={{0,96},{32,0},{64,32},{96,64},{1,97},{33,1},{65,33},{97,65},{2,98}... | collective-permute-start | bytes 1376264 | tf_op jit(solution)/shard_map/ppermute | solution.py:226
  89.8 28.4 %collective-permute-start.15 = (bf16[224,1024]{1,0:T(8,128)(2,1)S(1)}, bf16[224,1024]{1,0:T(8,128)(2,1)S(1)}, u32[]{:S(2)}, u32[]{:S(2)}) collective-permute-start(bf16[224,1024]{1,0:T(8,128)(2,1)S(1)} %get-tuple-element.40), channel_id=1, source_target_pairs={{0,32},{32,64},{64,96},{96,0},{1,33},{33,65},{65,97},{97,1},{2,34}... | collective-permute-start | bytes 1376264 | tf_op jit(solution)/shard_map/ppermute | solution.py:226
  90.1 21.4 %collective-permute-start.16 = (bf16[288,1024]{1,0:T(8,128)(2,1)S(1)}, bf16[288,1024]{1,0:T(8,128)(2,1)S(1)}, u32[]{:S(2)}, u32[]{:S(2)}) collective-permute-start(bf16[288,1024]{1,0:T(8,128)(2,1)S(1)} %get-tuple-element.42), channel_id=1, source_target_pairs={{0,96},{32,0},{64,32},{96,64},{1,97},{33,1},{65,33},{97,65},{2,98}... | collective-permute-start | bytes 1769480 | tf_op jit(solution)/shard_map/ppermute | solution.py:226
  98.6 18.0 %collective-permute-start.18 = (bf16[288,1024]{1,0:T(8,128)(2,1)S(1)}, bf16[288,1024]{1,0:T(8,128)(2,1)S(1)}, u32[]{:S(2)}, u32[]{:S(2)}) collective-permute-start(bf16[288,1024]{1,0:T(8,128)(2,1)S(1)} %blocks_1r0.1), channel_id=1, source_target_pairs={{0,32},{32,64},{64,96},{96,0},{1,33},{33,65},{65,97},{97,1},{2,34}... | collective-permute-start | bytes 1769480 | tf_op jit(solution)/shard_map/ppermute | solution.py:226
  102.5 15.7 %collective-permute-start.14 = (bf16[224,1024]{1,0:T(8,128)(2,1)S(1)}, bf16[224,1024]{1,0:T(8,128)(2,1)S(1)}, u32[]{:S(2)}, u32[]{:S(2)}) collective-permute-start(bf16[224,1024]{1,0:T(8,128)(2,1)S(1)} %blocks_3r288.1), channel_id=1, source_target_pairs={{0,96},{32,0},{64,32},{96,64},{1,97},{33,1},{65,33},{97,65},{2,98}... | collective-permute-start | bytes 1376264 | tf_op jit(solution)/shard_map/ppermute | solution.py:226

commit v3 on v2

--- a/solution.py
+++ b/solution.py
@@ -36,21 +36,26 @@
     return pairs
 
 
-def prep_kernel(a_ref, *o_refs):
+def prep_kernel(a_ref, o0_ref, o1_ref, a_vm, sem):
     z, c = lax.axis_index("z"), lax.axis_index("c")
     first = code_of(lax.rem(z - 2 * c + 4, 4))
-    for k in range(2):
-        off = pl.multiple_of(((first ^ (2 * k)) // 2) * 512, 512)
-        o_refs[k][0] = a_ref[0, :, pl.ds(off, 512)].T
+    copies = [pltpu.make_async_copy(a_ref.at[e], a_vm.at[e], sem.at[e]) for e in range(4)]
+    for copy in copies:
+        copy.start()
+    for e in range(4):
+        copies[e].wait()
+        for k, o_ref in enumerate((o0_ref, o1_ref)):
+            off = pl.multiple_of(((first ^ (2 * k)) // 2) * 512, 512)
+            o_ref[e] = a_vm[e, :, pl.ds(off, 512)].T
 
 
 def prep(a):
     return pl.pallas_call(
         prep_kernel,
-        grid=(4,),
         out_shape=[jax.ShapeDtypeStruct((4, 512, 128), BF)] * 2,
-        in_specs=[pl.BlockSpec((1, 128, 1024), lambda e: (e, 0, 0))],
-        out_specs=[pl.BlockSpec((1, 512, 128), lambda e: (e, 0, 0))] * 2,
+        in_specs=[pl.BlockSpec(memory_space=pltpu.HBM)],
+        out_specs=[VM] * 2,
+        scratch_shapes=[pltpu.VMEM((4, 128, 1024), BF), pltpu.SemaphoreType.DMA((4,))],
         compiler_params=pltpu.CompilerParams(vmem_limit_bytes=VMEM_LIMIT),
         name="prep",
     )(a)
@@ -58,7 +63,7 @@
 
 def encode(acc, o_ref):
     rows, cols = acc.shape
-    step = 32
+    step = 16
 
     def largest(i, top):
         part = acc[pl.ds(pl.multiple_of(i * step, step), step), :].reshape(step // 8, 8, cols)
@@ -100,9 +105,18 @@
     return jnp.where(t > 0, root, 0.0) * jnp.exp2(k - TOP)
 
 
-def gather_kernel(g, gp, h1, h2, gm, o_ref, sem):
-    copies = [pltpu.make_async_copy(src, o_ref.at[slot], sem.at[slot]) for slot, src in ((0, g), (1, gp), (3, gm))]
-    copies += [pltpu.make_async_copy(src, o_ref.at[2, pl.ds(2 * i, 2)], sem.at[2 + 2 * i]) for i, src in enumerate((h1, h2))]
+def gather_kernel(g, za, zb, zac, zbc, fa, fb, o_ref, sem):
+    c = lax.axis_index("c")
+    near, far = jnp.where(c == 0, 3, 1), jnp.where(c == 0, 1, 3)
+    copies = [
+        pltpu.make_async_copy(g, o_ref.at[0], sem.at[0]),
+        pltpu.make_async_copy(za.at[0], o_ref.at[near, 0:2], sem.at[1]),
+        pltpu.make_async_copy(zb.at[0], o_ref.at[near, 2:4], sem.at[2]),
+        pltpu.make_async_copy(zac, o_ref.at[far, 0:2], sem.at[3]),
+        pltpu.make_async_copy(zbc, o_ref.at[far, 2:4], sem.at[6]),
+        pltpu.make_async_copy(fa, o_ref.at[2, 0:2], sem.at[4]),
+        pltpu.make_async_copy(fb, o_ref.at[2, 2:4], sem.at[5]),
+    ]
     for copy in copies:
         copy.start()
     for copy in copies:
@@ -113,37 +127,41 @@
     return pl.pallas_call(
         gather_kernel,
         out_shape=jax.ShapeDtypeStruct((4, 4, 128, 1024), BF),
-        in_specs=[ANY] * 5,
+        in_specs=[ANY] * 7,
         out_specs=VM,
-        scratch_shapes=[pltpu.SemaphoreType.DMA((5,))],
-        compiler_params=pltpu.CompilerParams(vmem_limit_bytes=16 << 20),
+        scratch_shapes=[pltpu.SemaphoreType.DMA((7,))],
+        compiler_params=pltpu.CompilerParams(vmem_limit_bytes=VMEM_LIMIT),
         name="gather",
     )(*pieces)
 
 
-OWN = (((0, 0), (0, 4)), ((2, 0), (2, 4)), ((3, 0), (4, 0)), ((1, 0), (1, 4)))
-OTHER = (((5, 0), (5, 4)), ((6, 8), (6, 12)), ((7, 0), (7, 4)), ((6, 0), (6, 4)))
-
-
+PIECES = {
+    (0, None): ((0, 0), (1, 0), (2, 0), (3, 0)),
+    (2, None): ((8, 0), (9, 0), (10, 0), (10, 4)),
+    (3, 0): ((4, 0), (5, 0), (4, 4), (5, 4)),
+    (3, 1): ((6, 4), (7, 4), (6, 0), (7, 0)),
+    (1, 0): ((6, 4), (7, 4), (6, 0), (7, 0)),
+    (1, 1): ((4, 0), (5, 0), (4, 4), (5, 4)),
+}
 ALL, MINE, THEIRS = (0, 1, 2, 3), (0, 1), (2, 3)
-ROWS = (288, 224)
+ROWS = (272, 240)
 
 
 def blocks_kernel(jobs, n_extra, *refs):
     n = len(jobs)
-    a_refs, g_ref = refs[:8], refs[8]
-    extra = refs[9 : 9 + n_extra]
-    outs = refs[9 + n_extra : 9 + n_extra + n]
-    a_vm, acc_vm, sem = refs[9 + n_extra + n :]
+    a_refs, g_ref = refs[:11], refs[11]
+    extra = refs[12 : 12 + n_extra]
+    outs = refs[12 + n_extra : 12 + n_extra + n]
+    a_vm, acc_vm, sem = refs[12 + n_extra + n :]
     x, z, y, c = (lax.axis_index(name) for name in "xzyc")
     odd = lax.rem(z, 2)
     for j, (d, first_row, rows, _, _, _, pieces) in enumerate(jobs):
         r = lax.rem(x - y + d + 4, 4)
-        for value in range(4):
-            @pl.when(r == value)
+        for (value, on_core), places in PIECES.items():
+            @pl.when(r == value if on_core is None else (r == value) & (c == on_core))
             def _():
                 for piece in pieces:
-                    ref, first = (OWN[value] + OTHER[value])[piece]
+                    ref, first = places[piece]
                     src = a_refs[ref].at[pl.ds(first, 4), pl.ds(first_row, rows), :]
                     pltpu.make_async_copy(src, a_vm.at[j, piece, :, 0:rows, :], sem.at[j, piece]).start()
     for j, (_, first_row, rows, begin, add, coded, pieces) in enumerate(jobs):
@@ -166,9 +184,9 @@
         if add is not None:
             k = exponent(extra[add])
 
-            @pl.loop(0, rows // 32)
+            @pl.loop(0, rows // 16)
             def _(i):
-                at = pl.ds(pl.multiple_of(i * 32, 32), 32)
+                at = pl.ds(pl.multiple_of(i * 16, 16), 16)
                 acc[at, :] += decode(extra[add][at, :], k)
 
         if coded:
@@ -181,7 +199,7 @@
     return pl.pallas_call(
         functools.partial(blocks_kernel, jobs, len(extra)),
         out_shape=[jax.ShapeDtypeStruct((j[2], 1024), BF if j[5] else F32) for j in jobs],
-        in_specs=[ANY] * 8 + [VM] * (1 + len(extra)),
+        in_specs=[ANY] * 11 + [VM] * (1 + len(extra)),
         out_specs=[VM] * n,
         scratch_shapes=[
             pltpu.VMEM((n, 4, 4, most, 128), BF),
@@ -194,51 +212,68 @@
     )(*a_refs, g, *extra)
 
 
-def final_kernel(part, own, p1, p2, *rest):
+def final_kernel(part, own, p, *rest):
     o_ref, tmp, sem = rest[-3:]
     rows = ROWS[part]
-    k1, k2 = exponent(p1), exponent(p2)
-
-    @pl.loop(0, rows // 32)
+    k = exponent(p)
+
+    @pl.loop(0, rows // 16)
     def _(i):
-        at = pl.ds(pl.multiple_of(i * 32, 32), 32)
-        tmp[at, :] = own[at, :] + decode(p1[at, :], k1) + decode(p2[at, :], k2)
-        to = pl.ds(pl.multiple_of(ROWS[0] * part + i * 32, 32), 32)
+        at = pl.ds(pl.multiple_of(i * 16, 16), 16)
+        tmp[at, :] = own[at, :] + decode(p[at, :], k)
+        to = pl.ds(pl.multiple_of(ROWS[0] * part + i * 16, 16), 16)
         pltpu.make_async_copy(tmp.at[at], o_ref.at[to], sem).start()
 
     pltpu.make_async_copy(tmp, tmp, sem).wait()
 
 
-def final(part, own, one, two, result=None):
+def final(part, own, payload, result=None):
     return pl.pallas_call(
         functools.partial(final_kernel, part),
         out_shape=jax.ShapeDtypeStruct((512, 1024), F32),
-        in_specs=[VM] * 3 + ([] if result is None else [ANY]),
+        in_specs=[VM] * 2 + ([] if result is None else [ANY]),
         out_specs=ANY,
         scratch_shapes=[pltpu.VMEM((ROWS[part], 1024), F32), pltpu.SemaphoreType.DMA],
-        input_output_aliases={} if result is None else {3: 0},
+        input_output_aliases={} if result is None else {2: 0},
         compiler_params=pltpu.CompilerParams(vmem_limit_bytes=VMEM_LIMIT),
         name=f"final{part}",
-    )(own, one, two, *(() if result is None else (result,)))
+    )(own, payload, *(() if result is None else (result,)))
 
 
 def send(v, axis, step):
     return lax.ppermute(v, axis, ring(2 if axis == "c" else 4, step))
 
 
+def both_ways(v, axis):
+    pairs = [(2 * i, 2 * ((i + 1) % 4)) for i in range(4)] + [(2 * i + 1, 2 * ((i + 3) % 4) + 1) for i in range(4)]
+    return lax.ppermute(v, (axis, "c"), pairs)
+
+
+def cross(v):
+    return send(v, "c", 1)
+
+
 def body(a, g):
+    hold = lax.optimization_barrier
+    gc = cross(g)
     r0, r1 = (lax.ppermute(p, ("z", "c"), round_pairs(k)) for k, p in enumerate(prep(a)))
-    r0, r1, g = lax.optimization_barrier((r0, r1, g))
-    s = jnp.concatenate([r0, r1], axis=0)
-    sm, sp, gm, gp, sc = send(s, "y", 1), send(s, "y", -1), send(g, "z", 1), send(g, "z", -1), send(s, "c", 1)
-    sm, sp, gm, gp, sc = lax.optimization_barrier((sm, sp, gm, gp, sc))
-    t1, t2 = send(sm[:4], "y", 1), send(sp[4:], "y", -1)
-    h1, h2 = send(gm[:2], "z", 1), send(gp[2:], "z", -1)
-    both = send(jnp.concatenate([sm, sp], axis=0), "c", 1)
-    t1, t2, h1, h2, both = lax.optimization_barrier((t1, t2, h1, h2, both))
-    tc = send(jnp.concatenate([t1, t2], axis=0), "c", 1)
-    gs = gather(g, gp, h1, h2, gm)
-    a_refs = (s, sm, sp, t1, t2, sc, both, tc)
+    r0, r1, gc = hold((r0, r1, gc))
+    r1c, r0c = cross(r1), cross(r0)
+    za = both_ways(jnp.stack([g[:2], gc[:2]]), "z")
+    zb = both_ways(jnp.stack([g[2:], gc[2:]]), "z")
+    m1 = both_ways(jnp.concatenate([r1, r1c]), "y")
+    m0 = both_ways(jnp.concatenate([r0, r0c]), "y")
+    m1, za = hold((m1, za))
+    f1, fa, m1c = both_ways(m1[:4], "y"), both_ways(za[0], "z"), cross(m1)
+    zac = cross(za[1])
+    m0, zb, m1c, zac = hold((m0, zb, m1c, zac))
+    f0, fb, m0c = both_ways(m0[:4], "y"), both_ways(zb[0], "z"), cross(m0)
+    f1, zbh = hold((f1, zb[1]))
+    zbc = cross(zbh)
+    f0, f1, fa, fb, m0c, zac, zbc = hold((f0, f1, fa, fb, m0c, zac, zbc))
+    fc = cross(jnp.concatenate([f0, f1]))
+    gs = gather(g, za, zb, zac, zbc, fa, fb)
+    a_refs = (r0, r1, r0c, r1c, m0, m1, m0c, m1c, f0, f1, fc)
 
     def run(jobs, extra=()):
         return blocks(jobs, a_refs, gs, extra)
@@ -246,19 +281,22 @@
     def job(d, part, add=None, coded=True):
         return (d, ROWS[0] * part, ROWS[part], None, add, coded, ALL)
 
-    (early,) = blocks(((2, 0, 512, None, None, False, MINE),), (*a_refs[:5], s, s, s), gs)
+    (early,) = blocks(((2, 0, 512, None, None, False, MINE),), (*a_refs[:10], r0), gs)
     (far0,) = run(((2, 0, ROWS[0], 0, None, True, THEIRS),), (early,))
     up0 = send(far0, "x", 1)
     (far1,) = run(((2, ROWS[0], ROWS[1], 0, None, True, THEIRS),), (early,))
     up1 = send(far1, "x", -1)
-    left0, right1 = run((job(-1, 0), job(1, 1)))
-    left0, right1 = send(left0, "x", -1), send(right1, "x", 1)
+    (left0,) = run((job(-1, 0),))
+    left0 = send(left0, "x", -1)
+    (right1,) = run((job(1, 1),))
+    right1 = send(right1, "x", 1)
     (right0,) = run((job(1, 0, 0),), (up0,))
     right0 = send(right0, "x", 1)
     (left1,) = run((job(-1, 1, 0),), (up1,))
     left1 = send(left1, "x", -1)
-    own0, own1 = run((job(0, 0, coded=False), job(0, 1, coded=False)))
-    return final(1, own1, left1, right1, final(0, own0, left0, right0))
+    (own1,) = run((job(0, 1, 0, False),), (right1,))
+    (own0,) = run((job(0, 0, 0, False),), (left0,))
+    return final(1, own1, left1, final(0, own0, right0))
 
 
 def solution(mesh):

time: 120 us -> 115 us (0.958)
  waiting for transfers between devices: 58.1 us -> 41.8 us
  starting transfers between devices: 27 us -> 35.4 us
  Pallas kernels: 32.5 us -> 34.4 us
  local copies, waits for them, and re-layouts: 1.48 us -> 2.82 us
    ppermute x17 -> x14, waiting for transfers between devices: 44.8 us -> 4.75 us  [send(): return lax.ppermute(v, axis, ring(2 if axis == 'c' else 4, step))]
    ppermute x0 -> x8, waiting for transfers between devices: none -> 24.3 us  [both_ways(): return lax.ppermute(v, (axis, 'c'), pairs)]
    ppermute x0 -> x8, starting transfers between devices: none -> 12.6 us  [both_ways(): return lax.ppermute(v, (axis, 'c'), pairs)]
    ppermute x17 -> x14, starting transfers between devices: 20.6 us -> 17.2 us  [send(): return lax.ppermute(v, axis, ring(2 if axis == 'c' else 4, step))]
    pallas_call x7 -> x9, Pallas kernels: 28.5 us -> 30.8 us  [blocks(): pl.pallas_call(functools.partial(blocks_kernel, jobs, len(extra)), out_sh...]
    another operation x0 -> x2, local copies, waits for them, and re-layouts: none -> 1.34 us  [body(): za = both_ways(jnp.stack([g[:2], gc[:2]]), 'z')]
  transfers between devices with their start and end apart: 19 -> 24, of which waited for: 9 -> 13; matrix products, arithmetic and copies ran while one was open for 0% -> 2% of each run, Pallas kernels for 24% -> 27%
where the time goes in v3:
time: 115 us
  waiting for transfers between devices  41.8 us (36%)
  starting transfers between devices  35.4 us (31%)
  Pallas kernels  34.4 us (30%)
  local copies, waits for them, and re-layouts  2.82 us (2%)
    pallas_call x9, Pallas kernels, blocks(): pl.pallas_call(functools.partial(blocks_kernel, jobs, len(extra)), out_sh...  30.8 us
    ppermute x8, waiting for transfers between devices, both_ways(): return lax.ppermute(v, (axis, 'c'), pairs)  24.3 us
    ppermute x14, starting transfers between devices, send(): return lax.ppermute(v, axis, ring(2 if axis == 'c' else 4, step))  17.2 us
    ppermute x2, waiting for transfers between devices, body(): lax.ppermute(p, ('z', 'c'), round_pairs(k))  12.7 us
    ppermute x8, starting transfers between devices, both_ways(): return lax.ppermute(v, (axis, 'c'), pairs)  12.6 us
    ppermute x2, starting transfers between devices, body(): lax.ppermute(p, ('z', 'c'), round_pairs(k))  5.67 us
    ppermute x14, waiting for transfers between devices, send(): return lax.ppermute(v, axis, ring(2 if axis == 'c' else 4, step))  4.75 us
    pallas_call x2, Pallas kernels, final(): pl.pallas_call(functools.partial(final_kernel, part), out_shape=jax.Shape...  2.6 us
  transfers between devices with their start and end apart: 24, of which 13 were waited for; matrix products, arithmetic and copies ran while one was open for 2% of the time, Pallas kernels for 27%

profile of v3, /device:TPU:1, one launch (start us, length us, event | category | flops | bytes accessed | tf_op | source)
XLA Modules:
  0.0 115.3 jit_solution(2645060998399515375)
XLA Ops:
  0.0 1.4 %collective-permute-start.2 = (bf16[4,128,1024]{2,1,0:T(8,128)(2,1)}, bf16[4,128,1024]{2,1,0:T(8,128)(2,1)S(1)}, u32[]{:S(2)}, u32[]{:S(2)}) collective-permute-start(bf16[4,128,1024]{2,1,0:T(8,128)(2,1)} %g.1), channel_id=1, source_target_pairs={{0,1},{1,0},{2,3},{3,2},{4,5},{5,4},{6,7},{7,6},{8,9},{9,8},{10,11... | collective-permute-start | bytes 3145736 | tf_op jit(solution)/shard_map/ppermute | solution.py:244
  1.4 1.2 %copy-done.1 = bf16[4,128,1024]{2,1,0:T(8,128)(2,1)S(1)} copy-done((bf16[4,128,1024]{2,1,0:T(8,128)(2,1)S(1)}, bf16[4,128,1024]{2,1,0:T(8,128)(2,1)}, u32[]{:S(2)}) %copy-start.1) | copy-done | bytes 1048600
  2.6 0.6 prep.1
  3.3 5.6 %collective-permute-start = (bf16[4,512,128]{2,1,0:T(8,128)(2,1)S(1)}, bf16[4,512,128]{2,1,0:T(8,128)(2,1)S(1)}, u32[]{:S(2)}, u32[]{:S(2)}) collective-permute-start(bf16[4,512,128]{2,1,0:T(8,128)(2,1)S(1)} %get-tuple-element.25), channel_id=1, source_target_pairs={{0,0},{1,17},{8,9},{9,24},{16,1},{17,16},{24,8},{25,25},{2,2},{3,1... | collective-permute-start | bytes 1572872 | tf_op jit(solution)/shard_map/ppermute | solution.py:259
  9.0 10.7 %collective-permute-done.refs_0_.refs_10_ = bf16[4,512,128]{2,1,0:T(8,128)(2,1)S(1)} collective-permute-done((bf16[4,512,128]{2,1,0:T(8,128)(2,1)S(1)}, bf16[4,512,128]{2,1,0:T(8,128)(2,1)S(1)}, u32[]{:S(2)}, u32[]{:S(2)}) %collective-permute-start) | collective-permute-done | bytes 524320 | tf_op jit(solution)/shard_map/ppermute | solution.py:259
  19.7 2.0 %collective-permute-done.1.refs_1_ = bf16[4,512,128]{2,1,0:T(8,128)(2,1)S(1)} collective-permute-done((bf16[4,512,128]{2,1,0:T(8,128)(2,1)S(1)}, bf16[4,512,128]{2,1,0:T(8,128)(2,1)S(1)}, u32[]{:S(2)}, u32[]{:S(2)}) %collective-permute-start.1) | collective-permute-done | bytes 524320 | tf_op jit(solution)/shard_map/ppermute | solution.py:259
  21.7 0.2 collective-permute-start.4
  21.9 1.3 %slice_bitcast_fusion.5 = (bf16[1,2,128,1024]{3,2,1,0:T(8,128)(2,1)S(1)}, bf16[1,2,128,1024]{3,2,1,0:T(8,128)(2,1)S(1)}) fusion(bf16[4,128,1024]{2,1,0:T(8,128)(2,1)} %g.1), kind=kLoop, calls=%fused_computation.10 | loop fusion | bytes 2097152 | tf_op jit(solution)/shard_map/stack | solution.py:262
  23.4 2.0 %collective-permute-start.8 = (bf16[2,2,128,1024]{3,2,1,0:T(8,128)(2,1)S(1)}, bf16[2,2,128,1024]{3,2,1,0:T(8,128)(2,1)S(1)}, u32[]{:S(2)}, u32[]{:S(2)}) collective-permute-start(bf16[2,2,128,1024]{3,2,1,0:T(8,128)(2,1)S(1)} %pad_maximum_fusion.3), channel_id=1, source_target_pairs={{0,8},{8,16},{16,24},{24,0},{1,25},{9,1},{17,9},{25,17},{2,10},{10... | collective-permute-start | bytes 3145736 | tf_op jit(solution)/shard_map/ppermute | solution.py:249
  25.4 2.8 %collective-permute-start.7 = (bf16[8,512,128]{2,1,0:T(8,128)(2,1)S(1)}, bf16[8,512,128]{2,1,0:T(8,128)(2,1)S(1)}, u32[]{:S(2)}, u32[]{:S(2)}) collective-permute-start(bf16[8,512,128]{2,1,0:T(8,128)(2,1)S(1)} %pad_maximum_fusion.2), channel_id=1, source_target_pairs={{0,2},{2,4},{4,6},{6,0},{1,7},{3,1},{5,3},{7,5},{8,10},{10,12},{12... | collective-permute-start | bytes 3145736 | tf_op jit(solution)/shard_map/ppermute | solution.py:249
  28.3 0.8 collective-permute-start.6
  29.1 1.0 collective-permute-done.3.refs_2_
  30.3 0.5 collective-permute-start.5
  30.8 6.6 %collective-permute-done.8.za = bf16[2,2,128,1024]{3,2,1,0:T(8,128)(2,1)S(1)} collective-permute-done((bf16[2,2,128,1024]{3,2,1,0:T(8,128)(2,1)S(1)}, bf16[2,2,128,1024]{3,2,1,0:T(8,128)(2,1)S(1)}, u32[]{:S(2)}, u32[]{:S(2)}) %collective-permute-start.8) | collective-permute-done | bytes 1048608 | tf_op jit(solution)/shard_map/ppermute | solution.py:249
  37.4 2.6 %collective-permute-done.7.refs_5_ = bf16[8,512,128]{2,1,0:T(8,128)(2,1)S(1)} collective-permute-done((bf16[8,512,128]{2,1,0:T(8,128)(2,1)S(1)}, bf16[8,512,128]{2,1,0:T(8,128)(2,1)S(1)}, u32[]{:S(2)}, u32[]{:S(2)}) %collective-permute-start.7) | collective-permute-done | bytes 1048608 | tf_op jit(solution)/shard_map/ppermute | solution.py:249
  40.0 1.6 %collective-permute-start.9 = (bf16[8,512,128]{2,1,0:T(8,128)(2,1)S(1)}, bf16[8,512,128]{2,1,0:T(8,128)(2,1)S(1)}, u32[]{:S(2)}, u32[]{:S(2)}) collective-permute-start(bf16[8,512,128]{2,1,0:T(8,128)(2,1)S(1)} %collective-permute-done.7.refs_5_), channel_id=1, source_target_pairs={{0,1},{1,0},{2,3},{3,2},{4,5},{5,4},{6,7},{7,6},{8,9},{9,8},{10,11... | collective-permute-start | bytes 3145736 | tf_op jit(solution)/shard_map/ppermute | solution.py:244
  41.8 2.4 %collective-permute-start.12 = (bf16[4,512,128]{2,1,0:T(8,128)(2,1)S(1)}, bf16[4,512,128]{2,1,0:T(8,128)(2,1)S(1)}, u32[]{:S(2)}, u32[]{:S(2)}) collective-permute-start(bf16[4,512,128]{2,1,0:T(8,128)(2,1)S(1)} %slice.36), channel_id=1, source_target_pairs={{0,2},{2,4},{4,6},{6,0},{1,7},{3,1},{5,3},{7,5},{8,10},{10,12},{12... | collective-permute-start | bytes 1572872 | tf_op jit(solution)/shard_map/ppermute | solution.py:249
  44.2 4.4 %collective-permute-done.6.zb = bf16[2,2,128,1024]{3,2,1,0:T(8,128)(2,1)S(1)} collective-permute-done((bf16[2,2,128,1024]{3,2,1,0:T(8,128)(2,1)S(1)}, bf16[2,2,128,1024]{3,2,1,0:T(8,128)(2,1)S(1)}, u32[]{:S(2)}, u32[]{:S(2)}) %collective-permute-start.6) | collective-permute-done | bytes 1048608 | tf_op jit(solution)/shard_map/ppermute | solution.py:249
  48.6 2.6 %collective-permute-done.5.refs_4_ = bf16[8,512,128]{2,1,0:T(8,128)(2,1)S(1)} collective-permute-done((bf16[8,512,128]{2,1,0:T(8,128)(2,1)S(1)}, bf16[8,512,128]{2,1,0:T(8,128)(2,1)S(1)}, u32[]{:S(2)}, u32[]{:S(2)}) %collective-permute-start.5) | collective-permute-done | bytes 1048608 | tf_op jit(solution)/shard_map/ppermute | solution.py:249
  51.2 1.6 %collective-permute-start.15 = (bf16[8,512,128]{2,1,0:T(8,128)(2,1)S(1)}, bf16[8,512,128]{2,1,0:T(8,128)(2,1)S(1)}, u32[]{:S(2)}, u32[]{:S(2)}) collective-permute-start(bf16[8,512,128]{2,1,0:T(8,128)(2,1)S(1)} %collective-permute-done.5.refs_4_), channel_id=1, source_target_pairs={{0,1},{1,0},{2,3},{3,2},{4,5},{5,4},{6,7},{7,6},{8,9},{9,8},{10,11... | collective-permute-start | bytes 3145736 | tf_op jit(solution)/shard_map/ppermute | solution.py:244
  52.9 1.3 %collective-permute-start.13 = (bf16[2,128,1024]{2,1,0:T(8,128)(2,1)S(1)}, bf16[2,128,1024]{2,1,0:T(8,128)(2,1)S(1)}, u32[]{:S(2)}, u32[]{:S(2)}) collective-permute-start(bf16[2,128,1024]{2,1,0:T(8,128)(2,1)S(1)} %get-tuple-element.47), channel_id=1, source_target_pairs={{0,8},{8,16},{16,24},{24,0},{1,25},{9,1},{17,9},{25,17},{2,10},{10... | collective-permute-start | bytes 1572872 | tf_op jit(solution)/shard_map/ppermute | solution.py:249
  54.2 1.6 %collective-permute-start.11 = (bf16[4,512,128]{2,1,0:T(8,128)(2,1)S(1)}, bf16[4,512,128]{2,1,0:T(8,128)(2,1)S(1)}, u32[]{:S(2)}, u32[]{:S(2)}) collective-permute-start(bf16[4,512,128]{2,1,0:T(8,128)(2,1)S(1)} %slice.35), channel_id=1, source_target_pairs={{0,2},{2,4},{4,6},{6,0},{1,7},{3,1},{5,3},{7,5},{8,10},{10,12},{12... | collective-permute-start | bytes 1572872 | tf_op jit(solution)/shard_map/ppermute | solution.py:249
  55.9 1.0 collective-permute-done.12.refs_9_
  56.8 1.6 %collective-permute-start.16 = (bf16[2,128,1024]{2,1,0:T(8,128)(2,1)S(1)}, bf16[2,128,1024]{2,1,0:T(8,128)(2,1)S(1)}, u32[]{:S(2)}, u32[]{:S(2)}) collective-permute-start(bf16[2,128,1024]{2,1,0:T(8,128)(2,1)S(1)} %get-tuple-element.36), channel_id=1, source_target_pairs={{0,1},{1,0},{2,3},{3,2},{4,5},{5,4},{6,7},{7,6},{8,9},{9,8},{10,11... | collective-permute-start | bytes 1572872 | tf_op jit(solution)/shard_map/ppermute | solution.py:244
  58.5 1.3 %collective-permute-start.14 = (bf16[2,128,1024]{2,1,0:T(8,128)(2,1)S(1)}, bf16[2,128,1024]{2,1,0:T(8,128)(2,1)S(1)}, u32[]{:S(2)}, u32[]{:S(2)}) collective-permute-start(bf16[2,128,1024]{2,1,0:T(8,128)(2,1)S(1)} %get-tuple-element.45), channel_id=1, source_target_pairs={{0,8},{8,16},{16,24},{24,0},{1,25},{9,1},{17,9},{25,17},{2,10},{10... | collective-permute-start | bytes 1572872 | tf_op jit(solution)/shard_map/ppermute | solution.py:249
  59.7 1.4 %collective-permute-done.13.fa = bf16[2,128,1024]{2,1,0:T(8,128)(2,1)S(1)} collective-permute-done((bf16[2,128,1024]{2,1,0:T(8,128)(2,1)S(1)}, bf16[2,128,1024]{2,1,0:T(8,128)(2,1)S(1)}, u32[]{:S(2)}, u32[]{:S(2)}) %collective-permute-start.13) | collective-permute-done | bytes 524320 | tf_op jit(solution)/shard_map/ppermute | solution.py:249
  61.2 1.4 %collective-permute-done.11.refs_8_ = bf16[4,512,128]{2,1,0:T(8,128)(2,1)S(1)} collective-permute-done((bf16[4,512,128]{2,1,0:T(8,128)(2,1)S(1)}, bf16[4,512,128]{2,1,0:T(8,128)(2,1)S(1)}, u32[]{:S(2)}, u32[]{:S(2)}) %collective-permute-start.11) | collective-permute-done | bytes 524320 | tf_op jit(solution)/shard_map/ppermute | solution.py:249
  62.6 4.2 %collective-permute-done.14.fb = bf16[2,128,1024]{2,1,0:T(8,128)(2,1)S(1)} collective-permute-done((bf16[2,128,1024]{2,1,0:T(8,128)(2,1)S(1)}, bf16[2,128,1024]{2,1,0:T(8,128)(2,1)S(1)}, u32[]{:S(2)}, u32[]{:S(2)}) %collective-permute-start.14) | collective-permute-done | bytes 524320 | tf_op jit(solution)/shard_map/ppermute | solution.py:249
  66.9 2.2 %collective-permute-start.17 = (bf16[8,512,128]{2,1,0:T(8,128)(2,1)S(1)}, bf16[8,512,128]{2,1,0:T(8,128)(2,1)S(1)}, u32[]{:S(2)}, u32[]{:S(2)}) collective-permute-start(bf16[8,512,128]{2,1,0:T(8,128)(2,1)S(1)} %pad_maximum_fusion.4), channel_id=1, source_target_pairs={{0,1},{1,0},{2,3},{3,2},{4,5},{5,4},{6,7},{7,6},{8,9},{9,8},{10,11... | collective-permute-start | bytes 3145736 | tf_op jit(solution)/shard_map/ppermute | solution.py:244
  69.1 0.4 gather.1.refs_11_
  69.5 2.8 %blocks_2r0.2.refs_12_ = f32[512,1024]{1,0:T(8,128)S(1)} custom-call(bf16[4,512,128]{2,1,0:T(8,128)(2,1)S(1)} %collective-permute-done.refs_0_.refs_10_, bf16[4,512,128]{2,1,0:T(8,128)(2,1)S(1)} %collective-permute-done.1.refs_1_, bf16[4,512,128]{2,1,0:T(8,128)(2,1)S(1)} %collective-permute-done.3.refs_2_, ...), custom_call_target="tpu_custom_call" | custom-call | flops 2147483648 | bytes 5242880 | tf_op jit(solution)/shard_map/blocks_2r0/pallas_call | solution.py:199
  72.3 2.2 %blocks_2r0.3 = bf16[272,1024]{1,0:T(8,128)(2,1)S(1)} custom-call(bf16[4,512,128]{2,1,0:T(8,128)(2,1)S(1)} %collective-permute-done.refs_0_.refs_10_, bf16[4,512,128]{2,1,0:T(8,128)(2,1)S(1)} %collective-permute-done.1.refs_1_, bf16[4,512,128]{2,1,0:T(8,128)(2,1)S(1)} %collective-permute-done.3.refs_2_, ...), custom_call_target="tpu_custom_call" | custom-call | flops 2147483648 | bytes 5242880 | tf_op jit(solution)/shard_map/blocks_2r0/pallas_call | solution.py:199
  74.5 1.3 %collective-permute-start.22 = (bf16[272,1024]{1,0:T(8,128)(2,1)S(1)}, bf16[272,1024]{1,0:T(8,128)(2,1)S(1)}, u32[]{:S(2)}, u32[]{:S(2)}) collective-permute-start(bf16[272,1024]{1,0:T(8,128)(2,1)S(1)} %blocks_2r0.3), channel_id=1, source_target_pairs={{0,32},{32,64},{64,96},{96,0},{1,33},{33,65},{65,97},{97,1},{2,34}... | collective-permute-start | bytes 1671176 | tf_op jit(solution)/shard_map/ppermute | solution.py:244
  75.8 2.1 %blocks_2r272.1 = bf16[240,1024]{1,0:T(8,128)(2,1)S(1)} custom-call(bf16[4,512,128]{2,1,0:T(8,128)(2,1)S(1)} %collective-permute-done.refs_0_.refs_10_, bf16[4,512,128]{2,1,0:T(8,128)(2,1)S(1)} %collective-permute-done.1.refs_1_, bf16[4,512,128]{2,1,0:T(8,128)(2,1)S(1)} %collective-permute-done.3.refs_2_, ...), custom_call_target="tpu_custom_call" | custom-call | flops 2147483648 | bytes 5242880 | tf_op jit(solution)/shard_map/blocks_2r272/pallas_call | solution.py:199
  77.9 1.5 %collective-permute-start.19 = (bf16[240,1024]{1,0:T(8,128)(2,1)S(1)}, bf16[240,1024]{1,0:T(8,128)(2,1)S(1)}, u32[]{:S(2)}, u32[]{:S(2)}) collective-permute-start(bf16[240,1024]{1,0:T(8,128)(2,1)S(1)} %blocks_2r272.1), channel_id=1, source_target_pairs={{0,96},{32,0},{64,32},{96,64},{1,97},{33,1},{65,33},{97,65},{2,98}... | collective-permute-start | bytes 1474568 | tf_op jit(solution)/shard_map/ppermute | solution.py:244
  79.5 3.6 %blocks_1r272.1 = bf16[240,1024]{1,0:T(8,128)(2,1)S(1)} custom-call(bf16[4,512,128]{2,1,0:T(8,128)(2,1)S(1)} %collective-permute-done.refs_0_.refs_10_, bf16[4,512,128]{2,1,0:T(8,128)(2,1)S(1)} %collective-permute-done.1.refs_1_, bf16[4,512,128]{2,1,0:T(8,128)(2,1)S(1)} %collective-permute-done.3.refs_2_, ...), custom_call_target="tpu_custom_call" | custom-call | flops 2147483648 | bytes 5242880 | tf_op jit(solution)/shard_map/blocks_1r272/pallas_call | solution.py:199
  83.1 0.3 collective-permute-start.18
  83.4 3.7 %blocks_3r0.1 = bf16[272,1024]{1,0:T(8,128)(2,1)S(1)} custom-call(bf16[4,512,128]{2,1,0:T(8,128)(2,1)S(1)} %collective-permute-done.refs_0_.refs_10_, bf16[4,512,128]{2,1,0:T(8,128)(2,1)S(1)} %collective-permute-done.1.refs_1_, bf16[4,512,128]{2,1,0:T(8,128)(2,1)S(1)} %collective-permute-done.3.refs_2_, ...), custom_call_target="tpu_custom_call" | custom-call | flops 2147483648 | bytes 5242880 | tf_op jit(solution)/shard_map/blocks_3r0/pallas_call | solution.py:199
  87.1 2.5 %collective-permute-start.21 = (bf16[272,1024]{1,0:T(8,128)(2,1)S(1)}, bf16[272,1024]{1,0:T(8,128)(2,1)S(1)}, u32[]{:S(2)}, u32[]{:S(2)}) collective-permute-start(bf16[272,1024]{1,0:T(8,128)(2,1)S(1)} %blocks_3r0.1), channel_id=1, source_target_pairs={{0,96},{32,0},{64,32},{96,64},{1,97},{33,1},{65,33},{97,65},{2,98}... | collective-permute-start | bytes 1671176 | tf_op jit(solution)/shard_map/ppermute | solution.py:244
  89.6 0.4 collective-permute-done.22.refs_12_
  90.0 4.4 %blocks_1r0.1 = bf16[272,1024]{1,0:T(8,128)(2,1)S(1)} custom-call(bf16[4,512,128]{2,1,0:T(8,128)(2,1)S(1)} %collective-permute-done.refs_0_.refs_10_, bf16[4,512,128]{2,1,0:T(8,128)(2,1)S(1)} %collective-permute-done.1.refs_1_, bf16[4,512,128]{2,1,0:T(8,128)(2,1)S(1)} %collective-permute-done.3.refs_2_, ...), custom_call_target="tpu_custom_call" | custom-call | flops 2147483648 | bytes 5242880 | tf_op jit(solution)/shard_map/blocks_1r0/pallas_call | solution.py:199
  94.6 4.3 %blocks_3r272.1 = bf16[240,1024]{1,0:T(8,128)(2,1)S(1)} custom-call(bf16[4,512,128]{2,1,0:T(8,128)(2,1)S(1)} %collective-permute-done.refs_0_.refs_10_, bf16[4,512,128]{2,1,0:T(8,128)(2,1)S(1)} %collective-permute-done.1.refs_1_, bf16[4,512,128]{2,1,0:T(8,128)(2,1)S(1)} %collective-permute-done.3.refs_2_, ...), custom_call_target="tpu_custom_call" | custom-call | flops 2147483648 | bytes 5242880 | tf_op jit(solution)/shard_map/blocks_3r272/pallas_call | solution.py:199
  98.8 2.7 %collective-permute-start.20 = (bf16[240,1024]{1,0:T(8,128)(2,1)S(1)}, bf16[240,1024]{1,0:T(8,128)(2,1)S(1)}, u32[]{:S(2)}, u32[]{:S(2)}) collective-permute-start(bf16[240,1024]{1,0:T(8,128)(2,1)S(1)} %blocks_3r272.1), channel_id=1, source_target_pairs={{0,96},{32,0},{64,32},{96,64},{1,97},{33,1},{65,33},{97,65},{2,98}... | collective-permute-start | bytes 1474568 | tf_op jit(solution)/shard_map/ppermute | solution.py:244
  101.5 3.8 %blocks_0r272.1.own = f32[240,1024]{1,0:T(8,128)S(1)} custom-call(bf16[4,512,128]{2,1,0:T(8,128)(2,1)S(1)} %collective-permute-done.refs_0_.refs_10_, bf16[4,512,128]{2,1,0:T(8,128)(2,1)S(1)} %collective-permute-done.1.refs_1_, bf16[4,512,128]{2,1,0:T(8,128)(2,1)S(1)} %collective-permute-done.3.refs_2_, ...), custom_call_target="tpu_custom_call" | custom-call | flops 2147483648 | bytes 5242880 | tf_op jit(solution)/shard_map/blocks_0r272/pallas_call | solution.py:199
  105.3 3.9 %blocks_0r0.1.own = f32[272,1024]{1,0:T(8,128)S(1)} custom-call(bf16[4,512,128]{2,1,0:T(8,128)(2,1)S(1)} %collective-permute-done.refs_0_.refs_10_, bf16[4,512,128]{2,1,0:T(8,128)(2,1)S(1)} %collective-permute-done.1.refs_1_, bf16[4,512,128]{2,1,0:T(8,128)(2,1)S(1)} %collective-permute-done.3.refs_2_, ...), custom_call_target="tpu_custom_call" | custom-call | flops 2147483648 | bytes 5242880 | tf_op jit(solution)/shard_map/blocks_0r0/pallas_call | solution.py:199
  109.2 3.3 %collective-permute-done.23.p = bf16[272,1024]{1,0:T(8,128)(2,1)S(1)} collective-permute-done((bf16[272,1024]{1,0:T(8,128)(2,1)S(1)}, bf16[272,1024]{1,0:T(8,128)(2,1)S(1)}, u32[]{:S(2)}, u32[]{:S(2)}) %collective-permute-start.23) | collective-permute-done | bytes 557088 | tf_op jit(solution)/shard_map/ppermute | solution.py:244
  112.5 1.3 %final0.1.rest_0_ = f32[512,1024]{1,0:T(8,128)} custom-call(f32[272,1024]{1,0:T(8,128)S(1)} %blocks_0r0.1.own, bf16[272,1024]{1,0:T(8,128)(2,1)S(1)} %collective-permute-done.23.p), custom_call_target="tpu_custom_call" | custom-call | tf_op jit(solution)/shard_map/final0/pallas_call | solution.py:231
  113.9 1.3 %final1.1 = f32[512,1024]{1,0:T(8,128)} custom-call(f32[240,1024]{1,0:T(8,128)S(1)} %blocks_0r272.1.own, bf16[240,1024]{1,0:T(8,128)(2,1)S(1)} %collective-permute-done.20.p, f32[512,1024]{1,0:T(8,128)} %final0.1.rest_0_), custom_call_target="tpu_custom_call", output_to_operand_aliasing={{}: (2, {})} | custom-call | tf_op jit(solution)/shard_map/final1/pallas_call | solution.py:231
  (28 shorter events, 1.1 us)
Async XLA Ops:
  0.0 21.7 %collective-permute-start.2 = (bf16[4,128,1024]{2,1,0:T(8,128)(2,1)}, bf16[4,128,1024]{2,1,0:T(8,128)(2,1)S(1)}, u32[]{:S(2)}, u32[]{:S(2)}) collective-permute-start(bf16[4,128,1024]{2,1,0:T(8,128)(2,1)} %g.1), channel_id=1, source_target_pairs={{0,1},{1,0},{2,3},{3,2},{4,5},{5,4},{6,7},{7,6},{8,9},{9,8},{10,11... | collective-permute-start | bytes 3145736 | tf_op jit(solution)/shard_map/ppermute | solution.py:244
  1.4 1.2 %copy-start.1 = (bf16[4,128,1024]{2,1,0:T(8,128)(2,1)S(1)}, bf16[4,128,1024]{2,1,0:T(8,128)(2,1)}, u32[]{:S(2)}) copy-start(bf16[4,128,1024]{2,1,0:T(8,128)(2,1)} %a_ref.1) | copy-start | bytes 3145732
  3.3 16.4 %collective-permute-start = (bf16[4,512,128]{2,1,0:T(8,128)(2,1)S(1)}, bf16[4,512,128]{2,1,0:T(8,128)(2,1)S(1)}, u32[]{:S(2)}, u32[]{:S(2)}) collective-permute-start(bf16[4,512,128]{2,1,0:T(8,128)(2,1)S(1)} %get-tuple-element.25), channel_id=1, source_target_pairs={{0,0},{1,17},{8,9},{9,24},{16,1},{17,16},{24,8},{25,25},{2,2},{3,1... | collective-permute-start | bytes 1572872 | tf_op jit(solution)/shard_map/ppermute | solution.py:259
  8.9 12.8 %collective-permute-start.1 = (bf16[4,512,128]{2,1,0:T(8,128)(2,1)S(1)}, bf16[4,512,128]{2,1,0:T(8,128)(2,1)S(1)}, u32[]{:S(2)}, u32[]{:S(2)}) collective-permute-start(bf16[4,512,128]{2,1,0:T(8,128)(2,1)S(1)} %get-tuple-element.26), channel_id=1, source_target_pairs={{0,8},{1,25},{8,1},{9,16},{16,9},{17,24},{24,0},{25,17},{2,10},{3,... | collective-permute-start | bytes 1572872 | tf_op jit(solution)/shard_map/ppermute | solution.py:259
  21.7 3.6 %collective-permute-start.4 = (bf16[4,512,128]{2,1,0:T(8,128)(2,1)S(1)}, bf16[4,512,128]{2,1,0:T(8,128)(2,1)S(1)}, u32[]{:S(2)}, u32[]{:S(2)}) collective-permute-start(bf16[4,512,128]{2,1,0:T(8,128)(2,1)S(1)} %collective-permute-done.1.refs_1_), channel_id=1, source_target_pairs={{0,1},{1,0},{2,3},{3,2},{4,5},{5,4},{6,7},{7,6},{8,9},{9,8},{10,11... | collective-permute-start | bytes 1572872 | tf_op jit(solution)/shard_map/ppermute | solution.py:244
  23.4 14.0 %collective-permute-start.8 = (bf16[2,2,128,1024]{3,2,1,0:T(8,128)(2,1)S(1)}, bf16[2,2,128,1024]{3,2,1,0:T(8,128)(2,1)S(1)}, u32[]{:S(2)}, u32[]{:S(2)}) collective-permute-start(bf16[2,2,128,1024]{3,2,1,0:T(8,128)(2,1)S(1)} %pad_maximum_fusion.3), channel_id=1, source_target_pairs={{0,8},{8,16},{16,24},{24,0},{1,25},{9,1},{17,9},{25,17},{2,10},{10... | collective-permute-start | bytes 3145736 | tf_op jit(solution)/shard_map/ppermute | solution.py:249
  25.4 14.5 %collective-permute-start.7 = (bf16[8,512,128]{2,1,0:T(8,128)(2,1)S(1)}, bf16[8,512,128]{2,1,0:T(8,128)(2,1)S(1)}, u32[]{:S(2)}, u32[]{:S(2)}) collective-permute-start(bf16[8,512,128]{2,1,0:T(8,128)(2,1)S(1)} %pad_maximum_fusion.2), channel_id=1, source_target_pairs={{0,2},{2,4},{4,6},{6,0},{1,7},{3,1},{5,3},{7,5},{8,10},{10,12},{12... | collective-permute-start | bytes 3145736 | tf_op jit(solution)/shard_map/ppermute | solution.py:249
  28.2 1.9 %collective-permute-start.3 = (bf16[4,512,128]{2,1,0:T(8,128)(2,1)S(1)}, bf16[4,512,128]{2,1,0:T(8,128)(2,1)S(1)}, u32[]{:S(2)}, u32[]{:S(2)}) collective-permute-start(bf16[4,512,128]{2,1,0:T(8,128)(2,1)S(1)} %collective-permute-done.refs_0_.refs_10_), channel_id=1, source_target_pairs={{0,1},{1,0},{2,3},{3,2},{4,5},{5,4},{6,7},{7,6},{8,9},{9,8},{10,11... | collective-permute-start | bytes 1572872 | tf_op jit(solution)/shard_map/ppermute | solution.py:244
  28.3 20.3 %collective-permute-start.6 = (bf16[2,2,128,1024]{3,2,1,0:T(8,128)(2,1)S(1)}, bf16[2,2,128,1024]{3,2,1,0:T(8,128)(2,1)S(1)}, u32[]{:S(2)}, u32[]{:S(2)}) collective-permute-start(bf16[2,2,128,1024]{3,2,1,0:T(8,128)(2,1)S(1)} %pad_maximum_fusion.1), channel_id=1, source_target_pairs={{0,8},{8,16},{16,24},{24,0},{1,25},{9,1},{17,9},{25,17},{2,10},{10... | collective-permute-start | bytes 3145736 | tf_op jit(solution)/shard_map/ppermute | solution.py:249
  30.3 21.0 %collective-permute-start.5 = (bf16[8,512,128]{2,1,0:T(8,128)(2,1)S(1)}, bf16[8,512,128]{2,1,0:T(8,128)(2,1)S(1)}, u32[]{:S(2)}, u32[]{:S(2)}) collective-permute-start(bf16[8,512,128]{2,1,0:T(8,128)(2,1)S(1)} %pad_maximum_fusion), channel_id=1, source_target_pairs={{0,2},{2,4},{4,6},{6,0},{1,7},{3,1},{5,3},{7,5},{8,10},{10,12},{12... | collective-permute-start | bytes 3145736 | tf_op jit(solution)/shard_map/ppermute | solution.py:249
  40.0 11.2 %collective-permute-start.9 = (bf16[8,512,128]{2,1,0:T(8,128)(2,1)S(1)}, bf16[8,512,128]{2,1,0:T(8,128)(2,1)S(1)}, u32[]{:S(2)}, u32[]{:S(2)}) collective-permute-start(bf16[8,512,128]{2,1,0:T(8,128)(2,1)S(1)} %collective-permute-done.7.refs_5_), channel_id=1, source_target_pairs={{0,1},{1,0},{2,3},{3,2},{4,5},{5,4},{6,7},{7,6},{8,9},{9,8},{10,11... | collective-permute-start | bytes 3145736 | tf_op jit(solution)/shard_map/ppermute | solution.py:244
  41.7 9.5 %collective-permute-start.10 = (bf16[2,128,1024]{2,1,0:T(8,128)(2,1)S(1)}, bf16[2,128,1024]{2,1,0:T(8,128)(2,1)S(1)}, u32[]{:S(2)}, u32[]{:S(2)}) collective-permute-start(bf16[2,128,1024]{2,1,0:T(8,128)(2,1)S(1)} %get-tuple-element.48), channel_id=1, source_target_pairs={{0,1},{1,0},{2,3},{3,2},{4,5},{5,4},{6,7},{7,6},{8,9},{9,8},{10,11... | collective-permute-start | bytes 1572872 | tf_op jit(solution)/shard_map/ppermute | solution.py:244
  41.8 15.0 %collective-permute-start.12 = (bf16[4,512,128]{2,1,0:T(8,128)(2,1)S(1)}, bf16[4,512,128]{2,1,0:T(8,128)(2,1)S(1)}, u32[]{:S(2)}, u32[]{:S(2)}) collective-permute-start(bf16[4,512,128]{2,1,0:T(8,128)(2,1)S(1)} %slice.36), channel_id=1, source_target_pairs={{0,2},{2,4},{4,6},{6,0},{1,7},{3,1},{5,3},{7,5},{8,10},{10,12},{12... | collective-permute-start | bytes 1572872 | tf_op jit(solution)/shard_map/ppermute | solution.py:249
  51.2 15.6 %collective-permute-start.15 = (bf16[8,512,128]{2,1,0:T(8,128)(2,1)S(1)}, bf16[8,512,128]{2,1,0:T(8,128)(2,1)S(1)}, u32[]{:S(2)}, u32[]{:S(2)}) collective-permute-start(bf16[8,512,128]{2,1,0:T(8,128)(2,1)S(1)} %collective-permute-done.5.refs_4_), channel_id=1, source_target_pairs={{0,1},{1,0},{2,3},{3,2},{4,5},{5,4},{6,7},{7,6},{8,9},{9,8},{10,11... | collective-permute-start | bytes 3145736 | tf_op jit(solution)/shard_map/ppermute | solution.py:244
  52.9 8.3 %collective-permute-start.13 = (bf16[2,128,1024]{2,1,0:T(8,128)(2,1)S(1)}, bf16[2,128,1024]{2,1,0:T(8,128)(2,1)S(1)}, u32[]{:S(2)}, u32[]{:S(2)}) collective-permute-start(bf16[2,128,1024]{2,1,0:T(8,128)(2,1)S(1)} %get-tuple-element.47), channel_id=1, source_target_pairs={{0,8},{8,16},{16,24},{24,0},{1,25},{9,1},{17,9},{25,17},{2,10},{10... | collective-permute-start | bytes 1572872 | tf_op jit(solution)/shard_map/ppermute | solution.py:249
  54.2 15.0 %copy-start = (bf16[4,128,1024]{2,1,0:T(8,128)(2,1)S(1)}, bf16[4,128,1024]{2,1,0:T(8,128)(2,1)}, u32[]{:S(2)}) copy-start(bf16[4,128,1024]{2,1,0:T(8,128)(2,1)} %g.1) | copy-start | bytes 3145732
  54.2 8.4 %collective-permute-start.11 = (bf16[4,512,128]{2,1,0:T(8,128)(2,1)S(1)}, bf16[4,512,128]{2,1,0:T(8,128)(2,1)S(1)}, u32[]{:S(2)}, u32[]{:S(2)}) collective-permute-start(bf16[4,512,128]{2,1,0:T(8,128)(2,1)S(1)} %slice.35), channel_id=1, source_target_pairs={{0,2},{2,4},{4,6},{6,0},{1,7},{3,1},{5,3},{7,5},{8,10},{10,12},{12... | collective-permute-start | bytes 1572872 | tf_op jit(solution)/shard_map/ppermute | solution.py:249
  56.8 5.7 %collective-permute-start.16 = (bf16[2,128,1024]{2,1,0:T(8,128)(2,1)S(1)}, bf16[2,128,1024]{2,1,0:T(8,128)(2,1)S(1)}, u32[]{:S(2)}, u32[]{:S(2)}) collective-permute-start(bf16[2,128,1024]{2,1,0:T(8,128)(2,1)S(1)} %get-tuple-element.36), channel_id=1, source_target_pairs={{0,1},{1,0},{2,3},{3,2},{4,5},{5,4},{6,7},{7,6},{8,9},{9,8},{10,11... | collective-permute-start | bytes 1572872 | tf_op jit(solution)/shard_map/ppermute | solution.py:244
  58.5 8.3 %collective-permute-start.14 = (bf16[2,128,1024]{2,1,0:T(8,128)(2,1)S(1)}, bf16[2,128,1024]{2,1,0:T(8,128)(2,1)S(1)}, u32[]{:S(2)}, u32[]{:S(2)}) collective-permute-start(bf16[2,128,1024]{2,1,0:T(8,128)(2,1)S(1)} %get-tuple-element.45), channel_id=1, source_target_pairs={{0,8},{8,16},{16,24},{24,0},{1,25},{9,1},{17,9},{25,17},{2,10},{10... | collective-permute-start | bytes 1572872 | tf_op jit(solution)/shard_map/ppermute | solution.py:249
  66.9 5.4 %collective-permute-start.17 = (bf16[8,512,128]{2,1,0:T(8,128)(2,1)S(1)}, bf16[8,512,128]{2,1,0:T(8,128)(2,1)S(1)}, u32[]{:S(2)}, u32[]{:S(2)}) collective-permute-start(bf16[8,512,128]{2,1,0:T(8,128)(2,1)S(1)} %pad_maximum_fusion.4), channel_id=1, source_target_pairs={{0,1},{1,0},{2,3},{3,2},{4,5},{5,4},{6,7},{7,6},{8,9},{9,8},{10,11... | collective-permute-start | bytes 3145736 | tf_op jit(solution)/shard_map/ppermute | solution.py:244
  74.5 15.5 %collective-permute-start.22 = (bf16[272,1024]{1,0:T(8,128)(2,1)S(1)}, bf16[272,1024]{1,0:T(8,128)(2,1)S(1)}, u32[]{:S(2)}, u32[]{:S(2)}) collective-permute-start(bf16[272,1024]{1,0:T(8,128)(2,1)S(1)} %blocks_2r0.3), channel_id=1, source_target_pairs={{0,32},{32,64},{64,96},{96,0},{1,33},{33,65},{65,97},{97,1},{2,34}... | collective-permute-start | bytes 1671176 | tf_op jit(solution)/shard_map/ppermute | solution.py:244
  77.9 16.6 %collective-permute-start.19 = (bf16[240,1024]{1,0:T(8,128)(2,1)S(1)}, bf16[240,1024]{1,0:T(8,128)(2,1)S(1)}, u32[]{:S(2)}, u32[]{:S(2)}) collective-permute-start(bf16[240,1024]{1,0:T(8,128)(2,1)S(1)} %blocks_2r272.1), channel_id=1, source_target_pairs={{0,96},{32,0},{64,32},{96,64},{1,97},{33,1},{65,33},{97,65},{2,98}... | collective-permute-start | bytes 1474568 | tf_op jit(solution)/shard_map/ppermute | solution.py:244
  83.1 18.5 %collective-permute-start.18 = (bf16[240,1024]{1,0:T(8,128)(2,1)S(1)}, bf16[240,1024]{1,0:T(8,128)(2,1)S(1)}, u32[]{:S(2)}, u32[]{:S(2)}) collective-permute-start(bf16[240,1024]{1,0:T(8,128)(2,1)S(1)} %blocks_1r272.1), channel_id=1, source_target_pairs={{0,32},{32,64},{64,96},{96,0},{1,33},{33,65},{65,97},{97,1},{2,34}... | collective-permute-start | bytes 1474568 | tf_op jit(solution)/shard_map/ppermute | solution.py:244
  87.1 18.2 %collective-permute-start.21 = (bf16[272,1024]{1,0:T(8,128)(2,1)S(1)}, bf16[272,1024]{1,0:T(8,128)(2,1)S(1)}, u32[]{:S(2)}, u32[]{:S(2)}) collective-permute-start(bf16[272,1024]{1,0:T(8,128)(2,1)S(1)} %blocks_3r0.1), channel_id=1, source_target_pairs={{0,96},{32,0},{64,32},{96,64},{1,97},{33,1},{65,33},{97,65},{2,98}... | collective-permute-start | bytes 1671176 | tf_op jit(solution)/shard_map/ppermute | solution.py:244
  94.5 18.0 %collective-permute-start.23 = (bf16[272,1024]{1,0:T(8,128)(2,1)S(1)}, bf16[272,1024]{1,0:T(8,128)(2,1)S(1)}, u32[]{:S(2)}, u32[]{:S(2)}) collective-permute-start(bf16[272,1024]{1,0:T(8,128)(2,1)S(1)} %blocks_1r0.1), channel_id=1, source_target_pairs={{0,32},{32,64},{64,96},{96,0},{1,33},{33,65},{65,97},{97,1},{2,34}... | collective-permute-start | bytes 1671176 | tf_op jit(solution)/shard_map/ppermute | solution.py:244
  98.8 15.0 %collective-permute-start.20 = (bf16[240,1024]{1,0:T(8,128)(2,1)S(1)}, bf16[240,1024]{1,0:T(8,128)(2,1)S(1)}, u32[]{:S(2)}, u32[]{:S(2)}) collective-permute-start(bf16[240,1024]{1,0:T(8,128)(2,1)S(1)} %blocks_3r272.1), channel_id=1, source_target_pairs={{0,96},{32,0},{64,32},{96,64},{1,97},{33,1},{65,33},{97,65},{2,98}... | collective-permute-start | bytes 1474568 | tf_op jit(solution)/shard_map/ppermute | solution.py:244

commit v4 on v3

--- a/solution.py
+++ b/solution.py
@@ -36,29 +36,29 @@
     return pairs
 
 
-def prep_kernel(a_ref, o0_ref, o1_ref, a_vm, sem):
+def prep_kernel(k, a_ref, *rest):
+    o_ref, a_vm, sem = rest[-3:]
     z, c = lax.axis_index("z"), lax.axis_index("c")
-    first = code_of(lax.rem(z - 2 * c + 4, 4))
-    copies = [pltpu.make_async_copy(a_ref.at[e], a_vm.at[e], sem.at[e]) for e in range(4)]
+    code = code_of(lax.rem(z - 2 * c + 4, 4)) ^ (2 * k)
+    off = pl.multiple_of((code // 2) * 512, 512)
+    copies = [pltpu.make_async_copy(a_ref.at[e, :, pl.ds(off, 512)], a_vm.at[e], sem.at[e]) for e in range(4)]
     for copy in copies:
         copy.start()
     for e in range(4):
         copies[e].wait()
-        for k, o_ref in enumerate((o0_ref, o1_ref)):
-            off = pl.multiple_of(((first ^ (2 * k)) // 2) * 512, 512)
-            o_ref[e] = a_vm[e, :, pl.ds(off, 512)].T
-
-
-def prep(a):
+        o_ref[e] = a_vm[e].T
+
+
+def prep(k, a, *before):
     return pl.pallas_call(
-        prep_kernel,
-        out_shape=[jax.ShapeDtypeStruct((4, 512, 128), BF)] * 2,
-        in_specs=[pl.BlockSpec(memory_space=pltpu.HBM)],
-        out_specs=[VM] * 2,
-        scratch_shapes=[pltpu.VMEM((4, 128, 1024), BF), pltpu.SemaphoreType.DMA((4,))],
+        functools.partial(prep_kernel, k),
+        out_shape=jax.ShapeDtypeStruct((4, 512, 128), BF),
+        in_specs=[ANY] * (1 + len(before)),
+        out_specs=VM,
+        scratch_shapes=[pltpu.VMEM((4, 128, 512), BF), pltpu.SemaphoreType.DMA((4,))],
         compiler_params=pltpu.CompilerParams(vmem_limit_bytes=VMEM_LIMIT),
-        name="prep",
-    )(a)
+        name=f"prep{k}",
+    )(a, *before)
 
 
 def encode(acc, o_ref):
@@ -256,9 +256,14 @@
 def body(a, g):
     hold = lax.optimization_barrier
     gc = cross(g)
-    r0, r1 = (lax.ppermute(p, ("z", "c"), round_pairs(k)) for k, p in enumerate(prep(a)))
-    r0, r1, gc = hold((r0, r1, gc))
-    r1c, r0c = cross(r1), cross(r0)
+    p1 = prep(1, a)
+    p0 = prep(0, a, p1)
+    r1 = lax.ppermute(p1, ("z", "c"), round_pairs(1))
+    r0 = lax.ppermute(p0, ("z", "c"), round_pairs(0))
+    r1, gc = hold((r1, gc))
+    r1c = cross(r1)
+    r0, r1c = hold((r0, r1c))
+    r0c = cross(r0)
     za = both_ways(jnp.stack([g[:2], gc[:2]]), "z")
     zb = both_ways(jnp.stack([g[2:], gc[2:]]), "z")
     m1 = both_ways(jnp.concatenate([r1, r1c]), "y")

time: 115 us -> 111 us (0.965)
  waiting for transfers between devices: 41.8 us -> 35.2 us
  starting transfers between devices: 35.4 us -> 38.7 us
  local copies, waits for them, and re-layouts: 2.82 us -> 1.63 us
    ppermute x8, starting transfers between devices: 12.6 us -> 19.4 us  [both_ways(): return lax.ppermute(v, (axis, 'c'), pairs)]
    ppermute x14, starting transfers between devices: 17.2 us -> 12.3 us  [send(): return lax.ppermute(v, axis, ring(2 if axis == 'c' else 4, step))]
    ppermute x2, waiting for transfers between devices: 12.7 us -> 8.2 us  [the longest x1 8.19 us: body(): r1 = lax.ppermute(p1, ('z', 'c'), round_pairs(1))]
    ppermute x2, starting transfers between devices: 5.67 us -> 6.99 us  [the longest x1 3.92 us: body(): r1 = lax.ppermute(p1, ('z', 'c'), round_pairs(1))]
    ppermute x8, waiting for transfers between devices: 24.3 us -> 23 us  [both_ways(): return lax.ppermute(v, (axis, 'c'), pairs)]
    another operation x2, local copies, waits for them, and re-layouts: 1.34 us -> 0.15 us  [body(): za = both_ways(jnp.stack([g[:2], gc[:2]]), 'z')]
  transfers between devices with their start and end apart: 24 -> 24, of which waited for: 13 -> 12; matrix products, arithmetic and copies ran while one was open for 2% -> 1% of each run, Pallas kernels for 27% -> 28%
where the time goes in v4:
time: 111 us
  starting transfers between devices  38.7 us (35%)
  waiting for transfers between devices  35.2 us (32%)
  Pallas kernels  34.7 us (31%)
  local copies, waits for them, and re-layouts  1.63 us (1%)
    pallas_call x9, Pallas kernels, blocks(): pl.pallas_call(functools.partial(blocks_kernel, jobs, len(extra)), out_sh...  30.8 us
    ppermute x8, waiting for transfers between devices, both_ways(): return lax.ppermute(v, (axis, 'c'), pairs)  23 us
    ppermute x8, starting transfers between devices, both_ways(): return lax.ppermute(v, (axis, 'c'), pairs)  19.4 us
    ppermute x14, starting transfers between devices, send(): return lax.ppermute(v, axis, ring(2 if axis == 'c' else 4, step))  12.3 us
    ppermute x1, waiting for transfers between devices, body(): r1 = lax.ppermute(p1, ('z', 'c'), round_pairs(1))  8.19 us
    ppermute x14, waiting for transfers between devices, send(): return lax.ppermute(v, axis, ring(2 if axis == 'c' else 4, step))  3.94 us
    ppermute x1, starting transfers between devices, body(): r1 = lax.ppermute(p1, ('z', 'c'), round_pairs(1))  3.92 us
    ppermute x1, starting transfers between devices, body(): r0 = lax.ppermute(p0, ('z', 'c'), round_pairs(0))  3.07 us
  transfers between devices with their start and end apart: 24, of which 12 were waited for; matrix products, arithmetic and copies ran while one was open for 1% of the time, Pallas kernels for 28%

profile of v4, /device:TPU:1, one launch (start us, length us, event | category | flops | bytes accessed | tf_op | source)
XLA Modules:
  0.0 111.0 jit_solution(17200872128867591443)
XLA Ops:
  0.0 1.4 %collective-permute-start.2 = (bf16[4,128,1024]{2,1,0:T(8,128)(2,1)}, bf16[4,128,1024]{2,1,0:T(8,128)(2,1)S(1)}, u32[]{:S(2)}, u32[]{:S(2)}) collective-permute-start(bf16[4,128,1024]{2,1,0:T(8,128)(2,1)} %g.1), channel_id=1, source_target_pairs={{0,1},{1,0},{2,3},{3,2},{4,5},{5,4},{6,7},{7,6},{8,9},{9,8},{10,11... | collective-permute-start | bytes 3145736 | tf_op jit(solution)/shard_map/ppermute | solution.py:244
  1.4 1.2 %copy-done.1 = bf16[4,128,1024]{2,1,0:T(8,128)(2,1)S(1)} copy-done((bf16[4,128,1024]{2,1,0:T(8,128)(2,1)S(1)}, bf16[4,128,1024]{2,1,0:T(8,128)(2,1)}, u32[]{:S(2)}) %copy-start.1) | copy-done | bytes 1048600
  2.6 0.5 prep1.1.rest_0_
  3.1 3.9 %collective-permute-start.1 = (bf16[4,512,128]{2,1,0:T(8,128)(2,1)S(1)}, bf16[4,512,128]{2,1,0:T(8,128)(2,1)S(1)}, u32[]{:S(2)}, u32[]{:S(2)}) collective-permute-start(bf16[4,512,128]{2,1,0:T(8,128)(2,1)S(1)} %prep1.1.rest_0_), channel_id=1, source_target_pairs={{0,8},{1,25},{8,1},{9,16},{16,9},{17,24},{24,0},{25,17},{2,10},{3,... | collective-permute-start | bytes 1572872 | tf_op jit(solution)/shard_map/ppermute | solution.py:261
  7.0 0.5 prep0.1
  7.5 3.1 %collective-permute-start = (bf16[4,512,128]{2,1,0:T(8,128)(2,1)S(1)}, bf16[4,512,128]{2,1,0:T(8,128)(2,1)S(1)}, u32[]{:S(2)}, u32[]{:S(2)}) collective-permute-start(bf16[4,512,128]{2,1,0:T(8,128)(2,1)S(1)} %prep0.1), channel_id=1, source_target_pairs={{0,0},{1,17},{8,9},{9,24},{16,1},{17,16},{24,8},{25,25},{2,2},{3,1... | collective-permute-start | bytes 1572872 | tf_op jit(solution)/shard_map/ppermute | solution.py:262
  10.6 8.2 %collective-permute-done.1.refs_1_ = bf16[4,512,128]{2,1,0:T(8,128)(2,1)S(1)} collective-permute-done((bf16[4,512,128]{2,1,0:T(8,128)(2,1)S(1)}, bf16[4,512,128]{2,1,0:T(8,128)(2,1)S(1)}, u32[]{:S(2)}, u32[]{:S(2)}) %collective-permute-start.1) | collective-permute-done | bytes 524320 | tf_op jit(solution)/shard_map/ppermute | solution.py:261
  19.1 3.2 %collective-permute-start.8 = (bf16[2,2,128,1024]{3,2,1,0:T(8,128)(2,1)S(1)}, bf16[2,2,128,1024]{3,2,1,0:T(8,128)(2,1)S(1)}, u32[]{:S(2)}, u32[]{:S(2)}) collective-permute-start(bf16[2,2,128,1024]{3,2,1,0:T(8,128)(2,1)S(1)} %pad_maximum_fusion.3), channel_id=1, source_target_pairs={{0,8},{8,16},{16,24},{24,0},{1,25},{9,1},{17,9},{25,17},{2,10},{10... | collective-permute-start | bytes 3145736 | tf_op jit(solution)/shard_map/ppermute | solution.py:249
  22.4 2.8 %collective-permute-start.7 = (bf16[8,512,128]{2,1,0:T(8,128)(2,1)S(1)}, bf16[8,512,128]{2,1,0:T(8,128)(2,1)S(1)}, u32[]{:S(2)}, u32[]{:S(2)}) collective-permute-start(bf16[8,512,128]{2,1,0:T(8,128)(2,1)S(1)} %pad_maximum_fusion.2), channel_id=1, source_target_pairs={{0,2},{2,4},{4,6},{6,0},{1,7},{3,1},{5,3},{7,5},{8,10},{10,12},{12... | collective-permute-start | bytes 3145736 | tf_op jit(solution)/shard_map/ppermute | solution.py:249
  25.3 1.6 %collective-permute-start.6 = (bf16[2,2,128,1024]{3,2,1,0:T(8,128)(2,1)S(1)}, bf16[2,2,128,1024]{3,2,1,0:T(8,128)(2,1)S(1)}, u32[]{:S(2)}, u32[]{:S(2)}) collective-permute-start(bf16[2,2,128,1024]{3,2,1,0:T(8,128)(2,1)S(1)} %pad_maximum_fusion.1), channel_id=1, source_target_pairs={{0,8},{8,16},{16,24},{24,0},{1,25},{9,1},{17,9},{25,17},{2,10},{10... | collective-permute-start | bytes 3145736 | tf_op jit(solution)/shard_map/ppermute | solution.py:249
  26.9 0.2 collective-permute-done.4.refs_2_
  27.2 0.5 collective-permute-start.5
  27.7 6.3 %collective-permute-done.8.za = bf16[2,2,128,1024]{3,2,1,0:T(8,128)(2,1)S(1)} collective-permute-done((bf16[2,2,128,1024]{3,2,1,0:T(8,128)(2,1)S(1)}, bf16[2,2,128,1024]{3,2,1,0:T(8,128)(2,1)S(1)}, u32[]{:S(2)}, u32[]{:S(2)}) %collective-permute-start.8) | collective-permute-done | bytes 1048608 | tf_op jit(solution)/shard_map/ppermute | solution.py:249
  34.0 2.9 %collective-permute-done.7.refs_5_ = bf16[8,512,128]{2,1,0:T(8,128)(2,1)S(1)} collective-permute-done((bf16[8,512,128]{2,1,0:T(8,128)(2,1)S(1)}, bf16[8,512,128]{2,1,0:T(8,128)(2,1)S(1)}, u32[]{:S(2)}, u32[]{:S(2)}) %collective-permute-start.7) | collective-permute-done | bytes 1048608 | tf_op jit(solution)/shard_map/ppermute | solution.py:249
  36.9 0.1 collective-permute-start.9
  37.1 0.5 collective-permute-start.10
  37.6 3.5 %collective-permute-start.12 = (bf16[4,512,128]{2,1,0:T(8,128)(2,1)S(1)}, bf16[4,512,128]{2,1,0:T(8,128)(2,1)S(1)}, u32[]{:S(2)}, u32[]{:S(2)}) collective-permute-start(bf16[4,512,128]{2,1,0:T(8,128)(2,1)S(1)} %slice.36), channel_id=1, source_target_pairs={{0,2},{2,4},{4,6},{6,0},{1,7},{3,1},{5,3},{7,5},{8,10},{10,12},{12... | collective-permute-start | bytes 1572872 | tf_op jit(solution)/shard_map/ppermute | solution.py:249
  41.1 4.1 %collective-permute-done.6.zb = bf16[2,2,128,1024]{3,2,1,0:T(8,128)(2,1)S(1)} collective-permute-done((bf16[2,2,128,1024]{3,2,1,0:T(8,128)(2,1)S(1)}, bf16[2,2,128,1024]{3,2,1,0:T(8,128)(2,1)S(1)}, u32[]{:S(2)}, u32[]{:S(2)}) %collective-permute-start.6) | collective-permute-done | bytes 1048608 | tf_op jit(solution)/shard_map/ppermute | solution.py:249
  45.2 2.9 %collective-permute-done.5.refs_4_ = bf16[8,512,128]{2,1,0:T(8,128)(2,1)S(1)} collective-permute-done((bf16[8,512,128]{2,1,0:T(8,128)(2,1)S(1)}, bf16[8,512,128]{2,1,0:T(8,128)(2,1)S(1)}, u32[]{:S(2)}, u32[]{:S(2)}) %collective-permute-start.5) | collective-permute-done | bytes 1048608 | tf_op jit(solution)/shard_map/ppermute | solution.py:249
  48.2 0.1 collective-permute-start.15
  48.3 3.1 %collective-permute-start.13 = (bf16[2,128,1024]{2,1,0:T(8,128)(2,1)S(1)}, bf16[2,128,1024]{2,1,0:T(8,128)(2,1)S(1)}, u32[]{:S(2)}, u32[]{:S(2)}) collective-permute-start(bf16[2,128,1024]{2,1,0:T(8,128)(2,1)S(1)} %get-tuple-element.45), channel_id=1, source_target_pairs={{0,8},{8,16},{16,24},{24,0},{1,25},{9,1},{17,9},{25,17},{2,10},{10... | collective-permute-start | bytes 1572872 | tf_op jit(solution)/shard_map/ppermute | solution.py:249
  51.4 1.6 %collective-permute-start.11 = (bf16[4,512,128]{2,1,0:T(8,128)(2,1)S(1)}, bf16[4,512,128]{2,1,0:T(8,128)(2,1)S(1)}, u32[]{:S(2)}, u32[]{:S(2)}) collective-permute-start(bf16[4,512,128]{2,1,0:T(8,128)(2,1)S(1)} %slice.35), channel_id=1, source_target_pairs={{0,2},{2,4},{4,6},{6,0},{1,7},{3,1},{5,3},{7,5},{8,10},{10,12},{12... | collective-permute-start | bytes 1572872 | tf_op jit(solution)/shard_map/ppermute | solution.py:249
  53.1 0.7 collective-permute-done.12.refs_9_
  53.8 0.1 collective-permute-start.16
  53.9 3.1 %collective-permute-start.14 = (bf16[2,128,1024]{2,1,0:T(8,128)(2,1)S(1)}, bf16[2,128,1024]{2,1,0:T(8,128)(2,1)S(1)}, u32[]{:S(2)}, u32[]{:S(2)}) collective-permute-start(bf16[2,128,1024]{2,1,0:T(8,128)(2,1)S(1)} %get-tuple-element.43), channel_id=1, source_target_pairs={{0,8},{8,16},{16,24},{24,0},{1,25},{9,1},{17,9},{25,17},{2,10},{10... | collective-permute-start | bytes 1572872 | tf_op jit(solution)/shard_map/ppermute | solution.py:249
  57.0 0.5 collective-permute-done.13.fa
  57.5 2.3 %collective-permute-done.11.refs_8_ = bf16[4,512,128]{2,1,0:T(8,128)(2,1)S(1)} collective-permute-done((bf16[4,512,128]{2,1,0:T(8,128)(2,1)S(1)}, bf16[4,512,128]{2,1,0:T(8,128)(2,1)S(1)}, u32[]{:S(2)}, u32[]{:S(2)}) %collective-permute-start.11) | collective-permute-done | bytes 524320 | tf_op jit(solution)/shard_map/ppermute | solution.py:249
  59.8 3.3 %collective-permute-done.14.fb = bf16[2,128,1024]{2,1,0:T(8,128)(2,1)S(1)} collective-permute-done((bf16[2,128,1024]{2,1,0:T(8,128)(2,1)S(1)}, bf16[2,128,1024]{2,1,0:T(8,128)(2,1)S(1)}, u32[]{:S(2)}, u32[]{:S(2)}) %collective-permute-start.14) | collective-permute-done | bytes 524320 | tf_op jit(solution)/shard_map/ppermute | solution.py:249
  63.2 1.6 %collective-permute-start.17 = (bf16[8,512,128]{2,1,0:T(8,128)(2,1)S(1)}, bf16[8,512,128]{2,1,0:T(8,128)(2,1)S(1)}, u32[]{:S(2)}, u32[]{:S(2)}) collective-permute-start(bf16[8,512,128]{2,1,0:T(8,128)(2,1)S(1)} %pad_maximum_fusion.4), channel_id=1, source_target_pairs={{0,1},{1,0},{2,3},{3,2},{4,5},{5,4},{6,7},{7,6},{8,9},{9,8},{10,11... | collective-permute-start | bytes 3145736 | tf_op jit(solution)/shard_map/ppermute | solution.py:244
  64.9 0.4 gather.1.refs_11_
  65.2 2.8 %blocks_2r0.2.refs_12_ = f32[512,1024]{1,0:T(8,128)S(1)} custom-call(bf16[4,512,128]{2,1,0:T(8,128)(2,1)S(1)} %collective-permute-done.refs_0_.refs_10_, bf16[4,512,128]{2,1,0:T(8,128)(2,1)S(1)} %collective-permute-done.1.refs_1_, bf16[4,512,128]{2,1,0:T(8,128)(2,1)S(1)} %collective-permute-done.4.refs_2_, ...), custom_call_target="tpu_custom_call" | custom-call | flops 2147483648 | bytes 5242880 | tf_op jit(solution)/shard_map/blocks_2r0/pallas_call | solution.py:199
  68.0 2.2 %blocks_2r0.3 = bf16[272,1024]{1,0:T(8,128)(2,1)S(1)} custom-call(bf16[4,512,128]{2,1,0:T(8,128)(2,1)S(1)} %collective-permute-done.refs_0_.refs_10_, bf16[4,512,128]{2,1,0:T(8,128)(2,1)S(1)} %collective-permute-done.1.refs_1_, bf16[4,512,128]{2,1,0:T(8,128)(2,1)S(1)} %collective-permute-done.4.refs_2_, ...), custom_call_target="tpu_custom_call" | custom-call | flops 2147483648 | bytes 5242880 | tf_op jit(solution)/shard_map/blocks_2r0/pallas_call | solution.py:199
  70.3 1.3 %collective-permute-start.22 = (bf16[272,1024]{1,0:T(8,128)(2,1)S(1)}, bf16[272,1024]{1,0:T(8,128)(2,1)S(1)}, u32[]{:S(2)}, u32[]{:S(2)}) collective-permute-start(bf16[272,1024]{1,0:T(8,128)(2,1)S(1)} %blocks_2r0.3), channel_id=1, source_target_pairs={{0,32},{32,64},{64,96},{96,0},{1,33},{33,65},{65,97},{97,1},{2,34}... | collective-permute-start | bytes 1671176 | tf_op jit(solution)/shard_map/ppermute | solution.py:244
  71.6 2.1 %blocks_2r272.1 = bf16[240,1024]{1,0:T(8,128)(2,1)S(1)} custom-call(bf16[4,512,128]{2,1,0:T(8,128)(2,1)S(1)} %collective-permute-done.refs_0_.refs_10_, bf16[4,512,128]{2,1,0:T(8,128)(2,1)S(1)} %collective-permute-done.1.refs_1_, bf16[4,512,128]{2,1,0:T(8,128)(2,1)S(1)} %collective-permute-done.4.refs_2_, ...), custom_call_target="tpu_custom_call" | custom-call | flops 2147483648 | bytes 5242880 | tf_op jit(solution)/shard_map/blocks_2r272/pallas_call | solution.py:199
  73.7 1.5 %collective-permute-start.19 = (bf16[240,1024]{1,0:T(8,128)(2,1)S(1)}, bf16[240,1024]{1,0:T(8,128)(2,1)S(1)}, u32[]{:S(2)}, u32[]{:S(2)}) collective-permute-start(bf16[240,1024]{1,0:T(8,128)(2,1)S(1)} %blocks_2r272.1), channel_id=1, source_target_pairs={{0,96},{32,0},{64,32},{96,64},{1,97},{33,1},{65,33},{97,65},{2,98}... | collective-permute-start | bytes 1474568 | tf_op jit(solution)/shard_map/ppermute | solution.py:244
  75.2 3.6 %blocks_1r272.1 = bf16[240,1024]{1,0:T(8,128)(2,1)S(1)} custom-call(bf16[4,512,128]{2,1,0:T(8,128)(2,1)S(1)} %collective-permute-done.refs_0_.refs_10_, bf16[4,512,128]{2,1,0:T(8,128)(2,1)S(1)} %collective-permute-done.1.refs_1_, bf16[4,512,128]{2,1,0:T(8,128)(2,1)S(1)} %collective-permute-done.4.refs_2_, ...), custom_call_target="tpu_custom_call" | custom-call | flops 2147483648 | bytes 5242880 | tf_op jit(solution)/shard_map/blocks_1r272/pallas_call | solution.py:199
  78.8 0.3 collective-permute-start.18
  79.1 3.7 %blocks_3r0.1 = bf16[272,1024]{1,0:T(8,128)(2,1)S(1)} custom-call(bf16[4,512,128]{2,1,0:T(8,128)(2,1)S(1)} %collective-permute-done.refs_0_.refs_10_, bf16[4,512,128]{2,1,0:T(8,128)(2,1)S(1)} %collective-permute-done.1.refs_1_, bf16[4,512,128]{2,1,0:T(8,128)(2,1)S(1)} %collective-permute-done.4.refs_2_, ...), custom_call_target="tpu_custom_call" | custom-call | flops 2147483648 | bytes 5242880 | tf_op jit(solution)/shard_map/blocks_3r0/pallas_call | solution.py:199
  82.8 2.5 %collective-permute-start.21 = (bf16[272,1024]{1,0:T(8,128)(2,1)S(1)}, bf16[272,1024]{1,0:T(8,128)(2,1)S(1)}, u32[]{:S(2)}, u32[]{:S(2)}) collective-permute-start(bf16[272,1024]{1,0:T(8,128)(2,1)S(1)} %blocks_3r0.1), channel_id=1, source_target_pairs={{0,96},{32,0},{64,32},{96,64},{1,97},{33,1},{65,33},{97,65},{2,98}... | collective-permute-start | bytes 1671176 | tf_op jit(solution)/shard_map/ppermute | solution.py:244
  85.3 0.4 collective-permute-done.22.refs_12_
  85.8 4.4 %blocks_1r0.1 = bf16[272,1024]{1,0:T(8,128)(2,1)S(1)} custom-call(bf16[4,512,128]{2,1,0:T(8,128)(2,1)S(1)} %collective-permute-done.refs_0_.refs_10_, bf16[4,512,128]{2,1,0:T(8,128)(2,1)S(1)} %collective-permute-done.1.refs_1_, bf16[4,512,128]{2,1,0:T(8,128)(2,1)S(1)} %collective-permute-done.4.refs_2_, ...), custom_call_target="tpu_custom_call" | custom-call | flops 2147483648 | bytes 5242880 | tf_op jit(solution)/shard_map/blocks_1r0/pallas_call | solution.py:199
  90.3 4.3 %blocks_3r272.1 = bf16[240,1024]{1,0:T(8,128)(2,1)S(1)} custom-call(bf16[4,512,128]{2,1,0:T(8,128)(2,1)S(1)} %collective-permute-done.refs_0_.refs_10_, bf16[4,512,128]{2,1,0:T(8,128)(2,1)S(1)} %collective-permute-done.1.refs_1_, bf16[4,512,128]{2,1,0:T(8,128)(2,1)S(1)} %collective-permute-done.4.refs_2_, ...), custom_call_target="tpu_custom_call" | custom-call | flops 2147483648 | bytes 5242880 | tf_op jit(solution)/shard_map/blocks_3r272/pallas_call | solution.py:199
  94.6 2.7 %collective-permute-start.20 = (bf16[240,1024]{1,0:T(8,128)(2,1)S(1)}, bf16[240,1024]{1,0:T(8,128)(2,1)S(1)}, u32[]{:S(2)}, u32[]{:S(2)}) collective-permute-start(bf16[240,1024]{1,0:T(8,128)(2,1)S(1)} %blocks_3r272.1), channel_id=1, source_target_pairs={{0,96},{32,0},{64,32},{96,64},{1,97},{33,1},{65,33},{97,65},{2,98}... | collective-permute-start | bytes 1474568 | tf_op jit(solution)/shard_map/ppermute | solution.py:244
  97.3 3.8 %blocks_0r272.1.own = f32[240,1024]{1,0:T(8,128)S(1)} custom-call(bf16[4,512,128]{2,1,0:T(8,128)(2,1)S(1)} %collective-permute-done.refs_0_.refs_10_, bf16[4,512,128]{2,1,0:T(8,128)(2,1)S(1)} %collective-permute-done.1.refs_1_, bf16[4,512,128]{2,1,0:T(8,128)(2,1)S(1)} %collective-permute-done.4.refs_2_, ...), custom_call_target="tpu_custom_call" | custom-call | flops 2147483648 | bytes 5242880 | tf_op jit(solution)/shard_map/blocks_0r272/pallas_call | solution.py:199
  101.1 3.9 %blocks_0r0.1.own = f32[272,1024]{1,0:T(8,128)S(1)} custom-call(bf16[4,512,128]{2,1,0:T(8,128)(2,1)S(1)} %collective-permute-done.refs_0_.refs_10_, bf16[4,512,128]{2,1,0:T(8,128)(2,1)S(1)} %collective-permute-done.1.refs_1_, bf16[4,512,128]{2,1,0:T(8,128)(2,1)S(1)} %collective-permute-done.4.refs_2_, ...), custom_call_target="tpu_custom_call" | custom-call | flops 2147483648 | bytes 5242880 | tf_op jit(solution)/shard_map/blocks_0r0/pallas_call | solution.py:199
  105.0 3.3 %collective-permute-done.23.p = bf16[272,1024]{1,0:T(8,128)(2,1)S(1)} collective-permute-done((bf16[272,1024]{1,0:T(8,128)(2,1)S(1)}, bf16[272,1024]{1,0:T(8,128)(2,1)S(1)}, u32[]{:S(2)}, u32[]{:S(2)}) %collective-permute-start.23) | collective-permute-done | bytes 557088 | tf_op jit(solution)/shard_map/ppermute | solution.py:244
  108.3 1.3 %final0.1.rest_0_ = f32[512,1024]{1,0:T(8,128)} custom-call(f32[272,1024]{1,0:T(8,128)S(1)} %blocks_0r0.1.own, bf16[272,1024]{1,0:T(8,128)(2,1)S(1)} %collective-permute-done.23.p), custom_call_target="tpu_custom_call" | custom-call | tf_op jit(solution)/shard_map/final0/pallas_call | solution.py:231
  109.6 1.3 %final1.1 = f32[512,1024]{1,0:T(8,128)} custom-call(f32[240,1024]{1,0:T(8,128)S(1)} %blocks_0r272.1.own, bf16[240,1024]{1,0:T(8,128)(2,1)S(1)} %collective-permute-done.20.p, f32[512,1024]{1,0:T(8,128)} %final0.1.rest_0_), custom_call_target="tpu_custom_call", output_to_operand_aliasing={{}: (2, {})} | custom-call | tf_op jit(solution)/shard_map/final1/pallas_call | solution.py:231
  (29 shorter events, 1.0 us)
Async XLA Ops:
  0.0 18.8 %copy-start = (bf16[4,128,1024]{2,1,0:T(8,128)(2,1)S(1)}, bf16[4,128,1024]{2,1,0:T(8,128)(2,1)}, u32[]{:S(2)}) copy-start(bf16[4,128,1024]{2,1,0:T(8,128)(2,1)} %g.1) | copy-start | bytes 3145732
  0.0 18.8 %collective-permute-start.2 = (bf16[4,128,1024]{2,1,0:T(8,128)(2,1)}, bf16[4,128,1024]{2,1,0:T(8,128)(2,1)S(1)}, u32[]{:S(2)}, u32[]{:S(2)}) collective-permute-start(bf16[4,128,1024]{2,1,0:T(8,128)(2,1)} %g.1), channel_id=1, source_target_pairs={{0,1},{1,0},{2,3},{3,2},{4,5},{5,4},{6,7},{7,6},{8,9},{9,8},{10,11... | collective-permute-start | bytes 3145736 | tf_op jit(solution)/shard_map/ppermute | solution.py:244
  1.4 1.2 %copy-start.1 = (bf16[4,128,1024]{2,1,0:T(8,128)(2,1)S(1)}, bf16[4,128,1024]{2,1,0:T(8,128)(2,1)}, u32[]{:S(2)}) copy-start(bf16[4,128,1024]{2,1,0:T(8,128)(2,1)} %a_ref.3) | copy-start | bytes 3145732
  3.1 15.7 %collective-permute-start.1 = (bf16[4,512,128]{2,1,0:T(8,128)(2,1)S(1)}, bf16[4,512,128]{2,1,0:T(8,128)(2,1)S(1)}, u32[]{:S(2)}, u32[]{:S(2)}) collective-permute-start(bf16[4,512,128]{2,1,0:T(8,128)(2,1)S(1)} %prep1.1.rest_0_), channel_id=1, source_target_pairs={{0,8},{1,25},{8,1},{9,16},{16,9},{17,24},{24,0},{25,17},{2,10},{3,... | collective-permute-start | bytes 1572872 | tf_op jit(solution)/shard_map/ppermute | solution.py:261
  7.5 14.7 %collective-permute-start = (bf16[4,512,128]{2,1,0:T(8,128)(2,1)S(1)}, bf16[4,512,128]{2,1,0:T(8,128)(2,1)S(1)}, u32[]{:S(2)}, u32[]{:S(2)}) collective-permute-start(bf16[4,512,128]{2,1,0:T(8,128)(2,1)S(1)} %prep0.1), channel_id=1, source_target_pairs={{0,0},{1,17},{8,9},{9,24},{16,1},{17,16},{24,8},{25,25},{2,2},{3,1... | collective-permute-start | bytes 1572872 | tf_op jit(solution)/shard_map/ppermute | solution.py:262
  18.8 3.5 %collective-permute-start.3 = (bf16[4,512,128]{2,1,0:T(8,128)(2,1)S(1)}, bf16[4,512,128]{2,1,0:T(8,128)(2,1)S(1)}, u32[]{:S(2)}, u32[]{:S(2)}) collective-permute-start(bf16[4,512,128]{2,1,0:T(8,128)(2,1)S(1)} %collective-permute-done.1.refs_1_), channel_id=1, source_target_pairs={{0,1},{1,0},{2,3},{3,2},{4,5},{5,4},{6,7},{7,6},{8,9},{9,8},{10,11... | collective-permute-start | bytes 1572872 | tf_op jit(solution)/shard_map/ppermute | solution.py:244
  19.1 14.9 %collective-permute-start.8 = (bf16[2,2,128,1024]{3,2,1,0:T(8,128)(2,1)S(1)}, bf16[2,2,128,1024]{3,2,1,0:T(8,128)(2,1)S(1)}, u32[]{:S(2)}, u32[]{:S(2)}) collective-permute-start(bf16[2,2,128,1024]{3,2,1,0:T(8,128)(2,1)S(1)} %pad_maximum_fusion.3), channel_id=1, source_target_pairs={{0,8},{8,16},{16,24},{24,0},{1,25},{9,1},{17,9},{25,17},{2,10},{10... | collective-permute-start | bytes 3145736 | tf_op jit(solution)/shard_map/ppermute | solution.py:249
  22.4 14.5 %collective-permute-start.7 = (bf16[8,512,128]{2,1,0:T(8,128)(2,1)S(1)}, bf16[8,512,128]{2,1,0:T(8,128)(2,1)S(1)}, u32[]{:S(2)}, u32[]{:S(2)}) collective-permute-start(bf16[8,512,128]{2,1,0:T(8,128)(2,1)S(1)} %pad_maximum_fusion.2), channel_id=1, source_target_pairs={{0,2},{2,4},{4,6},{6,0},{1,7},{3,1},{5,3},{7,5},{8,10},{10,12},{12... | collective-permute-start | bytes 3145736 | tf_op jit(solution)/shard_map/ppermute | solution.py:249
  25.2 1.9 %collective-permute-start.4 = (bf16[4,512,128]{2,1,0:T(8,128)(2,1)S(1)}, bf16[4,512,128]{2,1,0:T(8,128)(2,1)S(1)}, u32[]{:S(2)}, u32[]{:S(2)}) collective-permute-start(bf16[4,512,128]{2,1,0:T(8,128)(2,1)S(1)} %collective-permute-done.refs_0_.refs_10_), channel_id=1, source_target_pairs={{0,1},{1,0},{2,3},{3,2},{4,5},{5,4},{6,7},{7,6},{8,9},{9,8},{10,11... | collective-permute-start | bytes 1572872 | tf_op jit(solution)/shard_map/ppermute | solution.py:244
  25.3 20.0 %collective-permute-start.6 = (bf16[2,2,128,1024]{3,2,1,0:T(8,128)(2,1)S(1)}, bf16[2,2,128,1024]{3,2,1,0:T(8,128)(2,1)S(1)}, u32[]{:S(2)}, u32[]{:S(2)}) collective-permute-start(bf16[2,2,128,1024]{3,2,1,0:T(8,128)(2,1)S(1)} %pad_maximum_fusion.1), channel_id=1, source_target_pairs={{0,8},{8,16},{16,24},{24,0},{1,25},{9,1},{17,9},{25,17},{2,10},{10... | collective-permute-start | bytes 3145736 | tf_op jit(solution)/shard_map/ppermute | solution.py:249
  27.2 21.0 %collective-permute-start.5 = (bf16[8,512,128]{2,1,0:T(8,128)(2,1)S(1)}, bf16[8,512,128]{2,1,0:T(8,128)(2,1)S(1)}, u32[]{:S(2)}, u32[]{:S(2)}) collective-permute-start(bf16[8,512,128]{2,1,0:T(8,128)(2,1)S(1)} %pad_maximum_fusion), channel_id=1, source_target_pairs={{0,2},{2,4},{4,6},{6,0},{1,7},{3,1},{5,3},{7,5},{8,10},{10,12},{12... | collective-permute-start | bytes 3145736 | tf_op jit(solution)/shard_map/ppermute | solution.py:249
  36.9 11.2 %collective-permute-start.9 = (bf16[8,512,128]{2,1,0:T(8,128)(2,1)S(1)}, bf16[8,512,128]{2,1,0:T(8,128)(2,1)S(1)}, u32[]{:S(2)}, u32[]{:S(2)}) collective-permute-start(bf16[8,512,128]{2,1,0:T(8,128)(2,1)S(1)} %collective-permute-done.7.refs_5_), channel_id=1, source_target_pairs={{0,1},{1,0},{2,3},{3,2},{4,5},{5,4},{6,7},{7,6},{8,9},{9,8},{10,11... | collective-permute-start | bytes 3145736 | tf_op jit(solution)/shard_map/ppermute | solution.py:244
  37.1 11.0 %collective-permute-start.10 = (bf16[2,128,1024]{2,1,0:T(8,128)(2,1)S(1)}, bf16[2,128,1024]{2,1,0:T(8,128)(2,1)S(1)}, u32[]{:S(2)}, u32[]{:S(2)}) collective-permute-start(bf16[2,128,1024]{2,1,0:T(8,128)(2,1)S(1)} %get-tuple-element.46), channel_id=1, source_target_pairs={{0,1},{1,0},{2,3},{3,2},{4,5},{5,4},{6,7},{7,6},{8,9},{9,8},{10,11... | collective-permute-start | bytes 1572872 | tf_op jit(solution)/shard_map/ppermute | solution.py:244
  37.6 16.1 %collective-permute-start.12 = (bf16[4,512,128]{2,1,0:T(8,128)(2,1)S(1)}, bf16[4,512,128]{2,1,0:T(8,128)(2,1)S(1)}, u32[]{:S(2)}, u32[]{:S(2)}) collective-permute-start(bf16[4,512,128]{2,1,0:T(8,128)(2,1)S(1)} %slice.36), channel_id=1, source_target_pairs={{0,2},{2,4},{4,6},{6,0},{1,7},{3,1},{5,3},{7,5},{8,10},{10,12},{12... | collective-permute-start | bytes 1572872 | tf_op jit(solution)/shard_map/ppermute | solution.py:249
  48.2 15.0 %collective-permute-start.15 = (bf16[8,512,128]{2,1,0:T(8,128)(2,1)S(1)}, bf16[8,512,128]{2,1,0:T(8,128)(2,1)S(1)}, u32[]{:S(2)}, u32[]{:S(2)}) collective-permute-start(bf16[8,512,128]{2,1,0:T(8,128)(2,1)S(1)} %collective-permute-done.5.refs_4_), channel_id=1, source_target_pairs={{0,1},{1,0},{2,3},{3,2},{4,5},{5,4},{6,7},{7,6},{8,9},{9,8},{10,11... | collective-permute-start | bytes 3145736 | tf_op jit(solution)/shard_map/ppermute | solution.py:244
  48.3 9.2 %collective-permute-start.13 = (bf16[2,128,1024]{2,1,0:T(8,128)(2,1)S(1)}, bf16[2,128,1024]{2,1,0:T(8,128)(2,1)S(1)}, u32[]{:S(2)}, u32[]{:S(2)}) collective-permute-start(bf16[2,128,1024]{2,1,0:T(8,128)(2,1)S(1)} %get-tuple-element.45), channel_id=1, source_target_pairs={{0,8},{8,16},{16,24},{24,0},{1,25},{9,1},{17,9},{25,17},{2,10},{10... | collective-permute-start | bytes 1572872 | tf_op jit(solution)/shard_map/ppermute | solution.py:249
  51.4 8.4 %collective-permute-start.11 = (bf16[4,512,128]{2,1,0:T(8,128)(2,1)S(1)}, bf16[4,512,128]{2,1,0:T(8,128)(2,1)S(1)}, u32[]{:S(2)}, u32[]{:S(2)}) collective-permute-start(bf16[4,512,128]{2,1,0:T(8,128)(2,1)S(1)} %slice.35), channel_id=1, source_target_pairs={{0,2},{2,4},{4,6},{6,0},{1,7},{3,1},{5,3},{7,5},{8,10},{10,12},{12... | collective-permute-start | bytes 1572872 | tf_op jit(solution)/shard_map/ppermute | solution.py:249
  53.8 6.0 %collective-permute-start.16 = (bf16[2,128,1024]{2,1,0:T(8,128)(2,1)S(1)}, bf16[2,128,1024]{2,1,0:T(8,128)(2,1)S(1)}, u32[]{:S(2)}, u32[]{:S(2)}) collective-permute-start(bf16[2,128,1024]{2,1,0:T(8,128)(2,1)S(1)} %get-tuple-element.34), channel_id=1, source_target_pairs={{0,1},{1,0},{2,3},{3,2},{4,5},{5,4},{6,7},{7,6},{8,9},{9,8},{10,11... | collective-permute-start | bytes 1572872 | tf_op jit(solution)/shard_map/ppermute | solution.py:244
  53.9 9.3 %collective-permute-start.14 = (bf16[2,128,1024]{2,1,0:T(8,128)(2,1)S(1)}, bf16[2,128,1024]{2,1,0:T(8,128)(2,1)S(1)}, u32[]{:S(2)}, u32[]{:S(2)}) collective-permute-start(bf16[2,128,1024]{2,1,0:T(8,128)(2,1)S(1)} %get-tuple-element.43), channel_id=1, source_target_pairs={{0,8},{8,16},{16,24},{24,0},{1,25},{9,1},{17,9},{25,17},{2,10},{10... | collective-permute-start | bytes 1572872 | tf_op jit(solution)/shard_map/ppermute | solution.py:249
  63.2 4.8 %collective-permute-start.17 = (bf16[8,512,128]{2,1,0:T(8,128)(2,1)S(1)}, bf16[8,512,128]{2,1,0:T(8,128)(2,1)S(1)}, u32[]{:S(2)}, u32[]{:S(2)}) collective-permute-start(bf16[8,512,128]{2,1,0:T(8,128)(2,1)S(1)} %pad_maximum_fusion.4), channel_id=1, source_target_pairs={{0,1},{1,0},{2,3},{3,2},{4,5},{5,4},{6,7},{7,6},{8,9},{9,8},{10,11... | collective-permute-start | bytes 3145736 | tf_op jit(solution)/shard_map/ppermute | solution.py:244
  70.3 15.5 %collective-permute-start.22 = (bf16[272,1024]{1,0:T(8,128)(2,1)S(1)}, bf16[272,1024]{1,0:T(8,128)(2,1)S(1)}, u32[]{:S(2)}, u32[]{:S(2)}) collective-permute-start(bf16[272,1024]{1,0:T(8,128)(2,1)S(1)} %blocks_2r0.3), channel_id=1, source_target_pairs={{0,32},{32,64},{64,96},{96,0},{1,33},{33,65},{65,97},{97,1},{2,34}... | collective-permute-start | bytes 1671176 | tf_op jit(solution)/shard_map/ppermute | solution.py:244
  73.7 16.6 %collective-permute-start.19 = (bf16[240,1024]{1,0:T(8,128)(2,1)S(1)}, bf16[240,1024]{1,0:T(8,128)(2,1)S(1)}, u32[]{:S(2)}, u32[]{:S(2)}) collective-permute-start(bf16[240,1024]{1,0:T(8,128)(2,1)S(1)} %blocks_2r272.1), channel_id=1, source_target_pairs={{0,96},{32,0},{64,32},{96,64},{1,97},{33,1},{65,33},{97,65},{2,98}... | collective-permute-start | bytes 1474568 | tf_op jit(solution)/shard_map/ppermute | solution.py:244
  78.8 18.5 %collective-permute-start.18 = (bf16[240,1024]{1,0:T(8,128)(2,1)S(1)}, bf16[240,1024]{1,0:T(8,128)(2,1)S(1)}, u32[]{:S(2)}, u32[]{:S(2)}) collective-permute-start(bf16[240,1024]{1,0:T(8,128)(2,1)S(1)} %blocks_1r272.1), channel_id=1, source_target_pairs={{0,32},{32,64},{64,96},{96,0},{1,33},{33,65},{65,97},{97,1},{2,34}... | collective-permute-start | bytes 1474568 | tf_op jit(solution)/shard_map/ppermute | solution.py:244
  82.8 18.2 %collective-permute-start.21 = (bf16[272,1024]{1,0:T(8,128)(2,1)S(1)}, bf16[272,1024]{1,0:T(8,128)(2,1)S(1)}, u32[]{:S(2)}, u32[]{:S(2)}) collective-permute-start(bf16[272,1024]{1,0:T(8,128)(2,1)S(1)} %blocks_3r0.1), channel_id=1, source_target_pairs={{0,96},{32,0},{64,32},{96,64},{1,97},{33,1},{65,33},{97,65},{2,98}... | collective-permute-start | bytes 1671176 | tf_op jit(solution)/shard_map/ppermute | solution.py:244
  90.2 18.1 %collective-permute-start.23 = (bf16[272,1024]{1,0:T(8,128)(2,1)S(1)}, bf16[272,1024]{1,0:T(8,128)(2,1)S(1)}, u32[]{:S(2)}, u32[]{:S(2)}) collective-permute-start(bf16[272,1024]{1,0:T(8,128)(2,1)S(1)} %blocks_1r0.1), channel_id=1, source_target_pairs={{0,32},{32,64},{64,96},{96,0},{1,33},{33,65},{65,97},{97,1},{2,34}... | collective-permute-start | bytes 1671176 | tf_op jit(solution)/shard_map/ppermute | solution.py:244
  94.6 15.0 %collective-permute-start.20 = (bf16[240,1024]{1,0:T(8,128)(2,1)S(1)}, bf16[240,1024]{1,0:T(8,128)(2,1)S(1)}, u32[]{:S(2)}, u32[]{:S(2)}) collective-permute-start(bf16[240,1024]{1,0:T(8,128)(2,1)S(1)} %blocks_3r272.1), channel_id=1, source_target_pairs={{0,96},{32,0},{64,32},{96,64},{1,97},{33,1},{65,33},{97,65},{2,98}... | collective-permute-start | bytes 1474568 | tf_op jit(solution)/shard_map/ppermute | solution.py:244

commit v5 on v4

--- a/solution.py
+++ b/solution.py
@@ -270,11 +270,9 @@
     m0 = both_ways(jnp.concatenate([r0, r0c]), "y")
     m1, za = hold((m1, za))
     f1, fa, m1c = both_ways(m1[:4], "y"), both_ways(za[0], "z"), cross(m1)
-    zac = cross(za[1])
-    m0, zb, m1c, zac = hold((m0, zb, m1c, zac))
+    m0, zb, m1c, zah = hold((m0, zb, m1c, za[1]))
     f0, fb, m0c = both_ways(m0[:4], "y"), both_ways(zb[0], "z"), cross(m0)
-    f1, zbh = hold((f1, zb[1]))
-    zbc = cross(zbh)
+    zac, zbc = cross(zah), cross(zb[1])
     f0, f1, fa, fb, m0c, zac, zbc = hold((f0, f1, fa, fb, m0c, zac, zbc))
     fc = cross(jnp.concatenate([f0, f1]))
     gs = gather(g, za, zb, zac, zbc, fa, fb)

time: 111 us -> 111 us (level)
  transfers between devices with their start and end apart: 24 -> 24, of which waited for: 12 -> 11; matrix products, arithmetic and copies ran while one was open for 1% -> 1% of each run, Pallas kernels for 28% -> 28%
where the time goes in v5:
time: 111 us
  starting transfers between devices  38.2 us (34%)
  waiting for transfers between devices  35.7 us (32%)
  Pallas kernels  34.7 us (31%)
  local copies, waits for them, and re-layouts  1.6 us (1%)
    pallas_call x9, Pallas kernels, blocks(): pl.pallas_call(functools.partial(blocks_kernel, jobs, len(extra)), out_sh...  30.8 us
    ppermute x8, waiting for transfers between devices, both_ways(): return lax.ppermute(v, (axis, 'c'), pairs)  23.6 us
    ppermute x8, starting transfers between devices, both_ways(): return lax.ppermute(v, (axis, 'c'), pairs)  19.4 us
    ppermute x14, starting transfers between devices, send(): return lax.ppermute(v, axis, ring(2 if axis == 'c' else 4, step))  11.8 us
    ppermute x1, waiting for transfers between devices, body(): r1 = lax.ppermute(p1, ('z', 'c'), round_pairs(1))  8.19 us
    ppermute x14, waiting for transfers between devices, send(): return lax.ppermute(v, axis, ring(2 if axis == 'c' else 4, step))  3.94 us
    ppermute x1, starting transfers between devices, body(): r1 = lax.ppermute(p1, ('z', 'c'), round_pairs(1))  3.92 us
    ppermute x1, starting transfers between devices, body(): r0 = lax.ppermute(p0, ('z', 'c'), round_pairs(0))  3.07 us
  transfers between devices with their start and end apart: 24, of which 11 were waited for; matrix products, arithmetic and copies ran while one was open for 1% of the time, Pallas kernels for 28%

profile of v5, /device:TPU:1, one launch (start us, length us, event | category | flops | bytes accessed | tf_op | source)
XLA Modules:
  0.0 111.0 jit_solution(13723644671027231052)
XLA Ops:
  0.0 1.4 %collective-permute-start.2 = (bf16[4,128,1024]{2,1,0:T(8,128)(2,1)}, bf16[4,128,1024]{2,1,0:T(8,128)(2,1)S(1)}, u32[]{:S(2)}, u32[]{:S(2)}) collective-permute-start(bf16[4,128,1024]{2,1,0:T(8,128)(2,1)} %g.1), channel_id=1, source_target_pairs={{0,1},{1,0},{2,3},{3,2},{4,5},{5,4},{6,7},{7,6},{8,9},{9,8},{10,11... | collective-permute-start | bytes 3145736 | tf_op jit(solution)/shard_map/ppermute | solution.py:244
  1.4 1.2 %copy-done.1 = bf16[4,128,1024]{2,1,0:T(8,128)(2,1)S(1)} copy-done((bf16[4,128,1024]{2,1,0:T(8,128)(2,1)S(1)}, bf16[4,128,1024]{2,1,0:T(8,128)(2,1)}, u32[]{:S(2)}) %copy-start.1) | copy-done | bytes 1048600
  2.6 0.5 prep1.1.rest_0_
  3.1 3.9 %collective-permute-start.1 = (bf16[4,512,128]{2,1,0:T(8,128)(2,1)S(1)}, bf16[4,512,128]{2,1,0:T(8,128)(2,1)S(1)}, u32[]{:S(2)}, u32[]{:S(2)}) collective-permute-start(bf16[4,512,128]{2,1,0:T(8,128)(2,1)S(1)} %prep1.1.rest_0_), channel_id=1, source_target_pairs={{0,8},{1,25},{8,1},{9,16},{16,9},{17,24},{24,0},{25,17},{2,10},{3,... | collective-permute-start | bytes 1572872 | tf_op jit(solution)/shard_map/ppermute | solution.py:261
  7.0 0.5 prep0.1
  7.5 3.1 %collective-permute-start = (bf16[4,512,128]{2,1,0:T(8,128)(2,1)S(1)}, bf16[4,512,128]{2,1,0:T(8,128)(2,1)S(1)}, u32[]{:S(2)}, u32[]{:S(2)}) collective-permute-start(bf16[4,512,128]{2,1,0:T(8,128)(2,1)S(1)} %prep0.1), channel_id=1, source_target_pairs={{0,0},{1,17},{8,9},{9,24},{16,1},{17,16},{24,8},{25,25},{2,2},{3,1... | collective-permute-start | bytes 1572872 | tf_op jit(solution)/shard_map/ppermute | solution.py:262
  10.6 8.2 %collective-permute-done.1.refs_1_ = bf16[4,512,128]{2,1,0:T(8,128)(2,1)S(1)} collective-permute-done((bf16[4,512,128]{2,1,0:T(8,128)(2,1)S(1)}, bf16[4,512,128]{2,1,0:T(8,128)(2,1)S(1)}, u32[]{:S(2)}, u32[]{:S(2)}) %collective-permute-start.1) | collective-permute-done | bytes 524320 | tf_op jit(solution)/shard_map/ppermute | solution.py:261
  19.0 0.1 pad_maximum_fusion.3
  19.1 3.2 %collective-permute-start.8 = (bf16[2,2,128,1024]{3,2,1,0:T(8,128)(2,1)S(1)}, bf16[2,2,128,1024]{3,2,1,0:T(8,128)(2,1)S(1)}, u32[]{:S(2)}, u32[]{:S(2)}) collective-permute-start(bf16[2,2,128,1024]{3,2,1,0:T(8,128)(2,1)S(1)} %pad_maximum_fusion.3), channel_id=1, source_target_pairs={{0,8},{8,16},{16,24},{24,0},{1,25},{9,1},{17,9},{25,17},{2,10},{10... | collective-permute-start | bytes 3145736 | tf_op jit(solution)/shard_map/ppermute | solution.py:249
  22.4 2.8 %collective-permute-start.7 = (bf16[8,512,128]{2,1,0:T(8,128)(2,1)S(1)}, bf16[8,512,128]{2,1,0:T(8,128)(2,1)S(1)}, u32[]{:S(2)}, u32[]{:S(2)}) collective-permute-start(bf16[8,512,128]{2,1,0:T(8,128)(2,1)S(1)} %pad_maximum_fusion.2), channel_id=1, source_target_pairs={{0,2},{2,4},{4,6},{6,0},{1,7},{3,1},{5,3},{7,5},{8,10},{10,12},{12... | collective-permute-start | bytes 3145736 | tf_op jit(solution)/shard_map/ppermute | solution.py:249
  25.2 0.1 pad_maximum_fusion.1
  25.3 1.6 %collective-permute-start.6 = (bf16[2,2,128,1024]{3,2,1,0:T(8,128)(2,1)S(1)}, bf16[2,2,128,1024]{3,2,1,0:T(8,128)(2,1)S(1)}, u32[]{:S(2)}, u32[]{:S(2)}) collective-permute-start(bf16[2,2,128,1024]{3,2,1,0:T(8,128)(2,1)S(1)} %pad_maximum_fusion.1), channel_id=1, source_target_pairs={{0,8},{8,16},{16,24},{24,0},{1,25},{9,1},{17,9},{25,17},{2,10},{10... | collective-permute-start | bytes 3145736 | tf_op jit(solution)/shard_map/ppermute | solution.py:249
  26.9 0.2 collective-permute-done.4.refs_2_
  27.2 0.5 collective-permute-start.5
  27.7 6.3 %collective-permute-done.8.za = bf16[2,2,128,1024]{3,2,1,0:T(8,128)(2,1)S(1)} collective-permute-done((bf16[2,2,128,1024]{3,2,1,0:T(8,128)(2,1)S(1)}, bf16[2,2,128,1024]{3,2,1,0:T(8,128)(2,1)S(1)}, u32[]{:S(2)}, u32[]{:S(2)}) %collective-permute-start.8) | collective-permute-done | bytes 1048608 | tf_op jit(solution)/shard_map/ppermute | solution.py:249
  34.0 2.9 %collective-permute-done.7.refs_5_ = bf16[8,512,128]{2,1,0:T(8,128)(2,1)S(1)} collective-permute-done((bf16[8,512,128]{2,1,0:T(8,128)(2,1)S(1)}, bf16[8,512,128]{2,1,0:T(8,128)(2,1)S(1)}, u32[]{:S(2)}, u32[]{:S(2)}) %collective-permute-start.7) | collective-permute-done | bytes 1048608 | tf_op jit(solution)/shard_map/ppermute | solution.py:249
  36.9 0.1 collective-permute-start.9
  37.1 3.4 %collective-permute-start.11 = (bf16[4,512,128]{2,1,0:T(8,128)(2,1)S(1)}, bf16[4,512,128]{2,1,0:T(8,128)(2,1)S(1)}, u32[]{:S(2)}, u32[]{:S(2)}) collective-permute-start(bf16[4,512,128]{2,1,0:T(8,128)(2,1)S(1)} %slice.36), channel_id=1, source_target_pairs={{0,2},{2,4},{4,6},{6,0},{1,7},{3,1},{5,3},{7,5},{8,10},{10,12},{12... | collective-permute-start | bytes 1572872 | tf_op jit(solution)/shard_map/ppermute | solution.py:249
  40.5 1.4 %collective-permute-start.12 = (bf16[2,128,1024]{2,1,0:T(8,128)(2,1)S(1)}, bf16[2,128,1024]{2,1,0:T(8,128)(2,1)S(1)}, u32[]{:S(2)}, u32[]{:S(2)}) collective-permute-start(bf16[2,128,1024]{2,1,0:T(8,128)(2,1)S(1)} %get-tuple-element.41), channel_id=1, source_target_pairs={{0,8},{8,16},{16,24},{24,0},{1,25},{9,1},{17,9},{25,17},{2,10},{10... | collective-permute-start | bytes 1572872 | tf_op jit(solution)/shard_map/ppermute | solution.py:249
  41.9 3.3 %collective-permute-done.6.zb = bf16[2,2,128,1024]{3,2,1,0:T(8,128)(2,1)S(1)} collective-permute-done((bf16[2,2,128,1024]{3,2,1,0:T(8,128)(2,1)S(1)}, bf16[2,2,128,1024]{3,2,1,0:T(8,128)(2,1)S(1)}, u32[]{:S(2)}, u32[]{:S(2)}) %collective-permute-start.6) | collective-permute-done | bytes 1048608 | tf_op jit(solution)/shard_map/ppermute | solution.py:249
  45.2 2.9 %collective-permute-done.5.refs_4_ = bf16[8,512,128]{2,1,0:T(8,128)(2,1)S(1)} collective-permute-done((bf16[8,512,128]{2,1,0:T(8,128)(2,1)S(1)}, bf16[8,512,128]{2,1,0:T(8,128)(2,1)S(1)}, u32[]{:S(2)}, u32[]{:S(2)}) %collective-permute-start.5) | collective-permute-done | bytes 1048608 | tf_op jit(solution)/shard_map/ppermute | solution.py:249
  48.2 0.1 collective-permute-start.14
  48.3 3.4 %collective-permute-start.10 = (bf16[4,512,128]{2,1,0:T(8,128)(2,1)S(1)}, bf16[4,512,128]{2,1,0:T(8,128)(2,1)S(1)}, u32[]{:S(2)}, u32[]{:S(2)}) collective-permute-start(bf16[4,512,128]{2,1,0:T(8,128)(2,1)S(1)} %slice.35), channel_id=1, source_target_pairs={{0,2},{2,4},{4,6},{6,0},{1,7},{3,1},{5,3},{7,5},{8,10},{10,12},{12... | collective-permute-start | bytes 1572872 | tf_op jit(solution)/shard_map/ppermute | solution.py:249
  51.8 2.0 %collective-permute-done.11.refs_9_ = bf16[4,512,128]{2,1,0:T(8,128)(2,1)S(1)} collective-permute-done((bf16[4,512,128]{2,1,0:T(8,128)(2,1)S(1)}, bf16[4,512,128]{2,1,0:T(8,128)(2,1)S(1)}, u32[]{:S(2)}, u32[]{:S(2)}) %collective-permute-start.11) | collective-permute-done | bytes 524320 | tf_op jit(solution)/shard_map/ppermute | solution.py:249
  53.8 0.1 collective-permute-start.16
  53.9 3.1 %collective-permute-start.13 = (bf16[2,128,1024]{2,1,0:T(8,128)(2,1)S(1)}, bf16[2,128,1024]{2,1,0:T(8,128)(2,1)S(1)}, u32[]{:S(2)}, u32[]{:S(2)}) collective-permute-start(bf16[2,128,1024]{2,1,0:T(8,128)(2,1)S(1)} %get-tuple-element.40), channel_id=1, source_target_pairs={{0,8},{8,16},{16,24},{24,0},{1,25},{9,1},{17,9},{25,17},{2,10},{10... | collective-permute-start | bytes 1572872 | tf_op jit(solution)/shard_map/ppermute | solution.py:249
  57.0 2.4 %collective-permute-done.10.refs_8_ = bf16[4,512,128]{2,1,0:T(8,128)(2,1)S(1)} collective-permute-done((bf16[4,512,128]{2,1,0:T(8,128)(2,1)S(1)}, bf16[4,512,128]{2,1,0:T(8,128)(2,1)S(1)}, u32[]{:S(2)}, u32[]{:S(2)}) %collective-permute-start.10) | collective-permute-done | bytes 524320 | tf_op jit(solution)/shard_map/ppermute | solution.py:249
  59.4 3.7 %collective-permute-done.13.fb = bf16[2,128,1024]{2,1,0:T(8,128)(2,1)S(1)} collective-permute-done((bf16[2,128,1024]{2,1,0:T(8,128)(2,1)S(1)}, bf16[2,128,1024]{2,1,0:T(8,128)(2,1)S(1)}, u32[]{:S(2)}, u32[]{:S(2)}) %collective-permute-start.13) | collective-permute-done | bytes 524320 | tf_op jit(solution)/shard_map/ppermute | solution.py:249
  63.2 1.6 %collective-permute-start.17 = (bf16[8,512,128]{2,1,0:T(8,128)(2,1)S(1)}, bf16[8,512,128]{2,1,0:T(8,128)(2,1)S(1)}, u32[]{:S(2)}, u32[]{:S(2)}) collective-permute-start(bf16[8,512,128]{2,1,0:T(8,128)(2,1)S(1)} %pad_maximum_fusion.4), channel_id=1, source_target_pairs={{0,1},{1,0},{2,3},{3,2},{4,5},{5,4},{6,7},{7,6},{8,9},{9,8},{10,11... | collective-permute-start | bytes 3145736 | tf_op jit(solution)/shard_map/ppermute | solution.py:244
  64.9 0.4 gather.1.refs_11_
  65.2 2.8 %blocks_2r0.2.refs_12_ = f32[512,1024]{1,0:T(8,128)S(1)} custom-call(bf16[4,512,128]{2,1,0:T(8,128)(2,1)S(1)} %collective-permute-done.refs_0_.refs_10_, bf16[4,512,128]{2,1,0:T(8,128)(2,1)S(1)} %collective-permute-done.1.refs_1_, bf16[4,512,128]{2,1,0:T(8,128)(2,1)S(1)} %collective-permute-done.4.refs_2_, ...), custom_call_target="tpu_custom_call" | custom-call | flops 2147483648 | bytes 5242880 | tf_op jit(solution)/shard_map/blocks_2r0/pallas_call | solution.py:199
  68.0 2.2 %blocks_2r0.3 = bf16[272,1024]{1,0:T(8,128)(2,1)S(1)} custom-call(bf16[4,512,128]{2,1,0:T(8,128)(2,1)S(1)} %collective-permute-done.refs_0_.refs_10_, bf16[4,512,128]{2,1,0:T(8,128)(2,1)S(1)} %collective-permute-done.1.refs_1_, bf16[4,512,128]{2,1,0:T(8,128)(2,1)S(1)} %collective-permute-done.4.refs_2_, ...), custom_call_target="tpu_custom_call" | custom-call | flops 2147483648 | bytes 5242880 | tf_op jit(solution)/shard_map/blocks_2r0/pallas_call | solution.py:199
  70.3 1.3 %collective-permute-start.22 = (bf16[272,1024]{1,0:T(8,128)(2,1)S(1)}, bf16[272,1024]{1,0:T(8,128)(2,1)S(1)}, u32[]{:S(2)}, u32[]{:S(2)}) collective-permute-start(bf16[272,1024]{1,0:T(8,128)(2,1)S(1)} %blocks_2r0.3), channel_id=1, source_target_pairs={{0,32},{32,64},{64,96},{96,0},{1,33},{33,65},{65,97},{97,1},{2,34}... | collective-permute-start | bytes 1671176 | tf_op jit(solution)/shard_map/ppermute | solution.py:244
  71.6 2.1 %blocks_2r272.1 = bf16[240,1024]{1,0:T(8,128)(2,1)S(1)} custom-call(bf16[4,512,128]{2,1,0:T(8,128)(2,1)S(1)} %collective-permute-done.refs_0_.refs_10_, bf16[4,512,128]{2,1,0:T(8,128)(2,1)S(1)} %collective-permute-done.1.refs_1_, bf16[4,512,128]{2,1,0:T(8,128)(2,1)S(1)} %collective-permute-done.4.refs_2_, ...), custom_call_target="tpu_custom_call" | custom-call | flops 2147483648 | bytes 5242880 | tf_op jit(solution)/shard_map/blocks_2r272/pallas_call | solution.py:199
  73.7 1.5 %collective-permute-start.19 = (bf16[240,1024]{1,0:T(8,128)(2,1)S(1)}, bf16[240,1024]{1,0:T(8,128)(2,1)S(1)}, u32[]{:S(2)}, u32[]{:S(2)}) collective-permute-start(bf16[240,1024]{1,0:T(8,128)(2,1)S(1)} %blocks_2r272.1), channel_id=1, source_target_pairs={{0,96},{32,0},{64,32},{96,64},{1,97},{33,1},{65,33},{97,65},{2,98}... | collective-permute-start | bytes 1474568 | tf_op jit(solution)/shard_map/ppermute | solution.py:244
  75.2 3.6 %blocks_1r272.1 = bf16[240,1024]{1,0:T(8,128)(2,1)S(1)} custom-call(bf16[4,512,128]{2,1,0:T(8,128)(2,1)S(1)} %collective-permute-done.refs_0_.refs_10_, bf16[4,512,128]{2,1,0:T(8,128)(2,1)S(1)} %collective-permute-done.1.refs_1_, bf16[4,512,128]{2,1,0:T(8,128)(2,1)S(1)} %collective-permute-done.4.refs_2_, ...), custom_call_target="tpu_custom_call" | custom-call | flops 2147483648 | bytes 5242880 | tf_op jit(solution)/shard_map/blocks_1r272/pallas_call | solution.py:199
  78.8 0.3 collective-permute-start.18
  79.1 3.7 %blocks_3r0.1 = bf16[272,1024]{1,0:T(8,128)(2,1)S(1)} custom-call(bf16[4,512,128]{2,1,0:T(8,128)(2,1)S(1)} %collective-permute-done.refs_0_.refs_10_, bf16[4,512,128]{2,1,0:T(8,128)(2,1)S(1)} %collective-permute-done.1.refs_1_, bf16[4,512,128]{2,1,0:T(8,128)(2,1)S(1)} %collective-permute-done.4.refs_2_, ...), custom_call_target="tpu_custom_call" | custom-call | flops 2147483648 | bytes 5242880 | tf_op jit(solution)/shard_map/blocks_3r0/pallas_call | solution.py:199
  82.8 2.5 %collective-permute-start.21 = (bf16[272,1024]{1,0:T(8,128)(2,1)S(1)}, bf16[272,1024]{1,0:T(8,128)(2,1)S(1)}, u32[]{:S(2)}, u32[]{:S(2)}) collective-permute-start(bf16[272,1024]{1,0:T(8,128)(2,1)S(1)} %blocks_3r0.1), channel_id=1, source_target_pairs={{0,96},{32,0},{64,32},{96,64},{1,97},{33,1},{65,33},{97,65},{2,98}... | collective-permute-start | bytes 1671176 | tf_op jit(solution)/shard_map/ppermute | solution.py:244
  85.3 0.4 collective-permute-done.22.refs_12_
  85.8 4.4 %blocks_1r0.1 = bf16[272,1024]{1,0:T(8,128)(2,1)S(1)} custom-call(bf16[4,512,128]{2,1,0:T(8,128)(2,1)S(1)} %collective-permute-done.refs_0_.refs_10_, bf16[4,512,128]{2,1,0:T(8,128)(2,1)S(1)} %collective-permute-done.1.refs_1_, bf16[4,512,128]{2,1,0:T(8,128)(2,1)S(1)} %collective-permute-done.4.refs_2_, ...), custom_call_target="tpu_custom_call" | custom-call | flops 2147483648 | bytes 5242880 | tf_op jit(solution)/shard_map/blocks_1r0/pallas_call | solution.py:199
  90.3 4.3 %blocks_3r272.1 = bf16[240,1024]{1,0:T(8,128)(2,1)S(1)} custom-call(bf16[4,512,128]{2,1,0:T(8,128)(2,1)S(1)} %collective-permute-done.refs_0_.refs_10_, bf16[4,512,128]{2,1,0:T(8,128)(2,1)S(1)} %collective-permute-done.1.refs_1_, bf16[4,512,128]{2,1,0:T(8,128)(2,1)S(1)} %collective-permute-done.4.refs_2_, ...), custom_call_target="tpu_custom_call" | custom-call | flops 2147483648 | bytes 5242880 | tf_op jit(solution)/shard_map/blocks_3r272/pallas_call | solution.py:199
  94.6 2.7 %collective-permute-start.20 = (bf16[240,1024]{1,0:T(8,128)(2,1)S(1)}, bf16[240,1024]{1,0:T(8,128)(2,1)S(1)}, u32[]{:S(2)}, u32[]{:S(2)}) collective-permute-start(bf16[240,1024]{1,0:T(8,128)(2,1)S(1)} %blocks_3r272.1), channel_id=1, source_target_pairs={{0,96},{32,0},{64,32},{96,64},{1,97},{33,1},{65,33},{97,65},{2,98}... | collective-permute-start | bytes 1474568 | tf_op jit(solution)/shard_map/ppermute | solution.py:244
  97.3 3.8 %blocks_0r272.1.own = f32[240,1024]{1,0:T(8,128)S(1)} custom-call(bf16[4,512,128]{2,1,0:T(8,128)(2,1)S(1)} %collective-permute-done.refs_0_.refs_10_, bf16[4,512,128]{2,1,0:T(8,128)(2,1)S(1)} %collective-permute-done.1.refs_1_, bf16[4,512,128]{2,1,0:T(8,128)(2,1)S(1)} %collective-permute-done.4.refs_2_, ...), custom_call_target="tpu_custom_call" | custom-call | flops 2147483648 | bytes 5242880 | tf_op jit(solution)/shard_map/blocks_0r272/pallas_call | solution.py:199
  101.1 3.9 %blocks_0r0.1.own = f32[272,1024]{1,0:T(8,128)S(1)} custom-call(bf16[4,512,128]{2,1,0:T(8,128)(2,1)S(1)} %collective-permute-done.refs_0_.refs_10_, bf16[4,512,128]{2,1,0:T(8,128)(2,1)S(1)} %collective-permute-done.1.refs_1_, bf16[4,512,128]{2,1,0:T(8,128)(2,1)S(1)} %collective-permute-done.4.refs_2_, ...), custom_call_target="tpu_custom_call" | custom-call | flops 2147483648 | bytes 5242880 | tf_op jit(solution)/shard_map/blocks_0r0/pallas_call | solution.py:199
  105.0 3.3 %collective-permute-done.23.p = bf16[272,1024]{1,0:T(8,128)(2,1)S(1)} collective-permute-done((bf16[272,1024]{1,0:T(8,128)(2,1)S(1)}, bf16[272,1024]{1,0:T(8,128)(2,1)S(1)}, u32[]{:S(2)}, u32[]{:S(2)}) %collective-permute-start.23) | collective-permute-done | bytes 557088 | tf_op jit(solution)/shard_map/ppermute | solution.py:244
  108.3 1.3 %final0.1.rest_0_ = f32[512,1024]{1,0:T(8,128)} custom-call(f32[272,1024]{1,0:T(8,128)S(1)} %blocks_0r0.1.own, bf16[272,1024]{1,0:T(8,128)(2,1)S(1)} %collective-permute-done.23.p), custom_call_target="tpu_custom_call" | custom-call | tf_op jit(solution)/shard_map/final0/pallas_call | solution.py:231
  109.6 1.3 %final1.1 = f32[512,1024]{1,0:T(8,128)} custom-call(f32[240,1024]{1,0:T(8,128)S(1)} %blocks_0r272.1.own, bf16[240,1024]{1,0:T(8,128)(2,1)S(1)} %collective-permute-done.20.p, f32[512,1024]{1,0:T(8,128)} %final0.1.rest_0_), custom_call_target="tpu_custom_call", output_to_operand_aliasing={{}: (2, {})} | custom-call | tf_op jit(solution)/shard_map/final1/pallas_call | solution.py:231
  (29 shorter events, 0.8 us)
Async XLA Ops:
  0.0 18.8 %copy-start = (bf16[4,128,1024]{2,1,0:T(8,128)(2,1)S(1)}, bf16[4,128,1024]{2,1,0:T(8,128)(2,1)}, u32[]{:S(2)}) copy-start(bf16[4,128,1024]{2,1,0:T(8,128)(2,1)} %g.1) | copy-start | bytes 3145732
  0.0 18.8 %collective-permute-start.2 = (bf16[4,128,1024]{2,1,0:T(8,128)(2,1)}, bf16[4,128,1024]{2,1,0:T(8,128)(2,1)S(1)}, u32[]{:S(2)}, u32[]{:S(2)}) collective-permute-start(bf16[4,128,1024]{2,1,0:T(8,128)(2,1)} %g.1), channel_id=1, source_target_pairs={{0,1},{1,0},{2,3},{3,2},{4,5},{5,4},{6,7},{7,6},{8,9},{9,8},{10,11... | collective-permute-start | bytes 3145736 | tf_op jit(solution)/shard_map/ppermute | solution.py:244
  1.4 1.2 %copy-start.1 = (bf16[4,128,1024]{2,1,0:T(8,128)(2,1)S(1)}, bf16[4,128,1024]{2,1,0:T(8,128)(2,1)}, u32[]{:S(2)}) copy-start(bf16[4,128,1024]{2,1,0:T(8,128)(2,1)} %a_ref.3) | copy-start | bytes 3145732
  3.1 15.7 %collective-permute-start.1 = (bf16[4,512,128]{2,1,0:T(8,128)(2,1)S(1)}, bf16[4,512,128]{2,1,0:T(8,128)(2,1)S(1)}, u32[]{:S(2)}, u32[]{:S(2)}) collective-permute-start(bf16[4,512,128]{2,1,0:T(8,128)(2,1)S(1)} %prep1.1.rest_0_), channel_id=1, source_target_pairs={{0,8},{1,25},{8,1},{9,16},{16,9},{17,24},{24,0},{25,17},{2,10},{3,... | collective-permute-start | bytes 1572872 | tf_op jit(solution)/shard_map/ppermute | solution.py:261
  7.5 14.7 %collective-permute-start = (bf16[4,512,128]{2,1,0:T(8,128)(2,1)S(1)}, bf16[4,512,128]{2,1,0:T(8,128)(2,1)S(1)}, u32[]{:S(2)}, u32[]{:S(2)}) collective-permute-start(bf16[4,512,128]{2,1,0:T(8,128)(2,1)S(1)} %prep0.1), channel_id=1, source_target_pairs={{0,0},{1,17},{8,9},{9,24},{16,1},{17,16},{24,8},{25,25},{2,2},{3,1... | collective-permute-start | bytes 1572872 | tf_op jit(solution)/shard_map/ppermute | solution.py:262
  18.8 3.5 %collective-permute-start.3 = (bf16[4,512,128]{2,1,0:T(8,128)(2,1)S(1)}, bf16[4,512,128]{2,1,0:T(8,128)(2,1)S(1)}, u32[]{:S(2)}, u32[]{:S(2)}) collective-permute-start(bf16[4,512,128]{2,1,0:T(8,128)(2,1)S(1)} %collective-permute-done.1.refs_1_), channel_id=1, source_target_pairs={{0,1},{1,0},{2,3},{3,2},{4,5},{5,4},{6,7},{7,6},{8,9},{9,8},{10,11... | collective-permute-start | bytes 1572872 | tf_op jit(solution)/shard_map/ppermute | solution.py:244
  19.1 14.9 %collective-permute-start.8 = (bf16[2,2,128,1024]{3,2,1,0:T(8,128)(2,1)S(1)}, bf16[2,2,128,1024]{3,2,1,0:T(8,128)(2,1)S(1)}, u32[]{:S(2)}, u32[]{:S(2)}) collective-permute-start(bf16[2,2,128,1024]{3,2,1,0:T(8,128)(2,1)S(1)} %pad_maximum_fusion.3), channel_id=1, source_target_pairs={{0,8},{8,16},{16,24},{24,0},{1,25},{9,1},{17,9},{25,17},{2,10},{10... | collective-permute-start | bytes 3145736 | tf_op jit(solution)/shard_map/ppermute | solution.py:249
  22.4 14.5 %collective-permute-start.7 = (bf16[8,512,128]{2,1,0:T(8,128)(2,1)S(1)}, bf16[8,512,128]{2,1,0:T(8,128)(2,1)S(1)}, u32[]{:S(2)}, u32[]{:S(2)}) collective-permute-start(bf16[8,512,128]{2,1,0:T(8,128)(2,1)S(1)} %pad_maximum_fusion.2), channel_id=1, source_target_pairs={{0,2},{2,4},{4,6},{6,0},{1,7},{3,1},{5,3},{7,5},{8,10},{10,12},{12... | collective-permute-start | bytes 3145736 | tf_op jit(solution)/shard_map/ppermute | solution.py:249
  25.2 1.9 %collective-permute-start.4 = (bf16[4,512,128]{2,1,0:T(8,128)(2,1)S(1)}, bf16[4,512,128]{2,1,0:T(8,128)(2,1)S(1)}, u32[]{:S(2)}, u32[]{:S(2)}) collective-permute-start(bf16[4,512,128]{2,1,0:T(8,128)(2,1)S(1)} %collective-permute-done.refs_0_.refs_10_), channel_id=1, source_target_pairs={{0,1},{1,0},{2,3},{3,2},{4,5},{5,4},{6,7},{7,6},{8,9},{9,8},{10,11... | collective-permute-start | bytes 1572872 | tf_op jit(solution)/shard_map/ppermute | solution.py:244
  25.3 20.0 %collective-permute-start.6 = (bf16[2,2,128,1024]{3,2,1,0:T(8,128)(2,1)S(1)}, bf16[2,2,128,1024]{3,2,1,0:T(8,128)(2,1)S(1)}, u32[]{:S(2)}, u32[]{:S(2)}) collective-permute-start(bf16[2,2,128,1024]{3,2,1,0:T(8,128)(2,1)S(1)} %pad_maximum_fusion.1), channel_id=1, source_target_pairs={{0,8},{8,16},{16,24},{24,0},{1,25},{9,1},{17,9},{25,17},{2,10},{10... | collective-permute-start | bytes 3145736 | tf_op jit(solution)/shard_map/ppermute | solution.py:249
  27.2 21.0 %collective-permute-start.5 = (bf16[8,512,128]{2,1,0:T(8,128)(2,1)S(1)}, bf16[8,512,128]{2,1,0:T(8,128)(2,1)S(1)}, u32[]{:S(2)}, u32[]{:S(2)}) collective-permute-start(bf16[8,512,128]{2,1,0:T(8,128)(2,1)S(1)} %pad_maximum_fusion), channel_id=1, source_target_pairs={{0,2},{2,4},{4,6},{6,0},{1,7},{3,1},{5,3},{7,5},{8,10},{10,12},{12... | collective-permute-start | bytes 3145736 | tf_op jit(solution)/shard_map/ppermute | solution.py:249
  36.9 11.2 %collective-permute-start.9 = (bf16[8,512,128]{2,1,0:T(8,128)(2,1)S(1)}, bf16[8,512,128]{2,1,0:T(8,128)(2,1)S(1)}, u32[]{:S(2)}, u32[]{:S(2)}) collective-permute-start(bf16[8,512,128]{2,1,0:T(8,128)(2,1)S(1)} %collective-permute-done.7.refs_5_), channel_id=1, source_target_pairs={{0,1},{1,0},{2,3},{3,2},{4,5},{5,4},{6,7},{7,6},{8,9},{9,8},{10,11... | collective-permute-start | bytes 3145736 | tf_op jit(solution)/shard_map/ppermute | solution.py:244
  37.1 16.7 %collective-permute-start.11 = (bf16[4,512,128]{2,1,0:T(8,128)(2,1)S(1)}, bf16[4,512,128]{2,1,0:T(8,128)(2,1)S(1)}, u32[]{:S(2)}, u32[]{:S(2)}) collective-permute-start(bf16[4,512,128]{2,1,0:T(8,128)(2,1)S(1)} %slice.36), channel_id=1, source_target_pairs={{0,2},{2,4},{4,6},{6,0},{1,7},{3,1},{5,3},{7,5},{8,10},{10,12},{12... | collective-permute-start | bytes 1572872 | tf_op jit(solution)/shard_map/ppermute | solution.py:249
  40.5 13.4 %collective-permute-start.12 = (bf16[2,128,1024]{2,1,0:T(8,128)(2,1)S(1)}, bf16[2,128,1024]{2,1,0:T(8,128)(2,1)S(1)}, u32[]{:S(2)}, u32[]{:S(2)}) collective-permute-start(bf16[2,128,1024]{2,1,0:T(8,128)(2,1)S(1)} %get-tuple-element.41), channel_id=1, source_target_pairs={{0,8},{8,16},{16,24},{24,0},{1,25},{9,1},{17,9},{25,17},{2,10},{10... | collective-permute-start | bytes 1572872 | tf_op jit(solution)/shard_map/ppermute | solution.py:249
  48.2 15.0 %collective-permute-start.14 = (bf16[8,512,128]{2,1,0:T(8,128)(2,1)S(1)}, bf16[8,512,128]{2,1,0:T(8,128)(2,1)S(1)}, u32[]{:S(2)}, u32[]{:S(2)}) collective-permute-start(bf16[8,512,128]{2,1,0:T(8,128)(2,1)S(1)} %collective-permute-done.5.refs_4_), channel_id=1, source_target_pairs={{0,1},{1,0},{2,3},{3,2},{4,5},{5,4},{6,7},{7,6},{8,9},{9,8},{10,11... | collective-permute-start | bytes 3145736 | tf_op jit(solution)/shard_map/ppermute | solution.py:244
  48.3 11.1 %collective-permute-start.10 = (bf16[4,512,128]{2,1,0:T(8,128)(2,1)S(1)}, bf16[4,512,128]{2,1,0:T(8,128)(2,1)S(1)}, u32[]{:S(2)}, u32[]{:S(2)}) collective-permute-start(bf16[4,512,128]{2,1,0:T(8,128)(2,1)S(1)} %slice.35), channel_id=1, source_target_pairs={{0,2},{2,4},{4,6},{6,0},{1,7},{3,1},{5,3},{7,5},{8,10},{10,12},{12... | collective-permute-start | bytes 1572872 | tf_op jit(solution)/shard_map/ppermute | solution.py:249
  51.7 7.7 %collective-permute-start.15 = (bf16[2,128,1024]{2,1,0:T(8,128)(2,1)S(1)}, bf16[2,128,1024]{2,1,0:T(8,128)(2,1)S(1)}, u32[]{:S(2)}, u32[]{:S(2)}) collective-permute-start(bf16[2,128,1024]{2,1,0:T(8,128)(2,1)S(1)} %get-tuple-element.30), channel_id=1, source_target_pairs={{0,1},{1,0},{2,3},{3,2},{4,5},{5,4},{6,7},{7,6},{8,9},{9,8},{10,11... | collective-permute-start | bytes 1572872 | tf_op jit(solution)/shard_map/ppermute | solution.py:244
  53.8 5.6 %collective-permute-start.16 = (bf16[2,128,1024]{2,1,0:T(8,128)(2,1)S(1)}, bf16[2,128,1024]{2,1,0:T(8,128)(2,1)S(1)}, u32[]{:S(2)}, u32[]{:S(2)}) collective-permute-start(bf16[2,128,1024]{2,1,0:T(8,128)(2,1)S(1)} %get-tuple-element.39), channel_id=1, source_target_pairs={{0,1},{1,0},{2,3},{3,2},{4,5},{5,4},{6,7},{7,6},{8,9},{9,8},{10,11... | collective-permute-start | bytes 1572872 | tf_op jit(solution)/shard_map/ppermute | solution.py:244
  53.9 9.2 %collective-permute-start.13 = (bf16[2,128,1024]{2,1,0:T(8,128)(2,1)S(1)}, bf16[2,128,1024]{2,1,0:T(8,128)(2,1)S(1)}, u32[]{:S(2)}, u32[]{:S(2)}) collective-permute-start(bf16[2,128,1024]{2,1,0:T(8,128)(2,1)S(1)} %get-tuple-element.40), channel_id=1, source_target_pairs={{0,8},{8,16},{16,24},{24,0},{1,25},{9,1},{17,9},{25,17},{2,10},{10... | collective-permute-start | bytes 1572872 | tf_op jit(solution)/shard_map/ppermute | solution.py:249
  63.2 4.8 %collective-permute-start.17 = (bf16[8,512,128]{2,1,0:T(8,128)(2,1)S(1)}, bf16[8,512,128]{2,1,0:T(8,128)(2,1)S(1)}, u32[]{:S(2)}, u32[]{:S(2)}) collective-permute-start(bf16[8,512,128]{2,1,0:T(8,128)(2,1)S(1)} %pad_maximum_fusion.4), channel_id=1, source_target_pairs={{0,1},{1,0},{2,3},{3,2},{4,5},{5,4},{6,7},{7,6},{8,9},{9,8},{10,11... | collective-permute-start | bytes 3145736 | tf_op jit(solution)/shard_map/ppermute | solution.py:244
  70.3 15.5 %collective-permute-start.22 = (bf16[272,1024]{1,0:T(8,128)(2,1)S(1)}, bf16[272,1024]{1,0:T(8,128)(2,1)S(1)}, u32[]{:S(2)}, u32[]{:S(2)}) collective-permute-start(bf16[272,1024]{1,0:T(8,128)(2,1)S(1)} %blocks_2r0.3), channel_id=1, source_target_pairs={{0,32},{32,64},{64,96},{96,0},{1,33},{33,65},{65,97},{97,1},{2,34}... | collective-permute-start | bytes 1671176 | tf_op jit(solution)/shard_map/ppermute | solution.py:244
  73.7 16.6 %collective-permute-start.19 = (bf16[240,1024]{1,0:T(8,128)(2,1)S(1)}, bf16[240,1024]{1,0:T(8,128)(2,1)S(1)}, u32[]{:S(2)}, u32[]{:S(2)}) collective-permute-start(bf16[240,1024]{1,0:T(8,128)(2,1)S(1)} %blocks_2r272.1), channel_id=1, source_target_pairs={{0,96},{32,0},{64,32},{96,64},{1,97},{33,1},{65,33},{97,65},{2,98}... | collective-permute-start | bytes 1474568 | tf_op jit(solution)/shard_map/ppermute | solution.py:244
  78.8 18.5 %collective-permute-start.18 = (bf16[240,1024]{1,0:T(8,128)(2,1)S(1)}, bf16[240,1024]{1,0:T(8,128)(2,1)S(1)}, u32[]{:S(2)}, u32[]{:S(2)}) collective-permute-start(bf16[240,1024]{1,0:T(8,128)(2,1)S(1)} %blocks_1r272.1), channel_id=1, source_target_pairs={{0,32},{32,64},{64,96},{96,0},{1,33},{33,65},{65,97},{97,1},{2,34}... | collective-permute-start | bytes 1474568 | tf_op jit(solution)/shard_map/ppermute | solution.py:244
  82.8 18.3 %collective-permute-start.21 = (bf16[272,1024]{1,0:T(8,128)(2,1)S(1)}, bf16[272,1024]{1,0:T(8,128)(2,1)S(1)}, u32[]{:S(2)}, u32[]{:S(2)}) collective-permute-start(bf16[272,1024]{1,0:T(8,128)(2,1)S(1)} %blocks_3r0.1), channel_id=1, source_target_pairs={{0,96},{32,0},{64,32},{96,64},{1,97},{33,1},{65,33},{97,65},{2,98}... | collective-permute-start | bytes 1671176 | tf_op jit(solution)/shard_map/ppermute | solution.py:244
  90.2 18.1 %collective-permute-start.23 = (bf16[272,1024]{1,0:T(8,128)(2,1)S(1)}, bf16[272,1024]{1,0:T(8,128)(2,1)S(1)}, u32[]{:S(2)}, u32[]{:S(2)}) collective-permute-start(bf16[272,1024]{1,0:T(8,128)(2,1)S(1)} %blocks_1r0.1), channel_id=1, source_target_pairs={{0,32},{32,64},{64,96},{96,0},{1,33},{33,65},{65,97},{97,1},{2,34}... | collective-permute-start | bytes 1671176 | tf_op jit(solution)/shard_map/ppermute | solution.py:244
  94.6 15.0 %collective-permute-start.20 = (bf16[240,1024]{1,0:T(8,128)(2,1)S(1)}, bf16[240,1024]{1,0:T(8,128)(2,1)S(1)}, u32[]{:S(2)}, u32[]{:S(2)}) collective-permute-start(bf16[240,1024]{1,0:T(8,128)(2,1)S(1)} %blocks_3r272.1), channel_id=1, source_target_pairs={{0,96},{32,0},{64,32},{96,64},{1,97},{33,1},{65,33},{97,65},{2,98}... | collective-permute-start | bytes 1474568 | tf_op jit(solution)/shard_map/ppermute | solution.py:244

commit v6 on v5

--- a/solution.py
+++ b/solution.py
@@ -273,7 +273,7 @@
     m0, zb, m1c, zah = hold((m0, zb, m1c, za[1]))
     f0, fb, m0c = both_ways(m0[:4], "y"), both_ways(zb[0], "z"), cross(m0)
     zac, zbc = cross(zah), cross(zb[1])
-    f0, f1, fa, fb, m0c, zac, zbc = hold((f0, f1, fa, fb, m0c, zac, zbc))
+    f0, f1, fa, fb, m0c = hold((f0, f1, fa, fb, m0c))
     fc = cross(jnp.concatenate([f0, f1]))
     gs = gather(g, za, zb, zac, zbc, fa, fb)
     a_refs = (r0, r1, r0c, r1c, m0, m1, m0c, m1c, f0, f1, fc)

time: 111 us -> 116 us (1.045)
  waiting for transfers between devices: 35.7 us -> 46.1 us
  starting transfers between devices: 38.2 us -> 32 us
    ppermute x8, waiting for transfers between devices: 23.6 us -> 31.1 us  [both_ways(): return lax.ppermute(v, (axis, 'c'), pairs)]
    ppermute x8, starting transfers between devices: 19.4 us -> 14 us  [both_ways(): return lax.ppermute(v, (axis, 'c'), pairs)]
    ppermute x14, waiting for transfers between devices: 3.94 us -> 6.81 us  [send(): return lax.ppermute(v, axis, ring(2 if axis == 'c' else 4, step))]
  transfers between devices with their start and end apart: 24 -> 24, of which waited for: 11 -> 14; matrix products, arithmetic and copies ran while one was open for 1% -> 1% of each run, Pallas kernels for 28% -> 27%
where the time goes in v6:
time: 116 us; the launch traced here: 115 us
  waiting for transfers between devices  46.1 us (40%)
  Pallas kernels  34.7 us (30%)
  starting transfers between devices  32 us (28%)
  local copies, waits for them, and re-layouts  1.59 us (1%)
    ppermute x8, waiting for transfers between devices, both_ways(): return lax.ppermute(v, (axis, 'c'), pairs)  31.1 us
    pallas_call x9, Pallas kernels, blocks(): pl.pallas_call(functools.partial(blocks_kernel, jobs, len(extra)), out_sh...  30.8 us
    ppermute x8, starting transfers between devices, both_ways(): return lax.ppermute(v, (axis, 'c'), pairs)  14 us
    ppermute x14, starting transfers between devices, send(): return lax.ppermute(v, axis, ring(2 if axis == 'c' else 4, step))  11 us
    ppermute x1, waiting for transfers between devices, body(): r1 = lax.ppermute(p1, ('z', 'c'), round_pairs(1))  8.19 us
    ppermute x14, waiting for transfers between devices, send(): return lax.ppermute(v, axis, ring(2 if axis == 'c' else 4, step))  6.81 us
    ppermute x1, starting transfers between devices, body(): r1 = lax.ppermute(p1, ('z', 'c'), round_pairs(1))  3.92 us
    ppermute x1, starting transfers between devices, body(): r0 = lax.ppermute(p0, ('z', 'c'), round_pairs(0))  3.07 us
  transfers between devices with their start and end apart: 24, of which 14 were waited for; matrix products, arithmetic and copies ran while one was open for 1% of the time, Pallas kernels for 27%

profile of v6, /device:TPU:1, one launch (start us, length us, event | category | flops | bytes accessed | tf_op | source)
XLA Modules:
  0.0 115.3 jit_solution(6991441642577320022)
XLA Ops:
  0.0 1.4 %collective-permute-start.2 = (bf16[4,128,1024]{2,1,0:T(8,128)(2,1)}, bf16[4,128,1024]{2,1,0:T(8,128)(2,1)S(1)}, u32[]{:S(2)}, u32[]{:S(2)}) collective-permute-start(bf16[4,128,1024]{2,1,0:T(8,128)(2,1)} %g.1), channel_id=1, source_target_pairs={{0,1},{1,0},{2,3},{3,2},{4,5},{5,4},{6,7},{7,6},{8,9},{9,8},{10,11... | collective-permute-start | bytes 3145736 | tf_op jit(solution)/shard_map/ppermute | solution.py:244
  1.4 1.2 %copy-done.1 = bf16[4,128,1024]{2,1,0:T(8,128)(2,1)S(1)} copy-done((bf16[4,128,1024]{2,1,0:T(8,128)(2,1)S(1)}, bf16[4,128,1024]{2,1,0:T(8,128)(2,1)}, u32[]{:S(2)}) %copy-start.1) | copy-done | bytes 1048600
  2.6 0.5 prep1.1.rest_0_
  3.1 3.9 %collective-permute-start.1 = (bf16[4,512,128]{2,1,0:T(8,128)(2,1)S(1)}, bf16[4,512,128]{2,1,0:T(8,128)(2,1)S(1)}, u32[]{:S(2)}, u32[]{:S(2)}) collective-permute-start(bf16[4,512,128]{2,1,0:T(8,128)(2,1)S(1)} %prep1.1.rest_0_), channel_id=1, source_target_pairs={{0,8},{1,25},{8,1},{9,16},{16,9},{17,24},{24,0},{25,17},{2,10},{3,... | collective-permute-start | bytes 1572872 | tf_op jit(solution)/shard_map/ppermute | solution.py:261
  7.0 0.5 prep0.1
  7.5 3.1 %collective-permute-start = (bf16[4,512,128]{2,1,0:T(8,128)(2,1)S(1)}, bf16[4,512,128]{2,1,0:T(8,128)(2,1)S(1)}, u32[]{:S(2)}, u32[]{:S(2)}) collective-permute-start(bf16[4,512,128]{2,1,0:T(8,128)(2,1)S(1)} %prep0.1), channel_id=1, source_target_pairs={{0,0},{1,17},{8,9},{9,24},{16,1},{17,16},{24,8},{25,25},{2,2},{3,1... | collective-permute-start | bytes 1572872 | tf_op jit(solution)/shard_map/ppermute | solution.py:262
  10.6 8.2 %collective-permute-done.1.refs_1_ = bf16[4,512,128]{2,1,0:T(8,128)(2,1)S(1)} collective-permute-done((bf16[4,512,128]{2,1,0:T(8,128)(2,1)S(1)}, bf16[4,512,128]{2,1,0:T(8,128)(2,1)S(1)}, u32[]{:S(2)}, u32[]{:S(2)}) %collective-permute-start.1) | collective-permute-done | bytes 524320 | tf_op jit(solution)/shard_map/ppermute | solution.py:261
  19.1 3.2 %collective-permute-start.8 = (bf16[2,2,128,1024]{3,2,1,0:T(8,128)(2,1)S(1)}, bf16[2,2,128,1024]{3,2,1,0:T(8,128)(2,1)S(1)}, u32[]{:S(2)}, u32[]{:S(2)}) collective-permute-start(bf16[2,2,128,1024]{3,2,1,0:T(8,128)(2,1)S(1)} %pad_maximum_fusion.3), channel_id=1, source_target_pairs={{0,8},{8,16},{16,24},{24,0},{1,25},{9,1},{17,9},{25,17},{2,10},{10... | collective-permute-start | bytes 3145736 | tf_op jit(solution)/shard_map/ppermute | solution.py:249
  22.4 2.8 %collective-permute-start.7 = (bf16[8,512,128]{2,1,0:T(8,128)(2,1)S(1)}, bf16[8,512,128]{2,1,0:T(8,128)(2,1)S(1)}, u32[]{:S(2)}, u32[]{:S(2)}) collective-permute-start(bf16[8,512,128]{2,1,0:T(8,128)(2,1)S(1)} %pad_maximum_fusion.2), channel_id=1, source_target_pairs={{0,2},{2,4},{4,6},{6,0},{1,7},{3,1},{5,3},{7,5},{8,10},{10,12},{12... | collective-permute-start | bytes 3145736 | tf_op jit(solution)/shard_map/ppermute | solution.py:249
  25.3 1.6 %collective-permute-start.6 = (bf16[2,2,128,1024]{3,2,1,0:T(8,128)(2,1)S(1)}, bf16[2,2,128,1024]{3,2,1,0:T(8,128)(2,1)S(1)}, u32[]{:S(2)}, u32[]{:S(2)}) collective-permute-start(bf16[2,2,128,1024]{3,2,1,0:T(8,128)(2,1)S(1)} %pad_maximum_fusion.1), channel_id=1, source_target_pairs={{0,8},{8,16},{16,24},{24,0},{1,25},{9,1},{17,9},{25,17},{2,10},{10... | collective-permute-start | bytes 3145736 | tf_op jit(solution)/shard_map/ppermute | solution.py:249
  26.9 0.2 collective-permute-done.4.refs_2_
  27.2 0.5 collective-permute-start.5
  27.7 6.3 %collective-permute-done.8.za = bf16[2,2,128,1024]{3,2,1,0:T(8,128)(2,1)S(1)} collective-permute-done((bf16[2,2,128,1024]{3,2,1,0:T(8,128)(2,1)S(1)}, bf16[2,2,128,1024]{3,2,1,0:T(8,128)(2,1)S(1)}, u32[]{:S(2)}, u32[]{:S(2)}) %collective-permute-start.8) | collective-permute-done | bytes 1048608 | tf_op jit(solution)/shard_map/ppermute | solution.py:249
  34.0 2.9 %collective-permute-done.7.refs_5_ = bf16[8,512,128]{2,1,0:T(8,128)(2,1)S(1)} collective-permute-done((bf16[8,512,128]{2,1,0:T(8,128)(2,1)S(1)}, bf16[8,512,128]{2,1,0:T(8,128)(2,1)S(1)}, u32[]{:S(2)}, u32[]{:S(2)}) %collective-permute-start.7) | collective-permute-done | bytes 1048608 | tf_op jit(solution)/shard_map/ppermute | solution.py:249
  37.1 8.1 %collective-permute-done.6.zb = bf16[2,2,128,1024]{3,2,1,0:T(8,128)(2,1)S(1)} collective-permute-done((bf16[2,2,128,1024]{3,2,1,0:T(8,128)(2,1)S(1)}, bf16[2,2,128,1024]{3,2,1,0:T(8,128)(2,1)S(1)}, u32[]{:S(2)}, u32[]{:S(2)}) %collective-permute-start.6) | collective-permute-done | bytes 1048608 | tf_op jit(solution)/shard_map/ppermute | solution.py:249
  45.2 2.9 %collective-permute-done.5.refs_4_ = bf16[8,512,128]{2,1,0:T(8,128)(2,1)S(1)} collective-permute-done((bf16[8,512,128]{2,1,0:T(8,128)(2,1)S(1)}, bf16[8,512,128]{2,1,0:T(8,128)(2,1)S(1)}, u32[]{:S(2)}, u32[]{:S(2)}) %collective-permute-start.5) | collective-permute-done | bytes 1048608 | tf_op jit(solution)/shard_map/ppermute | solution.py:249
  48.2 0.1 collective-permute-start.14
  48.3 3.1 %collective-permute-start.11 = (bf16[4,512,128]{2,1,0:T(8,128)(2,1)S(1)}, bf16[4,512,128]{2,1,0:T(8,128)(2,1)S(1)}, u32[]{:S(2)}, u32[]{:S(2)}) collective-permute-start(bf16[4,512,128]{2,1,0:T(8,128)(2,1)S(1)} %slice.36), channel_id=1, source_target_pairs={{0,2},{2,4},{4,6},{6,0},{1,7},{3,1},{5,3},{7,5},{8,10},{10,12},{12... | collective-permute-start | bytes 1572872 | tf_op jit(solution)/shard_map/ppermute | solution.py:249
  51.4 1.6 %collective-permute-start.12 = (bf16[2,128,1024]{2,1,0:T(8,128)(2,1)S(1)}, bf16[2,128,1024]{2,1,0:T(8,128)(2,1)S(1)}, u32[]{:S(2)}, u32[]{:S(2)}) collective-permute-start(bf16[2,128,1024]{2,1,0:T(8,128)(2,1)S(1)} %get-tuple-element.37), channel_id=1, source_target_pairs={{0,8},{8,16},{16,24},{24,0},{1,25},{9,1},{17,9},{25,17},{2,10},{10... | collective-permute-start | bytes 1572872 | tf_op jit(solution)/shard_map/ppermute | solution.py:249
  53.0 0.5 collective-permute-start.10
  53.6 0.6 collective-permute-start.13
  54.3 3.2 %collective-permute-done.11.refs_9_ = bf16[4,512,128]{2,1,0:T(8,128)(2,1)S(1)} collective-permute-done((bf16[4,512,128]{2,1,0:T(8,128)(2,1)S(1)}, bf16[4,512,128]{2,1,0:T(8,128)(2,1)S(1)}, u32[]{:S(2)}, u32[]{:S(2)}) %collective-permute-start.11) | collective-permute-done | bytes 524320 | tf_op jit(solution)/shard_map/ppermute | solution.py:249
  57.5 2.2 %collective-permute-done.12.fa = bf16[2,128,1024]{2,1,0:T(8,128)(2,1)S(1)} collective-permute-done((bf16[2,128,1024]{2,1,0:T(8,128)(2,1)S(1)}, bf16[2,128,1024]{2,1,0:T(8,128)(2,1)S(1)}, u32[]{:S(2)}, u32[]{:S(2)}) %collective-permute-start.12) | collective-permute-done | bytes 524320 | tf_op jit(solution)/shard_map/ppermute | solution.py:249
  59.7 3.4 %collective-permute-done.10.refs_8_ = bf16[4,512,128]{2,1,0:T(8,128)(2,1)S(1)} collective-permute-done((bf16[4,512,128]{2,1,0:T(8,128)(2,1)S(1)}, bf16[4,512,128]{2,1,0:T(8,128)(2,1)S(1)}, u32[]{:S(2)}, u32[]{:S(2)}) %collective-permute-start.10) | collective-permute-done | bytes 524320 | tf_op jit(solution)/shard_map/ppermute | solution.py:249
  63.1 2.0 %collective-permute-done.13.fb = bf16[2,128,1024]{2,1,0:T(8,128)(2,1)S(1)} collective-permute-done((bf16[2,128,1024]{2,1,0:T(8,128)(2,1)S(1)}, bf16[2,128,1024]{2,1,0:T(8,128)(2,1)S(1)}, u32[]{:S(2)}, u32[]{:S(2)}) %collective-permute-start.13) | collective-permute-done | bytes 524320 | tf_op jit(solution)/shard_map/ppermute | solution.py:249
  65.2 0.5 collective-permute-start.15
  65.7 0.1 collective-permute-start.16
  65.8 0.4 collective-permute-start.17
  66.2 2.5 %collective-permute-done.16.zac = bf16[2,128,1024]{2,1,0:T(8,128)(2,1)S(1)} collective-permute-done((bf16[2,128,1024]{2,1,0:T(8,128)(2,1)S(1)}, bf16[2,128,1024]{2,1,0:T(8,128)(2,1)S(1)}, u32[]{:S(2)}, u32[]{:S(2)}) %collective-permute-start.16) | collective-permute-done | bytes 524320 | tf_op jit(solution)/shard_map/ppermute | solution.py:244
  68.7 0.7 collective-permute-done.17.zbc
  69.5 0.4 gather.1.refs_11_
  69.9 2.8 %blocks_2r0.2.refs_12_ = f32[512,1024]{1,0:T(8,128)S(1)} custom-call(bf16[4,512,128]{2,1,0:T(8,128)(2,1)S(1)} %collective-permute-done.refs_0_.refs_10_, bf16[4,512,128]{2,1,0:T(8,128)(2,1)S(1)} %collective-permute-done.1.refs_1_, bf16[4,512,128]{2,1,0:T(8,128)(2,1)S(1)} %collective-permute-done.4.refs_2_, ...), custom_call_target="tpu_custom_call" | custom-call | flops 2147483648 | bytes 5242880 | tf_op jit(solution)/shard_map/blocks_2r0/pallas_call | solution.py:199
  72.7 2.2 %blocks_2r0.3 = bf16[272,1024]{1,0:T(8,128)(2,1)S(1)} custom-call(bf16[4,512,128]{2,1,0:T(8,128)(2,1)S(1)} %collective-permute-done.refs_0_.refs_10_, bf16[4,512,128]{2,1,0:T(8,128)(2,1)S(1)} %collective-permute-done.1.refs_1_, bf16[4,512,128]{2,1,0:T(8,128)(2,1)S(1)} %collective-permute-done.4.refs_2_, ...), custom_call_target="tpu_custom_call" | custom-call | flops 2147483648 | bytes 5242880 | tf_op jit(solution)/shard_map/blocks_2r0/pallas_call | solution.py:199
  74.9 1.3 %collective-permute-start.22 = (bf16[272,1024]{1,0:T(8,128)(2,1)S(1)}, bf16[272,1024]{1,0:T(8,128)(2,1)S(1)}, u32[]{:S(2)}, u32[]{:S(2)}) collective-permute-start(bf16[272,1024]{1,0:T(8,128)(2,1)S(1)} %blocks_2r0.3), channel_id=1, source_target_pairs={{0,32},{32,64},{64,96},{96,0},{1,33},{33,65},{65,97},{97,1},{2,34}... | collective-permute-start | bytes 1671176 | tf_op jit(solution)/shard_map/ppermute | solution.py:244
  76.2 2.1 %blocks_2r272.1 = bf16[240,1024]{1,0:T(8,128)(2,1)S(1)} custom-call(bf16[4,512,128]{2,1,0:T(8,128)(2,1)S(1)} %collective-permute-done.refs_0_.refs_10_, bf16[4,512,128]{2,1,0:T(8,128)(2,1)S(1)} %collective-permute-done.1.refs_1_, bf16[4,512,128]{2,1,0:T(8,128)(2,1)S(1)} %collective-permute-done.4.refs_2_, ...), custom_call_target="tpu_custom_call" | custom-call | flops 2147483648 | bytes 5242880 | tf_op jit(solution)/shard_map/blocks_2r272/pallas_call | solution.py:199
  78.3 1.5 %collective-permute-start.19 = (bf16[240,1024]{1,0:T(8,128)(2,1)S(1)}, bf16[240,1024]{1,0:T(8,128)(2,1)S(1)}, u32[]{:S(2)}, u32[]{:S(2)}) collective-permute-start(bf16[240,1024]{1,0:T(8,128)(2,1)S(1)} %blocks_2r272.1), channel_id=1, source_target_pairs={{0,96},{32,0},{64,32},{96,64},{1,97},{33,1},{65,33},{97,65},{2,98}... | collective-permute-start | bytes 1474568 | tf_op jit(solution)/shard_map/ppermute | solution.py:244
  79.8 3.6 %blocks_1r272.1 = bf16[240,1024]{1,0:T(8,128)(2,1)S(1)} custom-call(bf16[4,512,128]{2,1,0:T(8,128)(2,1)S(1)} %collective-permute-done.refs_0_.refs_10_, bf16[4,512,128]{2,1,0:T(8,128)(2,1)S(1)} %collective-permute-done.1.refs_1_, bf16[4,512,128]{2,1,0:T(8,128)(2,1)S(1)} %collective-permute-done.4.refs_2_, ...), custom_call_target="tpu_custom_call" | custom-call | flops 2147483648 | bytes 5242880 | tf_op jit(solution)/shard_map/blocks_1r272/pallas_call | solution.py:199
  83.4 0.3 collective-permute-start.18
  83.7 3.7 %blocks_3r0.1 = bf16[272,1024]{1,0:T(8,128)(2,1)S(1)} custom-call(bf16[4,512,128]{2,1,0:T(8,128)(2,1)S(1)} %collective-permute-done.refs_0_.refs_10_, bf16[4,512,128]{2,1,0:T(8,128)(2,1)S(1)} %collective-permute-done.1.refs_1_, bf16[4,512,128]{2,1,0:T(8,128)(2,1)S(1)} %collective-permute-done.4.refs_2_, ...), custom_call_target="tpu_custom_call" | custom-call | flops 2147483648 | bytes 5242880 | tf_op jit(solution)/shard_map/blocks_3r0/pallas_call | solution.py:199
  87.4 2.5 %collective-permute-start.21 = (bf16[272,1024]{1,0:T(8,128)(2,1)S(1)}, bf16[272,1024]{1,0:T(8,128)(2,1)S(1)}, u32[]{:S(2)}, u32[]{:S(2)}) collective-permute-start(bf16[272,1024]{1,0:T(8,128)(2,1)S(1)} %blocks_3r0.1), channel_id=1, source_target_pairs={{0,96},{32,0},{64,32},{96,64},{1,97},{33,1},{65,33},{97,65},{2,98}... | collective-permute-start | bytes 1671176 | tf_op jit(solution)/shard_map/ppermute | solution.py:244
  90.0 4.4 %blocks_1r0.1 = bf16[272,1024]{1,0:T(8,128)(2,1)S(1)} custom-call(bf16[4,512,128]{2,1,0:T(8,128)(2,1)S(1)} %collective-permute-done.refs_0_.refs_10_, bf16[4,512,128]{2,1,0:T(8,128)(2,1)S(1)} %collective-permute-done.1.refs_1_, bf16[4,512,128]{2,1,0:T(8,128)(2,1)S(1)} %collective-permute-done.4.refs_2_, ...), custom_call_target="tpu_custom_call" | custom-call | flops 2147483648 | bytes 5242880 | tf_op jit(solution)/shard_map/blocks_1r0/pallas_call | solution.py:199
  94.5 4.3 %blocks_3r272.1 = bf16[240,1024]{1,0:T(8,128)(2,1)S(1)} custom-call(bf16[4,512,128]{2,1,0:T(8,128)(2,1)S(1)} %collective-permute-done.refs_0_.refs_10_, bf16[4,512,128]{2,1,0:T(8,128)(2,1)S(1)} %collective-permute-done.1.refs_1_, bf16[4,512,128]{2,1,0:T(8,128)(2,1)S(1)} %collective-permute-done.4.refs_2_, ...), custom_call_target="tpu_custom_call" | custom-call | flops 2147483648 | bytes 5242880 | tf_op jit(solution)/shard_map/blocks_3r272/pallas_call | solution.py:199
  98.8 2.7 %collective-permute-start.20 = (bf16[240,1024]{1,0:T(8,128)(2,1)S(1)}, bf16[240,1024]{1,0:T(8,128)(2,1)S(1)}, u32[]{:S(2)}, u32[]{:S(2)}) collective-permute-start(bf16[240,1024]{1,0:T(8,128)(2,1)S(1)} %blocks_3r272.1), channel_id=1, source_target_pairs={{0,96},{32,0},{64,32},{96,64},{1,97},{33,1},{65,33},{97,65},{2,98}... | collective-permute-start | bytes 1474568 | tf_op jit(solution)/shard_map/ppermute | solution.py:244
  101.5 3.8 %blocks_0r272.1.own = f32[240,1024]{1,0:T(8,128)S(1)} custom-call(bf16[4,512,128]{2,1,0:T(8,128)(2,1)S(1)} %collective-permute-done.refs_0_.refs_10_, bf16[4,512,128]{2,1,0:T(8,128)(2,1)S(1)} %collective-permute-done.1.refs_1_, bf16[4,512,128]{2,1,0:T(8,128)(2,1)S(1)} %collective-permute-done.4.refs_2_, ...), custom_call_target="tpu_custom_call" | custom-call | flops 2147483648 | bytes 5242880 | tf_op jit(solution)/shard_map/blocks_0r272/pallas_call | solution.py:199
  105.3 3.9 %blocks_0r0.1.own = f32[272,1024]{1,0:T(8,128)S(1)} custom-call(bf16[4,512,128]{2,1,0:T(8,128)(2,1)S(1)} %collective-permute-done.refs_0_.refs_10_, bf16[4,512,128]{2,1,0:T(8,128)(2,1)S(1)} %collective-permute-done.1.refs_1_, bf16[4,512,128]{2,1,0:T(8,128)(2,1)S(1)} %collective-permute-done.4.refs_2_, ...), custom_call_target="tpu_custom_call" | custom-call | flops 2147483648 | bytes 5242880 | tf_op jit(solution)/shard_map/blocks_0r0/pallas_call | solution.py:199
  109.2 3.3 %collective-permute-done.23.p = bf16[272,1024]{1,0:T(8,128)(2,1)S(1)} collective-permute-done((bf16[272,1024]{1,0:T(8,128)(2,1)S(1)}, bf16[272,1024]{1,0:T(8,128)(2,1)S(1)}, u32[]{:S(2)}, u32[]{:S(2)}) %collective-permute-start.23) | collective-permute-done | bytes 557088 | tf_op jit(solution)/shard_map/ppermute | solution.py:244
  112.5 1.3 %final0.1.rest_0_ = f32[512,1024]{1,0:T(8,128)} custom-call(f32[272,1024]{1,0:T(8,128)S(1)} %blocks_0r0.1.own, bf16[272,1024]{1,0:T(8,128)(2,1)S(1)} %collective-permute-done.23.p), custom_call_target="tpu_custom_call" | custom-call | tf_op jit(solution)/shard_map/final0/pallas_call | solution.py:231
  113.9 1.3 %final1.1 = f32[512,1024]{1,0:T(8,128)} custom-call(f32[240,1024]{1,0:T(8,128)S(1)} %blocks_0r272.1.own, bf16[240,1024]{1,0:T(8,128)(2,1)S(1)} %collective-permute-done.20.p, f32[512,1024]{1,0:T(8,128)} %final0.1.rest_0_), custom_call_target="tpu_custom_call", output_to_operand_aliasing={{}: (2, {})} | custom-call | tf_op jit(solution)/shard_map/final1/pallas_call | solution.py:231
  (29 shorter events, 1.1 us)
Async XLA Ops:
  0.0 18.8 %copy-start = (bf16[4,128,1024]{2,1,0:T(8,128)(2,1)S(1)}, bf16[4,128,1024]{2,1,0:T(8,128)(2,1)}, u32[]{:S(2)}) copy-start(bf16[4,128,1024]{2,1,0:T(8,128)(2,1)} %g.1) | copy-start | bytes 3145732
  0.0 18.8 %collective-permute-start.2 = (bf16[4,128,1024]{2,1,0:T(8,128)(2,1)}, bf16[4,128,1024]{2,1,0:T(8,128)(2,1)S(1)}, u32[]{:S(2)}, u32[]{:S(2)}) collective-permute-start(bf16[4,128,1024]{2,1,0:T(8,128)(2,1)} %g.1), channel_id=1, source_target_pairs={{0,1},{1,0},{2,3},{3,2},{4,5},{5,4},{6,7},{7,6},{8,9},{9,8},{10,11... | collective-permute-start | bytes 3145736 | tf_op jit(solution)/shard_map/ppermute | solution.py:244
  1.4 1.2 %copy-start.1 = (bf16[4,128,1024]{2,1,0:T(8,128)(2,1)S(1)}, bf16[4,128,1024]{2,1,0:T(8,128)(2,1)}, u32[]{:S(2)}) copy-start(bf16[4,128,1024]{2,1,0:T(8,128)(2,1)} %a_ref.3) | copy-start | bytes 3145732
  3.1 15.7 %collective-permute-start.1 = (bf16[4,512,128]{2,1,0:T(8,128)(2,1)S(1)}, bf16[4,512,128]{2,1,0:T(8,128)(2,1)S(1)}, u32[]{:S(2)}, u32[]{:S(2)}) collective-permute-start(bf16[4,512,128]{2,1,0:T(8,128)(2,1)S(1)} %prep1.1.rest_0_), channel_id=1, source_target_pairs={{0,8},{1,25},{8,1},{9,16},{16,9},{17,24},{24,0},{25,17},{2,10},{3,... | collective-permute-start | bytes 1572872 | tf_op jit(solution)/shard_map/ppermute | solution.py:261
  7.5 14.7 %collective-permute-start = (bf16[4,512,128]{2,1,0:T(8,128)(2,1)S(1)}, bf16[4,512,128]{2,1,0:T(8,128)(2,1)S(1)}, u32[]{:S(2)}, u32[]{:S(2)}) collective-permute-start(bf16[4,512,128]{2,1,0:T(8,128)(2,1)S(1)} %prep0.1), channel_id=1, source_target_pairs={{0,0},{1,17},{8,9},{9,24},{16,1},{17,16},{24,8},{25,25},{2,2},{3,1... | collective-permute-start | bytes 1572872 | tf_op jit(solution)/shard_map/ppermute | solution.py:262
  18.8 3.5 %collective-permute-start.3 = (bf16[4,512,128]{2,1,0:T(8,128)(2,1)S(1)}, bf16[4,512,128]{2,1,0:T(8,128)(2,1)S(1)}, u32[]{:S(2)}, u32[]{:S(2)}) collective-permute-start(bf16[4,512,128]{2,1,0:T(8,128)(2,1)S(1)} %collective-permute-done.1.refs_1_), channel_id=1, source_target_pairs={{0,1},{1,0},{2,3},{3,2},{4,5},{5,4},{6,7},{7,6},{8,9},{9,8},{10,11... | collective-permute-start | bytes 1572872 | tf_op jit(solution)/shard_map/ppermute | solution.py:244
  19.1 14.9 %collective-permute-start.8 = (bf16[2,2,128,1024]{3,2,1,0:T(8,128)(2,1)S(1)}, bf16[2,2,128,1024]{3,2,1,0:T(8,128)(2,1)S(1)}, u32[]{:S(2)}, u32[]{:S(2)}) collective-permute-start(bf16[2,2,128,1024]{3,2,1,0:T(8,128)(2,1)S(1)} %pad_maximum_fusion.3), channel_id=1, source_target_pairs={{0,8},{8,16},{16,24},{24,0},{1,25},{9,1},{17,9},{25,17},{2,10},{10... | collective-permute-start | bytes 3145736 | tf_op jit(solution)/shard_map/ppermute | solution.py:249
  22.4 14.5 %collective-permute-start.7 = (bf16[8,512,128]{2,1,0:T(8,128)(2,1)S(1)}, bf16[8,512,128]{2,1,0:T(8,128)(2,1)S(1)}, u32[]{:S(2)}, u32[]{:S(2)}) collective-permute-start(bf16[8,512,128]{2,1,0:T(8,128)(2,1)S(1)} %pad_maximum_fusion.2), channel_id=1, source_target_pairs={{0,2},{2,4},{4,6},{6,0},{1,7},{3,1},{5,3},{7,5},{8,10},{10,12},{12... | collective-permute-start | bytes 3145736 | tf_op jit(solution)/shard_map/ppermute | solution.py:249
  25.2 1.9 %collective-permute-start.4 = (bf16[4,512,128]{2,1,0:T(8,128)(2,1)S(1)}, bf16[4,512,128]{2,1,0:T(8,128)(2,1)S(1)}, u32[]{:S(2)}, u32[]{:S(2)}) collective-permute-start(bf16[4,512,128]{2,1,0:T(8,128)(2,1)S(1)} %collective-permute-done.refs_0_.refs_10_), channel_id=1, source_target_pairs={{0,1},{1,0},{2,3},{3,2},{4,5},{5,4},{6,7},{7,6},{8,9},{9,8},{10,11... | collective-permute-start | bytes 1572872 | tf_op jit(solution)/shard_map/ppermute | solution.py:244
  25.3 20.0 %collective-permute-start.6 = (bf16[2,2,128,1024]{3,2,1,0:T(8,128)(2,1)S(1)}, bf16[2,2,128,1024]{3,2,1,0:T(8,128)(2,1)S(1)}, u32[]{:S(2)}, u32[]{:S(2)}) collective-permute-start(bf16[2,2,128,1024]{3,2,1,0:T(8,128)(2,1)S(1)} %pad_maximum_fusion.1), channel_id=1, source_target_pairs={{0,8},{8,16},{16,24},{24,0},{1,25},{9,1},{17,9},{25,17},{2,10},{10... | collective-permute-start | bytes 3145736 | tf_op jit(solution)/shard_map/ppermute | solution.py:249
  27.2 21.0 %collective-permute-start.5 = (bf16[8,512,128]{2,1,0:T(8,128)(2,1)S(1)}, bf16[8,512,128]{2,1,0:T(8,128)(2,1)S(1)}, u32[]{:S(2)}, u32[]{:S(2)}) collective-permute-start(bf16[8,512,128]{2,1,0:T(8,128)(2,1)S(1)} %pad_maximum_fusion), channel_id=1, source_target_pairs={{0,2},{2,4},{4,6},{6,0},{1,7},{3,1},{5,3},{7,5},{8,10},{10,12},{12... | collective-permute-start | bytes 3145736 | tf_op jit(solution)/shard_map/ppermute | solution.py:249
  36.9 11.2 %collective-permute-start.9 = (bf16[8,512,128]{2,1,0:T(8,128)(2,1)S(1)}, bf16[8,512,128]{2,1,0:T(8,128)(2,1)S(1)}, u32[]{:S(2)}, u32[]{:S(2)}) collective-permute-start(bf16[8,512,128]{2,1,0:T(8,128)(2,1)S(1)} %collective-permute-done.7.refs_5_), channel_id=1, source_target_pairs={{0,1},{1,0},{2,3},{3,2},{4,5},{5,4},{6,7},{7,6},{8,9},{9,8},{10,11... | collective-permute-start | bytes 3145736 | tf_op jit(solution)/shard_map/ppermute | solution.py:244
  48.2 17.0 %collective-permute-start.14 = (bf16[8,512,128]{2,1,0:T(8,128)(2,1)S(1)}, bf16[8,512,128]{2,1,0:T(8,128)(2,1)S(1)}, u32[]{:S(2)}, u32[]{:S(2)}) collective-permute-start(bf16[8,512,128]{2,1,0:T(8,128)(2,1)S(1)} %collective-permute-done.5.refs_4_), channel_id=1, source_target_pairs={{0,1},{1,0},{2,3},{3,2},{4,5},{5,4},{6,7},{7,6},{8,9},{9,8},{10,11... | collective-permute-start | bytes 3145736 | tf_op jit(solution)/shard_map/ppermute | solution.py:244
  48.3 9.2 %collective-permute-start.11 = (bf16[4,512,128]{2,1,0:T(8,128)(2,1)S(1)}, bf16[4,512,128]{2,1,0:T(8,128)(2,1)S(1)}, u32[]{:S(2)}, u32[]{:S(2)}) collective-permute-start(bf16[4,512,128]{2,1,0:T(8,128)(2,1)S(1)} %slice.36), channel_id=1, source_target_pairs={{0,2},{2,4},{4,6},{6,0},{1,7},{3,1},{5,3},{7,5},{8,10},{10,12},{12... | collective-permute-start | bytes 1572872 | tf_op jit(solution)/shard_map/ppermute | solution.py:249
  51.4 8.3 %collective-permute-start.12 = (bf16[2,128,1024]{2,1,0:T(8,128)(2,1)S(1)}, bf16[2,128,1024]{2,1,0:T(8,128)(2,1)S(1)}, u32[]{:S(2)}, u32[]{:S(2)}) collective-permute-start(bf16[2,128,1024]{2,1,0:T(8,128)(2,1)S(1)} %get-tuple-element.37), channel_id=1, source_target_pairs={{0,8},{8,16},{16,24},{24,0},{1,25},{9,1},{17,9},{25,17},{2,10},{10... | collective-permute-start | bytes 1572872 | tf_op jit(solution)/shard_map/ppermute | solution.py:249
  53.0 10.1 %collective-permute-start.10 = (bf16[4,512,128]{2,1,0:T(8,128)(2,1)S(1)}, bf16[4,512,128]{2,1,0:T(8,128)(2,1)S(1)}, u32[]{:S(2)}, u32[]{:S(2)}) collective-permute-start(bf16[4,512,128]{2,1,0:T(8,128)(2,1)S(1)} %slice.35), channel_id=1, source_target_pairs={{0,2},{2,4},{4,6},{6,0},{1,7},{3,1},{5,3},{7,5},{8,10},{10,12},{12... | collective-permute-start | bytes 1572872 | tf_op jit(solution)/shard_map/ppermute | solution.py:249
  53.6 11.5 %collective-permute-start.13 = (bf16[2,128,1024]{2,1,0:T(8,128)(2,1)S(1)}, bf16[2,128,1024]{2,1,0:T(8,128)(2,1)S(1)}, u32[]{:S(2)}, u32[]{:S(2)}) collective-permute-start(bf16[2,128,1024]{2,1,0:T(8,128)(2,1)S(1)} %get-tuple-element.36), channel_id=1, source_target_pairs={{0,8},{8,16},{16,24},{24,0},{1,25},{9,1},{17,9},{25,17},{2,10},{10... | collective-permute-start | bytes 1572872 | tf_op jit(solution)/shard_map/ppermute | solution.py:249
  65.2 7.4 %collective-permute-start.15 = (bf16[8,512,128]{2,1,0:T(8,128)(2,1)S(1)}, bf16[8,512,128]{2,1,0:T(8,128)(2,1)S(1)}, u32[]{:S(2)}, u32[]{:S(2)}) collective-permute-start(bf16[8,512,128]{2,1,0:T(8,128)(2,1)S(1)} %pad_maximum_fusion.4), channel_id=1, source_target_pairs={{0,1},{1,0},{2,3},{3,2},{4,5},{5,4},{6,7},{7,6},{8,9},{9,8},{10,11... | collective-permute-start | bytes 3145736 | tf_op jit(solution)/shard_map/ppermute | solution.py:244
  65.7 3.0 %collective-permute-start.16 = (bf16[2,128,1024]{2,1,0:T(8,128)(2,1)S(1)}, bf16[2,128,1024]{2,1,0:T(8,128)(2,1)S(1)}, u32[]{:S(2)}, u32[]{:S(2)}) collective-permute-start(bf16[2,128,1024]{2,1,0:T(8,128)(2,1)S(1)} %get-tuple-element.32), channel_id=1, source_target_pairs={{0,1},{1,0},{2,3},{3,2},{4,5},{5,4},{6,7},{7,6},{8,9},{9,8},{10,11... | collective-permute-start | bytes 1572872 | tf_op jit(solution)/shard_map/ppermute | solution.py:244
  65.8 3.7 %collective-permute-start.17 = (bf16[2,128,1024]{2,1,0:T(8,128)(2,1)S(1)}, bf16[2,128,1024]{2,1,0:T(8,128)(2,1)S(1)}, u32[]{:S(2)}, u32[]{:S(2)}) collective-permute-start(bf16[2,128,1024]{2,1,0:T(8,128)(2,1)S(1)} %get-tuple-element.35), channel_id=1, source_target_pairs={{0,1},{1,0},{2,3},{3,2},{4,5},{5,4},{6,7},{7,6},{8,9},{9,8},{10,11... | collective-permute-start | bytes 1572872 | tf_op jit(solution)/shard_map/ppermute | solution.py:244
  74.9 15.1 %collective-permute-start.22 = (bf16[272,1024]{1,0:T(8,128)(2,1)S(1)}, bf16[272,1024]{1,0:T(8,128)(2,1)S(1)}, u32[]{:S(2)}, u32[]{:S(2)}) collective-permute-start(bf16[272,1024]{1,0:T(8,128)(2,1)S(1)} %blocks_2r0.3), channel_id=1, source_target_pairs={{0,32},{32,64},{64,96},{96,0},{1,33},{33,65},{65,97},{97,1},{2,34}... | collective-permute-start | bytes 1671176 | tf_op jit(solution)/shard_map/ppermute | solution.py:244
  78.3 16.2 %collective-permute-start.19 = (bf16[240,1024]{1,0:T(8,128)(2,1)S(1)}, bf16[240,1024]{1,0:T(8,128)(2,1)S(1)}, u32[]{:S(2)}, u32[]{:S(2)}) collective-permute-start(bf16[240,1024]{1,0:T(8,128)(2,1)S(1)} %blocks_2r272.1), channel_id=1, source_target_pairs={{0,96},{32,0},{64,32},{96,64},{1,97},{33,1},{65,33},{97,65},{2,98}... | collective-permute-start | bytes 1474568 | tf_op jit(solution)/shard_map/ppermute | solution.py:244
  83.4 18.1 %collective-permute-start.18 = (bf16[240,1024]{1,0:T(8,128)(2,1)S(1)}, bf16[240,1024]{1,0:T(8,128)(2,1)S(1)}, u32[]{:S(2)}, u32[]{:S(2)}) collective-permute-start(bf16[240,1024]{1,0:T(8,128)(2,1)S(1)} %blocks_1r272.1), channel_id=1, source_target_pairs={{0,32},{32,64},{64,96},{96,0},{1,33},{33,65},{65,97},{97,1},{2,34}... | collective-permute-start | bytes 1474568 | tf_op jit(solution)/shard_map/ppermute | solution.py:244
  87.4 17.9 %collective-permute-start.21 = (bf16[272,1024]{1,0:T(8,128)(2,1)S(1)}, bf16[272,1024]{1,0:T(8,128)(2,1)S(1)}, u32[]{:S(2)}, u32[]{:S(2)}) collective-permute-start(bf16[272,1024]{1,0:T(8,128)(2,1)S(1)} %blocks_3r0.1), channel_id=1, source_target_pairs={{0,96},{32,0},{64,32},{96,64},{1,97},{33,1},{65,33},{97,65},{2,98}... | collective-permute-start | bytes 1671176 | tf_op jit(solution)/shard_map/ppermute | solution.py:244
  94.5 18.1 %collective-permute-start.23 = (bf16[272,1024]{1,0:T(8,128)(2,1)S(1)}, bf16[272,1024]{1,0:T(8,128)(2,1)S(1)}, u32[]{:S(2)}, u32[]{:S(2)}) collective-permute-start(bf16[272,1024]{1,0:T(8,128)(2,1)S(1)} %blocks_1r0.1), channel_id=1, source_target_pairs={{0,32},{32,64},{64,96},{96,0},{1,33},{33,65},{65,97},{97,1},{2,34}... | collective-permute-start | bytes 1671176 | tf_op jit(solution)/shard_map/ppermute | solution.py:244
  98.8 15.0 %collective-permute-start.20 = (bf16[240,1024]{1,0:T(8,128)(2,1)S(1)}, bf16[240,1024]{1,0:T(8,128)(2,1)S(1)}, u32[]{:S(2)}, u32[]{:S(2)}) collective-permute-start(bf16[240,1024]{1,0:T(8,128)(2,1)S(1)} %blocks_3r272.1), channel_id=1, source_target_pairs={{0,96},{32,0},{64,32},{96,64},{1,97},{33,1},{65,33},{97,65},{2,98}... | collective-permute-start | bytes 1474568 | tf_op jit(solution)/shard_map/ppermute | solution.py:244
